TPU v7x, 32 devices: a whole 2x2x4 slice. The times are simulated.
32 devices in a mesh: seq: 8 (over y, x, core), req: 4 (over z).
Axes of the slice: x: 2, y: 2, z: 4, core: 2. Of those that a mesh axis runs over, the one named last changes fastest.
Arguments:
- x_in: bfloat16 [24, 4, 1536], P('req'), may hold values from -6 to 6
- attn_gain: float32 [1536], replicated, may hold values from 0.25 to 1.75
- moe_gain: float32 [1536], replicated, may hold values from 0.25 to 1.75
- w_qkv: bfloat16 [1536, 2560], P(None, 'seq'), may hold values from -0.15625 to 0.15625
- w_o: bfloat16 [1536, 1536], P(None, 'seq'), may hold values from -0.3125 to 0.3125
- cache_k: bfloat16 [24, 1024, 512], P('req', 'seq'), may hold values from -1024 to 1024
- cache_v: bfloat16 [24, 1024, 512], P('req', 'seq'), may hold values from -6 to 6
- page_map: int32 [24, 64], P('req', 'seq'), may hold values from 0 to 63, as said below
- lengths: int32 [24], P('req'), may hold values from 2 to 1024, as said below
- routes: int32 [24, 4, 8], P('req'), may hold values from 0 to 31, all different within a row; in each aligned block of 24 rows (0 to 23, 24 to 47, ..., all dimensions but the last counted through in order) at most 12 rows name the same one
- route_weights: float32 [24, 4, 8], P('req'), may hold values from 0.1 to 1
- w_gate_up: bfloat16 [32, 1536, 1024], P('seq', 'req'), may hold values from -0.15625 to 0.15625
- w_down: bfloat16 [32, 512, 1536], P('seq', None, 'req'), may hold values from -0.375 to 0.375
Outputs:
- layer_out: bfloat16 [24, 4, 1536], P('req', None, 'seq')
Inputs may be any that keep to these rules, and one draw needn't show every extreme that they name: `lengths`: every index of req holds one request with exactly 1024 cached positions. `page_map`: each row is a permutation of the request's 64 logical pages. `routes`: A token names 8 different experts. Among the 24 tokens of one index of req no expert is named more than 12 times.
All inputs are finite; a program needn't handle non-finite values.
Results may differ from a plain program's by a relative error of at most 0.01.
Values may be sent and summed in bfloat16 or wider, within the bound.
No kernel may reach another device: no remote copies, remote signals or barrier semaphores. Data moves between devices by JAX's collectives and lax.ppermute only.
A program may use at most 64 MiB of HBM per device.

v0:
```python
import math

import jax
import jax.numpy as jnp
from jax import lax
from jax.sharding import PartitionSpec as P

D = 1536
HEADS = 24
KVH = 8
HD = 64
FFE = 512
TOP = 8
NSTEP = 4
PAGE = 16
ATT = 1536
KVD = 512
GROUP = 3
CAP = 12


EPS = 1e-05
NEG = -1e30


def combined_all(value, axis, join):
    pieces = jax.tree.map(lambda part: lax.all_gather(part, axis), value)
    head = jax.tree.map(lambda part: part[0], pieces)
    tail = jax.tree.map(lambda part: part[1:], pieces)
    so_far, _ = lax.scan(lambda so_far, piece: (join(so_far, piece), None), head, tail)
    return so_far


def normalize(values, gain):
    power = jnp.mean(values * values, axis=-1, keepdims=True)
    return values * lax.rsqrt(power + EPS) * gain


def rotate(values, position):
    half = values.shape[-1] // 2
    rates = jnp.exp(
        jnp.arange(half, dtype=jnp.float32) * (-2.0 * math.log(10000.0) / values.shape[-1])
    )
    angle = position[..., None, None] * rates
    cosine = jnp.cos(angle)
    sine = jnp.sin(angle)
    first_half = values[..., :half]
    second_half = values[..., half:]
    return jnp.concatenate(
        [first_half * cosine - second_half * sine, second_half * cosine + first_half * sine],
        axis=-1,
    )


def softmax_join(left, right):
    left_top, left_total, left_sums = left
    right_top, right_total, right_sums = right
    highest = jnp.maximum(left_top, right_top)
    left_factor = jnp.exp(left_top - highest)
    right_factor = jnp.exp(right_top - highest)
    row_count, head_count = highest.shape
    left_part = left_sums.reshape(row_count, head_count, -1) * left_factor[:, :, None]
    right_part = right_sums.reshape(row_count, head_count, -1) * right_factor[:, :, None]
    joined = (left_part + right_part).reshape(row_count, -1)
    return (highest, left_total * left_factor + right_total * right_factor, joined)


def project_with(left, piece):
    return jnp.dot(left, piece, preferred_element_type=jnp.float32)


def local(
    x_in,
    attn_gain,
    moe_gain,
    w_qkv,
    w_o,
    cache_k,
    cache_v,
    page_map,
    lengths,
    routes,
    route_weights,
    w_gate_up,
    w_down,
):
    local_requests = x_in.shape[0]
    row_count = local_requests * NSTEP
    inputs = x_in.astype(jnp.float32).reshape(row_count, D)
    normed = normalize(inputs, attn_gain).astype(jnp.bfloat16)
    projected = project_with(normed, lax.all_gather(w_qkv, "seq", axis=1, tiled=True))
    queries = projected[:, :ATT].reshape(local_requests, NSTEP, HEADS, HD)
    keys_new = projected[:, ATT : ATT + KVD].reshape(local_requests, NSTEP, KVH, HD)
    values_new = (
        projected[:, ATT + KVD :].reshape(local_requests, NSTEP, KVH, HD).astype(jnp.bfloat16)
    )
    position = (lengths[:, None] + jnp.arange(NSTEP, dtype=jnp.int32)[None, :]).astype(jnp.float32)
    queries = (
        rotate(queries, position)
        .astype(jnp.bfloat16)
        .reshape(local_requests, NSTEP, KVH, GROUP, HD)
    )
    keys_new = rotate(keys_new, position).astype(jnp.bfloat16)
    scale = HD ** (-0.5)
    slot_count = cache_k.shape[1]
    cached_keys = cache_k.reshape(local_requests, slot_count, KVH, HD)
    cached_values = cache_v.reshape(local_requests, slot_count, KVH, HD)
    slot_position = (
        page_map[:, :, None] * PAGE + jnp.arange(PAGE, dtype=jnp.int32)[None, None, :]
    ).reshape(local_requests, slot_count)
    live = (slot_position < lengths[:, None])[:, None, None, None, :]
    scores = (
        jnp.einsum("rskgd,rtkd->rskgt", queries, cached_keys, preferred_element_type=jnp.float32)
        * scale
    )
    scores = jnp.where(live, scores, NEG)
    local_top = jnp.max(scores, axis=-1)
    exp_scores = jnp.where(live, jnp.exp(scores - local_top[..., None]), 0.0)
    local_total = jnp.sum(exp_scores, axis=-1).reshape(row_count, HEADS)
    local_sums = jnp.einsum(
        "rskgt,rtkd->rskgd",
        exp_scores.astype(jnp.bfloat16),
        cached_values,
        preferred_element_type=jnp.float32,
    ).reshape(row_count, ATT)
    local_top = local_top.reshape(row_count, HEADS)
    cache_top, cache_total, cache_sums = combined_all(
        (local_top, local_total, local_sums), "seq", softmax_join
    )
    causal = (
        jnp.arange(NSTEP, dtype=jnp.int32)[:, None] >= jnp.arange(NSTEP, dtype=jnp.int32)[None, :]
    )[None, :, None, None, :]
    fresh = (
        jnp.einsum("rskgd,rukd->rskgu", queries, keys_new, preferred_element_type=jnp.float32)
        * scale
    )
    fresh = jnp.where(causal, fresh, NEG).reshape(row_count, HEADS, NSTEP)
    highest = jnp.maximum(cache_top, jnp.max(fresh, axis=-1))
    fresh_exp = jnp.exp(fresh - highest[:, :, None])
    carried = jnp.exp(cache_top - highest)
    denominator = cache_total * carried + jnp.sum(fresh_exp, axis=-1)
    fresh_probs = fresh_exp.reshape(local_requests, NSTEP, KVH, GROUP, NSTEP).astype(jnp.bfloat16)
    fresh_sums = jnp.einsum(
        "rskgu,rukd->rskgd", fresh_probs, values_new, preferred_element_type=jnp.float32
    ).reshape(row_count, HEADS, HD)
    numerator = cache_sums.reshape(row_count, HEADS, HD) * carried[:, :, None] + fresh_sums
    attended = (numerator / denominator[:, :, None]).reshape(row_count, ATT).astype(jnp.bfloat16)
    attn_mixed = project_with(attended, lax.all_gather(w_o, "seq", axis=1, tiled=True))
    resid = inputs + attn_mixed
    mixed_in = normalize(resid, moe_gain).astype(jnp.bfloat16)
    local_experts = w_gate_up.shape[0]
    groups = lax.axis_size("req")
    owned = lax.axis_index("seq") * local_experts + jnp.arange(local_experts, dtype=jnp.int32)
    chosen = routes.reshape(row_count, TOP)
    gates = route_weights.reshape(row_count, TOP)
    matches = chosen[None, :, :] == owned[:, None, None]
    routed = jnp.any(matches, axis=-1)
    route_scale = jnp.sum(jnp.where(matches, gates[None, :, :], 0.0), axis=-1)
    ordinal = jnp.cumsum(routed.astype(jnp.int32), axis=1) - 1
    placed = routed[:, :, None] & (
        ordinal[:, :, None] == jnp.arange(CAP, dtype=jnp.int32)[None, None, :]
    )
    outgoing = jnp.einsum(
        "erc,rd->ecd", placed.astype(jnp.bfloat16), mixed_in, preferred_element_type=jnp.float32
    ).astype(jnp.bfloat16)
    arrived = lax.all_to_all(outgoing[:, None], "req", split_axis=3, concat_axis=1, tiled=True)
    slice_width = arrived.shape[3]
    arrived = arrived.reshape(local_experts, groups * CAP, slice_width)
    partial_values = jnp.einsum(
        "end,edf->enf", arrived, w_gate_up, preferred_element_type=jnp.float32
    )
    gate_up = lax.psum(partial_values, "req")
    hidden = (jax.nn.silu(gate_up[..., :FFE]) * gate_up[..., FFE:]).astype(jnp.bfloat16)
    produced = jnp.einsum("enf,efd->end", hidden, w_down, preferred_element_type=jnp.float32)
    returned = lax.all_to_all(
        produced.reshape(local_experts, groups, CAP, slice_width),
        "req",
        split_axis=1,
        concat_axis=3,
        tiled=True,
    )[:, 0]
    weighted = placed.astype(jnp.float32) * route_scale[:, :, None]
    expert_total = jnp.einsum("erc,ecd->rd", weighted, returned, precision=lax.Precision.HIGHEST)
    own_share = lax.psum_scatter(expert_total, "seq", scatter_dimension=1, tiled=True)
    share_width = own_share.shape[1]
    resid_share = lax.dynamic_slice_in_dim(
        resid, lax.axis_index("seq") * share_width, share_width, 1
    )
    return (
        (resid_share + own_share).astype(jnp.bfloat16).reshape(local_requests, NSTEP, share_width)
    )


def solution(mesh):
    in_specs = (
        P("req", None, None),
        P(),
        P(),
        P(None, "seq"),
        P(None, "seq"),
        P("req", "seq", None),
        P("req", "seq", None),
        P("req", "seq"),
        P("req"),
        P("req", None, None),
        P("req", None, None),
        P("seq", "req", None),
        P("seq", None, "req"),
    )
    out_specs = P("req", None, "seq")
    return jax.shard_map(local, mesh=mesh, in_specs=in_specs, out_specs=out_specs, check_vma=False)
```

profile of v0, /device:TPU:0, one launch (start us, length us, event | category | flops | bytes accessed | tf_op | source)
XLA Modules:
  0.0 312.2 jit_solution(7771608253584951887)
XLA Ops:
  10.4 2.4 copy.68
  12.8 2.4 copy.71
  15.5 48.7 %all-gather.4.cloned.1.call-done = bf16[1536,2560]{0,1:T(8,128)(2,1)} async-done(((bf16[1536,320]{0,1:T(8,128)(2,1)}), bf16[1536,2560]{0,1:T(8,128)(2,1)}) %all-gather.4.cloned.1.call-update) | async-done | bytes 7864336 | tf_op jit(solution)/shard_map/all_gather | solution.py:91
  64.2 5.4 %fusion.24 = f32[24,2560]{1,0:T(8,128)S(1)} fusion(bf16[1536,2560]{0,1:T(8,128)(2,1)} %all-gather.4.cloned.1.call-done, f32[24,1536]{1,0:T(8,128)S(1)} %reshape.189, f32[1536]{0:T(1024)S(1)} %copy-done.20, f32[24]{0:T(128)S(1)} %rsqrt.20), kind=kOutput, calls=%fused_computation.47 | convolution fusion | flops 188854272 | bytes 8263776 | tf_op jit(solution)/shard_map/dot_general | solution.py:69
  86.1 2.1 fusion.15
  88.2 1.9 copy.70
  91.7 9.3 %all_gather.17 = f32[8,24,24]{2,1,0:T(8,128)S(1)} all-gather(f32[1,24,24]{2,1,0:T(8,128)} %all_gather_reshape.10), channel_id=1, replica_groups=mesh['seq'=8,'req'=4] {'seq'}, dimensions={0}, use_global_device_ids=true | all-gather | bytes 20736 | tf_op jit(solution)/shard_map/all_gather | solution.py:27
  103.0 8.6 %all_gather.16 = f32[8,24,24]{2,1,0:T(8,128)S(1)} all-gather(f32[1,24,24]{2,1,0:T(8,128)} %all_gather_reshape.9), channel_id=1, replica_groups=mesh['seq'=8,'req'=4] {'seq'}, dimensions={0}, use_global_device_ids=true | all-gather | bytes 20736 | tf_op jit(solution)/shard_map/all_gather | solution.py:27
  114.6 3.1 %fusion.52 = (f32[6,4,8,3]{1,3,2,0:T(4,128)}, f32[6,4,8,3,4]{1,4,3,2,0:T(4,128)}) fusion(bf16[6,4,8,3,32]{4,1,3,2,0:T(4,128)(2,1)S(1)} %bitcast.103, bf16[6,4,8,3,32]{4,1,3,2,0:T(4,128)(2,1)S(1)} %bitcast.101, bf16[6,4,8,32]{3,1,2,0:T(4,128)(2,1)S(1)} %get-tuple-element.70, bf16[6,4,8,32]{3,1,2,0:T(4,128)(2,1)S(1)} %get-tuple-element.69, ...), kind=kOutput, calls=%fused_computation.92 | convolution fusion | flops 497856 | bytes 109840 | tf_op jit(solution)/shard_map/rskgd,rukd->rskgu/dot_general | solution.py:134
  122.0 2.3 slice.69
  125.8 30.9 %while.14 = (s32[]{:T(128)}, f32[24,24]{1,0:T(8,128)S(1)}, f32[24,24]{1,0:T(8,128)S(1)}, f32[24,1536]{1,0:T(8,128)}, f32[7,24,24]{2,1,0:T(8,128)}, /*index=5*/f3...) while((s32[]{:T(128)}, f32[24,24]{1,0:T(8,128)S(1)}, f32[24,24]{1,0:T(8,128)S(1)}, f32[24,1536]{1,0:T(8,128)}, ...), condition=%wide.region_4.5_spmd, body=%wide.region_3.4_spmd.sunk | while | flops 114050 | bytes 1645149 | solution.py:30
  162.2 2.0 reshape.194
  173.9 4.0 %multiply_reduce_fusion = (f32[24]{0:T(128)S(1)}, f32[24,1536]{1,0:T(8,128)S(1)}) fusion(f32[24,1536]{1,0:T(8,128)S(1)} %copy-done.3, bf16[1536,1536]{0,1:T(8,128)(2,1)} %all-gather.8.cloned.1.call-done, f32[24,1536]{1,0:T(8,128)} %div.23, f32[24,1536]{1,0:T(8,128)} %reshape.194, f32[24,1536]{1,0:T(8,128)S(1)} %copy-done.1, f32[24,1536]{1,0:T(8,128)} %mul.246), kind=kOutput, calls=%fused_computation.37 | convolution fusion | flops 113504232 | bytes 5603424 | tf_op jit(solution)/shard_map/dot_general | solution.py:69
  178.9 2.2 copy.83
  181.2 4.3 %reshape.207 = bf16[4,2,9216]{2,1,0:T(2,128)(2,1)S(1)} reshape(bf16[1536,1,4,12]{3,2,1,0:T(4,128)(2,1)} %bitcast.94) | data formatting | bytes 294912
  185.5 11.4 %all_to_all.30 = bf16[4,2,9216]{2,1,0:T(2,128)(2,1)S(1)} all-to-all(bf16[4,2,9216]{2,1,0:T(2,128)(2,1)S(1)} %reshape.207), channel_id=1, replica_groups=mesh['seq'=8,'req'=4] {'req'}, dimensions={0} | all-to-all | bytes 294912 | tf_op jit(solution)/shard_map/all_to_all | solution.py:166
  196.8 4.8 %reshape.208 = bf16[1536,1,4,12]{3,2,1,0:T(4,128)(2,1)} reshape(bf16[4,2,9216]{2,1,0:T(2,128)(2,1)S(1)} %all_to_all.30) | data formatting | bytes 294912
  201.6 2.9 copy.97
  206.2 41.9 %all-reduce.2.cloned.1.call-done = f32[4,48,1024]{2,1,0:T(8,128)} async-done(((f32[4,48,1024]{2,1,0:T(8,128)}), f32[4,48,1024]{2,1,0:T(8,128)}) %all-reduce.2.cloned.1.call-update) | async-done | bytes 786448 | tf_op jit(solution)/shard_map/psum | solution.py:172
  248.1 2.0 fusion.11
  251.0 3.5 %all-to-all-start.1 = ((f32[4,4,12,384]{3,0,2,1:T(4,128)}), f32[4,4,12,384]{3,0,2,1:T(4,128)S(1)}, u32[]{:S(2)}, u32[]{:S(2)}) async-start(f32[4,4,12,384]{3,0,2,1:T(4,128)} %bitcast.98), calls=%async_computation.1 | async-start | bytes 589824 | tf_op jit(solution)/shard_map/all_to_all | solution.py:175
  255.2 9.0 %all-to-all-done.1 = f32[4,4,12,384]{3,0,2,1:T(4,128)S(1)} async-done(((f32[4,4,12,384]{3,0,2,1:T(4,128)}), f32[4,4,12,384]{3,0,2,1:T(4,128)S(1)}, u32[]{:S(2)}, u32[]{:S(2)}) %all-to-all-start.1) | async-done | bytes 294944 | tf_op jit(solution)/shard_map/all_to_all | solution.py:175
  266.1 3.0 convolution_bitcast_fusion
  269.1 34.1 %reduce-scatter.4.cloned.1.call-done = f32[192,24]{1,0:T(8,128)} async-done(((f32[1536,24]{1,0:T(8,128)}), f32[192,24]{1,0:T(8,128)}) %reduce-scatter.4.cloned.1.call-update) | async-done | bytes 18448
  (178 shorter events, 87.5 us)
Async XLA Ops:
  6.5 198.0 %copy-start = (bf16[4,384,1024]{2,1,0:T(8,128)(2,1)S(1)}, bf16[4,384,1024]{2,1,0:T(8,128)(2,1)}, u32[]{:S(2)}) copy-start(bf16[4,384,1024]{2,1,0:T(8,128)(2,1)} %param.26) | copy-start | bytes 9437188
  6.5 8.6 %copy-start.24 = (s32[6]{0:T(128)S(1)}, s32[6]{0:T(128)}, u32[]{:S(2)}) copy-start(s32[6]{0:T(128)} %param.23) | copy-start | bytes 76
  6.5 57.6 %copy-start.20 = (f32[1536]{0:T(1024)S(1)}, f32[1536]{0:T(1024)}, u32[]{:S(2)}) copy-start(f32[1536]{0:T(1024)} %param.16) | copy-start | bytes 18436
  6.5 57.6 %all-gather.4.cloned.1.call-start = ((), (), s32[]{:S(2)}) async-start(), calls=%async_computation.3 | async-start | bytes 8847360 | tf_op jit(solution)/shard_map/all_gather | solution.py:91
  7.3 114.7 %all-gather.6.cloned.1.call-start = ((), (), s32[]{:S(2)}) async-start(), calls=%async_computation.4 | async-start | bytes 1327104 | tf_op jit(solution)/shard_map/all_gather | solution.py:27
  8.4 61.2 %copy-start.2 = (f32[24,1536]{1,0:T(8,128)}, f32[24,1536]{1,0:T(8,128)S(1)}, u32[]{:S(2)}) copy-start(f32[24,1536]{1,0:T(8,128)S(1)} %reshape.189) | copy-start | bytes 442372
  15.3 59.2 %copy-start.19 = (pred[6,128]{1,0:T(8,128)(4,1)}, pred[6,128]{1,0:T(8,128)(4,1)S(1)}, u32[]{:S(2)}) copy-start(pred[6,128]{1,0:T(8,128)(4,1)S(1)} %add_compare_fusion) | copy-start | bytes 2308
  15.5 56.4 %copy-start.15 = (f32[6,4,32]{2,1,0:T(4,128)}, f32[6,4,32]{2,1,0:T(4,128)S(1)}, u32[]{:S(2)}) copy-start(f32[6,4,32]{2,1,0:T(4,128)S(1)} %get-tuple-element.74) | copy-start | bytes 9220
  72.3 2.2 copy-start.11
  74.5 0.7 copy-start.4
  74.5 2.4 copy-start.6
  78.0 36.6 %copy-start.10 = (bf16[6,4,24,32]{3,1,2,0:T(4,128)(2,1)S(1)}, bf16[6,4,24,32]{3,1,2,0:T(4,128)(2,1)}, u32[]{:S(2)}) copy-start(bf16[6,4,24,32]{3,1,2,0:T(4,128)(2,1)} %copy-done.9) | copy-start | bytes 110596
  78.0 36.6 %copy-start.12 = (bf16[6,4,24,32]{3,1,2,0:T(4,128)(2,1)S(1)}, bf16[6,4,24,32]{3,1,2,0:T(4,128)(2,1)}, u32[]{:S(2)}) copy-start(bf16[6,4,24,32]{3,1,2,0:T(4,128)(2,1)} %copy-done.11) | copy-start | bytes 110596
  78.0 95.9 %all-gather.8.cloned.1.call-start = ((), (), s32[]{:S(2)}) async-start(), calls=%async_computation.5 | async-start | bytes 5308416 | tf_op jit(solution)/shard_map/all_gather | solution.py:148
  78.8 169.3 %all-reduce.2.cloned.1.call-start = ((), (), s32[]{:S(2)}) async-start(), calls=%async_computation.6 | async-start | bytes 1572864 | tf_op jit(solution)/shard_map/psum | solution.py:172
  156.7 17.2 %copy-start.1 = (f32[24,1536]{1,0:T(8,128)S(1)}, f32[24,1536]{1,0:T(8,128)}, u32[]{:S(2)}) copy-start(f32[24,1536]{1,0:T(8,128)} %get-tuple-element.44) | copy-start | bytes 442372
  156.7 17.2 %copy-start.3 = (f32[24,1536]{1,0:T(8,128)S(1)}, f32[24,1536]{1,0:T(8,128)}, u32[]{:S(2)}) copy-start(f32[24,1536]{1,0:T(8,128)} %copy-done.2) | copy-start | bytes 442372
  171.3 7.3 %copy-start.17 = (s32[4,24]{1,0:T(4,128)S(1)}, s32[4,24]{1,0:T(4,128)}, u32[]{:S(2)}) copy-start(s32[4,24]{1,0:T(4,128)} %broadcast_add_fusion) | copy-start | bytes 1156
  171.3 7.3 %copy-start.22 = (pred[4,24]{1,0:T(4,128)(4,1)S(1)}, pred[4,24]{1,0:T(4,128)(4,1)}, u32[]{:S(2)}) copy-start(pred[4,24]{1,0:T(4,128)(4,1)} %copy-done.21) | copy-start | bytes 292
  171.3 7.3 %copy-start.23 = (f32[1536]{0:T(1024)S(1)}, f32[1536]{0:T(1024)}, u32[]{:S(2)}) copy-start(f32[1536]{0:T(1024)} %param.17) | copy-start | bytes 18436
  206.2 48.3 %copy-start.18 = (f32[6,4,8]{2,1,0:T(4,128)S(1)}, f32[6,4,8]{2,1,0:T(4,128)}, u32[]{:S(2)}) copy-start(f32[6,4,8]{2,1,0:T(4,128)} %param.25) | copy-start | bytes 2308
  206.2 48.4 %copy-start.26 = (s32[4]{0:T(128)S(1)}, s32[4]{0:T(128)}, u32[]{:S(2)}) copy-start(s32[4]{0:T(128)} %copy-done.25) | copy-start | bytes 52
  251.0 13.2 %all-to-all-start.1 = ((f32[4,4,12,384]{3,0,2,1:T(4,128)}), f32[4,4,12,384]{3,0,2,1:T(4,128)S(1)}, u32[]{:S(2)}, u32[]{:S(2)}) async-start(f32[4,4,12,384]{3,0,2,1:T(4,128)} %bitcast.98), calls=%async_computation.1 | async-start | bytes 589824 | tf_op jit(solution)/shard_map/all_to_all | solution.py:175
  254.4 48.8 %reduce-scatter.4.cloned.1.call-start = ((), (), s32[]{:S(2)}) async-start(), calls=%async_computation.7 | async-start | bytes 884736
  (9 other events, 5.5 us)
Sparse Core Ops, SparseCore 0:
  9.3 54.8 all-gather.3
  78.1 24.3 all-gather.5
  104.4 38.9 all-gather.7
  206.3 41.7 all-reduce.1
  269.2 33.9 reduce-scatter.3
where the time goes:
time: 315 us; the launch traced here: 312 us
  waiting for transfers between devices  135 us (43%)
  local copies, waits for them, and re-layouts  77.9 us (25%)
  blocking collectives  29.3 us (9%)
  other arithmetic  28.6 us (9%)
  matrix products  24.1 us (8%)
  between operations  13.5 us (4%)
  starting transfers between devices  3.61 us (1%)
    all_gather x1, waiting for transfers between devices, local(): lax.all_gather(w_qkv, 'seq', axis=1, tiled=True)  48.7 us
    psum x1, waiting for transfers between devices, local(): gate_up = lax.psum(partial_values, 'req')  41.9 us
    unnamed x6, waiting for transfers between devices  35.5 us
    unnamed x59, local copies, waits for them, and re-layouts  20.8 us
    all_gather x2, blocking collectives, combined_all(): pieces = jax.tree.map(lambda part: lax.all_gather(part, axis), value)  17.9 us
    add x7, other arithmetic, softmax_join(): joined = (left_part + right_part).reshape(row_count, -1)  12.7 us
    all_to_all x1, blocking collectives, local(): lax.all_to_all(outgoing[:, None], 'req', split_axis=3, concat_axis=1, til...  11.4 us
    dot_general x2, matrix products, project_with(): return jnp.dot(left, piece, preferred_element_type=jnp.float32)  9.39 us
  transfers between devices with their start and end apart: 6, of which 4 were waited for; matrix products, arithmetic and copies ran while one was open for 26% of the time, Pallas kernels for 0%

commit v1 on v0

--- a/solution.py
+++ b/solution.py
@@ -3,6 +3,8 @@
 import jax
 import jax.numpy as jnp
 from jax import lax
+from jax.experimental import pallas as pl
+from jax.experimental.pallas import tpu as pltpu
 from jax.sharding import PartitionSpec as P
 
 D = 1536
@@ -69,7 +71,7 @@
     return jnp.dot(left, piece, preferred_element_type=jnp.float32)
 
 
-def local(
+def plain(
     x_in,
     attn_gain,
     moe_gain,
@@ -191,6 +193,534 @@
     )
 
 
+F32 = jnp.float32
+BF16 = jnp.bfloat16
+STAT = 128
+WIDE = KVD + STAT
+VMEM = pl.BlockSpec(memory_space=pltpu.VMEM)
+SMEM = pl.BlockSpec(memory_space=pltpu.SMEM)
+
+
+def kernel_call(body, out_shape, in_specs, scratch=(), vmem_mib=24):
+    many = isinstance(out_shape, (list, tuple))
+    return pl.pallas_call(
+        body,
+        out_shape=out_shape,
+        in_specs=in_specs,
+        out_specs=[VMEM] * len(out_shape) if many else VMEM,
+        scratch_shapes=list(scratch),
+        compiler_params=pltpu.CompilerParams(vmem_limit_bytes=vmem_mib * 2**20),
+    )
+
+
+def iota(shape, dim):
+    return lax.broadcasted_iota(jnp.int32, shape, dim)
+
+
+def split3(value):
+    high = value.astype(BF16).astype(F32)
+    rest = value - high
+    middle = rest.astype(BF16).astype(F32)
+    return high, middle, rest - middle
+
+
+def rows_of(ref):
+    return jnp.concatenate([ref[r].astype(F32) for r in range(ref.shape[0])], axis=0)
+
+
+def xor_pairs(size, mask):
+    return [(i, i ^ mask) for i in range(size)]
+
+
+def swap(value, axis, mask):
+    return lax.ppermute(value, axis, xor_pairs(lax.axis_size(axis), mask))
+
+
+def project_kernel(
+    x_ref, gain_ref, w_ref, cos_ref, sin_ref, routes_ref, weights_ref, me_ref, heads_ref, *pack_refs
+):
+    x = rows_of(x_ref)
+    row_count = x.shape[0]
+    power = jnp.mean(x * x, axis=-1, keepdims=True)
+    normed = (x * lax.rsqrt(power + EPS) * gain_ref[...]).astype(BF16)
+    projected = jnp.dot(normed, w_ref[...], preferred_element_type=F32)
+    heads = w_ref.shape[1] // HD
+    cosine, sine = cos_ref[...], sin_ref[...]
+    for i in range(heads):
+        one = projected[:, i * HD : (i + 1) * HD]
+        both = jnp.concatenate([one, one], axis=1)
+        turned = both * cosine + pltpu.roll(both, HD // 2, 1) * sine
+        rotated = me_ref[0] * heads + i < HEADS + KVH
+        heads_ref[i] = jnp.where(rotated, turned, both).astype(BF16)
+    high, middle, low = split3(rows_of(weights_ref))
+    routing = jnp.concatenate(
+        [
+            rows_of(routes_ref),
+            high,
+            middle,
+            low,
+            jnp.zeros((row_count, STAT - 4 * TOP), F32),
+        ],
+        axis=1,
+    )
+    groups = len(pack_refs)
+    width = D // groups
+    for k in range(groups):
+        start = pl.multiple_of((me_ref[1] ^ k) * width, STAT)
+        part = jnp.concatenate(
+            [x_ref[r, :, pl.ds(start, width)].astype(F32) for r in range(x_ref.shape[0])], axis=0
+        )
+        pack_refs[k][...] = jnp.concatenate([part, routing], axis=1).astype(BF16)
+
+
+def gathered_heads(me_ref, near_refs, far_refs, all_ref):
+    chips = len(near_refs)
+    heads = all_ref.shape[2]
+    core = me_ref[0] % 2
+    chip = me_ref[0] // 2
+    for k in range(chips):
+        all_ref[core, k] = near_refs[k][...]
+        all_ref[1 - core, k] = far_refs[k][...]
+
+    def head(h):
+        owner = h // heads
+        return all_ref[owner % 2, chip ^ (owner // 2), h % heads].astype(F32)
+
+    return head
+
+
+def paired(head, left, right):
+    a = head(left)
+    return jnp.where(iota(a.shape, 1) < HD, a, head(right))
+
+
+def query_rows(head, q_ref):
+    for g in range(GROUP):
+        for m in range(KVH // 2):
+            q_ref[g, :, m * STAT : (m + 1) * STAT] = paired(
+                head, GROUP * 2 * m + g, GROUP * (2 * m + 1) + g
+            )
+
+
+def expanded(q_ref, r):
+    rows = [q_ref[g, r * NSTEP : (r + 1) * NSTEP, :] for g in range(GROUP)]
+    base = jnp.concatenate(rows + [jnp.zeros((NSTEP, KVD), F32)], axis=0)
+    owner = iota(base.shape, 1) // HD
+    return jnp.concatenate(
+        [jnp.where(owner == k, base, 0.0) for k in range(KVH)], axis=0
+    ).astype(BF16)
+
+
+def attend_part(query, keys, values, live):
+    scores = lax.dot_general(
+        query, keys, (((1,), (1,)), ((), ())), preferred_element_type=F32
+    ) * (HD ** (-0.5))
+    scores = jnp.where(live, scores, NEG)
+    top = jnp.max(scores, axis=1, keepdims=True)
+    exp_scores = jnp.where(live, jnp.exp(scores - top), 0.0)
+    total = jnp.sum(exp_scores, axis=1, keepdims=True)
+    sums = jnp.dot(exp_scores.astype(BF16), values, preferred_element_type=F32)
+    block = (GROUP + 1) * NSTEP
+    owner = iota((block, KVD), 1) // HD
+    lane = iota((block, STAT), 1)
+    own_sums = jnp.zeros((block, KVD), F32)
+    stats = jnp.zeros((block, STAT), F32)
+    for k in range(KVH):
+        rows = slice(k * block, (k + 1) * block)
+        own_sums = jnp.where(owner == k, sums[rows], own_sums)
+        value = jnp.where(lane < 3 * KVH, top[rows], total[rows])
+        stats = jnp.where(lane % KVH == k, value, stats)
+    high, middle, low = split3(stats)
+    part = (lane // KVH) % 3
+    return own_sums, jnp.where(part == 0, high, jnp.where(part == 1, middle, low))
+
+
+def place_rows(part_ref, r, row_count, own_sums, stats):
+    for g in range(GROUP):
+        rows = slice(g * row_count + r * NSTEP, g * row_count + (r + 1) * NSTEP)
+        part_ref[rows, :KVD] = own_sums[g * NSTEP : (g + 1) * NSTEP]
+        part_ref[rows, KVD:] = stats[g * NSTEP : (g + 1) * NSTEP]
+
+
+def attend_kernel(chips, *refs):
+    near_refs, far_refs = refs[:chips], refs[chips : 2 * chips]
+    me_ref, pages_ref, lengths_ref, k_ref, v_ref, out_ref, all_ref, q_ref, part_ref = refs[
+        2 * chips :
+    ]
+    head = gathered_heads(me_ref, near_refs, far_refs, all_ref)
+    query_rows(head, q_ref)
+    requests, slots = k_ref.shape[0], k_ref.shape[1]
+    lane = iota((1, slots), 1)
+    for r in range(requests):
+        page = jnp.zeros((1, slots), jnp.int32)
+        for j in range(slots // PAGE):
+            page = jnp.where(lane // PAGE == j, pages_ref[r, j], page)
+        live = page * PAGE + lane % PAGE < lengths_ref[r]
+        own_sums, stats = attend_part(expanded(q_ref, r), k_ref[r], v_ref[r], live)
+        place_rows(part_ref, r, requests * NSTEP, own_sums, stats)
+    out_ref[...] = part_ref[...].astype(BF16)
+
+
+def fresh_kernel(chips, *refs):
+    near_refs, far_refs = refs[:chips], refs[chips : 2 * chips]
+    me_ref, out_ref, all_ref, q_ref, part_ref = refs[2 * chips :]
+    head = gathered_heads(me_ref, near_refs, far_refs, all_ref)
+    query_rows(head, q_ref)
+    row_count = q_ref.shape[1]
+    pad = jnp.zeros((STAT - row_count, KVD), F32)
+
+    def new_rows(first):
+        pieces = [paired(head, first + 2 * m, first + 2 * m + 1) for m in range(KVH // 2)]
+        return jnp.concatenate([jnp.concatenate(pieces, axis=1), pad], axis=0).astype(BF16)
+
+    keys, values = new_rows(HEADS), new_rows(HEADS + KVH)
+    shape = ((GROUP + 1) * NSTEP * KVH, STAT)
+    slot, step = iota(shape, 1), iota(shape, 0) % NSTEP
+    for r in range(row_count // NSTEP):
+        live = (slot // NSTEP == r) & (slot % NSTEP <= step)
+        own_sums, stats = attend_part(expanded(q_ref, r), keys, values, live)
+        place_rows(part_ref, r, row_count, own_sums, stats)
+    out_ref[...] = part_ref[...]
+
+
+def merge_kernel(count, *refs):
+    part_refs = refs[:count]
+    fresh_ref, x_ref, w_ref, me_ref, out_ref, share_ref = refs[count:]
+    parts = [ref[...].astype(F32) for ref in part_refs] + [fresh_ref[...]]
+    tops, totals = [], []
+    for part in parts:
+        stats = part[:, KVD:]
+        full = stats + (
+            pltpu.roll(stats, STAT - KVH, 1) + pltpu.roll(stats, STAT - 2 * KVH, 1)
+        )
+        tops.append(full)
+        totals.append(pltpu.roll(full, STAT - 3 * KVH, 1))
+    highest = tops[0]
+    for top in tops[1:]:
+        highest = jnp.maximum(highest, top)
+    factors = [jnp.exp(top - highest) for top in tops]
+    denominator = factors[0] * totals[0]
+    for factor, total in zip(factors[1:], totals[1:]):
+        denominator = denominator + factor * total
+    inverse = 1.0 / denominator
+    row_total = parts[0].shape[0]
+    left = iota((row_total, STAT), 1) < HD
+    columns = []
+    for m in range(KVH // 2):
+        value = jnp.zeros((row_total, STAT), F32)
+        for part, factor in zip(parts, factors):
+            spread = jnp.where(left, factor[:, 2 * m : 2 * m + 1], factor[:, 2 * m + 1 : 2 * m + 2])
+            value = value + spread * part[:, m * STAT : (m + 1) * STAT]
+        spread = jnp.where(left, inverse[:, 2 * m : 2 * m + 1], inverse[:, 2 * m + 1 : 2 * m + 2])
+        columns.append(value * spread)
+    attended = jnp.concatenate(columns, axis=1)
+    out_ref[...] = attended.astype(BF16)
+    row_count = row_total // GROUP
+    width = w_ref.shape[1]
+    share = jnp.zeros((row_count, width), F32)
+    for g in range(GROUP):
+        share = share + jnp.dot(
+            attended[g * row_count : (g + 1) * row_count].astype(BF16),
+            group_weight(w_ref, g),
+            preferred_element_type=F32,
+        )
+    start = pl.multiple_of((me_ref[0] // 2) * (2 * width), STAT)
+    chunk = jnp.concatenate(
+        [x_ref[r, :, pl.ds(start, 2 * width)].astype(F32) for r in range(x_ref.shape[0])], axis=0
+    )
+    share_ref[...] = share + jnp.where(me_ref[0] % 2 == 0, chunk[:, :width], chunk[:, width:])
+
+
+def group_weight(w_ref, g):
+    return jnp.concatenate(
+        [w_ref[(k * GROUP + g) * HD : (k * GROUP + g + 1) * HD, :] for k in range(KVH)], axis=0
+    )
+
+
+def across(column, eye):
+    return jnp.sum(jnp.where(eye, column, 0.0), axis=0, keepdims=True)
+
+
+def gate_kernel(groups, *refs):
+    attended_refs, pack_refs = refs[:groups], refs[groups : 2 * groups]
+    near_ref, far_ref, gain_ref, w_ref, me_ref = refs[2 * groups : 2 * groups + 5]
+    message_refs = refs[2 * groups + 5 : 3 * groups + 5]
+    placed_ref, scale_ref, full_ref = refs[3 * groups + 5 :]
+    pieces = [ref[...].astype(F32) for ref in attended_refs]
+    packs = [ref[...].astype(F32) for ref in pack_refs]
+    row_count = packs[0].shape[0]
+    tokens = groups * row_count
+    width = near_ref.shape[1]
+    near = jnp.zeros((tokens, width), F32)
+    far = jnp.zeros((tokens, width), F32)
+    for g in range(GROUP):
+        rows = jnp.concatenate(
+            [piece[g * row_count : (g + 1) * row_count] for piece in pieces], axis=0
+        ).astype(BF16)
+        near = near + jnp.dot(rows, group_weight(near_ref, g), preferred_element_type=F32)
+        far = far + jnp.dot(rows, group_weight(far_ref, g), preferred_element_type=F32)
+    first = me_ref[0] % 2 == 0
+    mixed = jnp.concatenate([jnp.where(first, near, far), jnp.where(first, far, near)], axis=1)
+    resid = jnp.concatenate([pack[:, : 2 * width] for pack in packs], axis=0) + mixed
+    power = jnp.sum(resid * resid, axis=1, keepdims=True)
+    start = pl.multiple_of(me_ref[1] * (2 * width), STAT)
+    scaled = (resid * gain_ref[:, pl.ds(start, 2 * width)]).astype(BF16)
+
+    routing = jnp.concatenate([pack[:, 2 * width :] for pack in packs], axis=0)
+    chosen = routing[:, :TOP]
+    gates = routing[:, TOP : 2 * TOP] + (
+        routing[:, 2 * TOP : 3 * TOP] + routing[:, 3 * TOP : 4 * TOP]
+    )
+    experts = w_ref.shape[0]
+    eye = iota((tokens, tokens), 0) == iota((tokens, tokens), 1)
+    earlier = (iota((tokens, tokens), 0) < iota((tokens, tokens), 1)) & (
+        iota((tokens, tokens), 0) // row_count == iota((tokens, tokens), 1) // row_count
+    )
+    slots = groups * CAP
+    shape = (slots, tokens)
+    home = (iota(shape, 1) // row_count) ^ me_ref[1]
+    slot = iota(shape, 0)
+    same_group = slot // CAP == home
+    ordinal_of_slot = (slot % CAP).astype(F32)
+    placed, scales = [], []
+    for e in range(experts):
+        match = chosen == (me_ref[0] * experts + e).astype(F32)
+        routed = jnp.max(jnp.where(match, 1.0, 0.0), axis=1, keepdims=True)
+        scale = jnp.sum(jnp.where(match, gates, 0.0), axis=1, keepdims=True)
+        ordinal = across(routed, earlier)
+        here = same_group & (across(routed, eye) > 0.5) & (ordinal_of_slot == ordinal)
+        placed.append(jnp.where(here, 1.0, 0.0))
+        scales.append(jnp.sum(jnp.where(here, across(scale, eye), 0.0), axis=1, keepdims=True))
+    placed = jnp.concatenate(placed, axis=0).astype(BF16)
+    placed_ref[...] = placed
+    scale_ref[...] = jnp.broadcast_to(jnp.concatenate(scales, axis=0), scale_ref.shape)
+    taken = jnp.dot(placed, scaled, preferred_element_type=F32).astype(BF16)
+    for e in range(experts):
+        full_ref[e * slots : (e + 1) * slots, :] = jnp.dot(
+            taken[e * slots : (e + 1) * slots], w_ref[e], preferred_element_type=F32
+        )
+    parts = split3(across(power, eye))
+    row = iota((16, tokens), 0)
+    power_rows = jnp.where(
+        row == 0, parts[0], jnp.where(row == 1, parts[1], jnp.where(row == 2, parts[2], 0.0))
+    ).astype(BF16)
+    slot_power = lax.dot_general(
+        power_rows, placed, (((1,), (1,)), ((), ())), preferred_element_type=F32
+    ).astype(BF16)
+    total_slots = experts * slots
+    piece = FFE // groups
+    for k in range(groups):
+        begin = pl.multiple_of((me_ref[1] ^ k) * piece, STAT)
+        message_refs[k][:total_slots, :piece] = full_ref[:, pl.ds(begin, piece)].astype(BF16)
+        message_refs[k][:total_slots, piece:] = full_ref[:, pl.ds(begin + FFE, piece)].astype(BF16)
+        message_refs[k][total_slots:, :total_slots] = slot_power
+        message_refs[k][total_slots:, total_slots:] = jnp.zeros(
+            (16, 2 * piece - total_slots), BF16
+        )
+
+
+def down_kernel(groups, *refs):
+    message_refs = refs[:groups]
+    own_ref = refs[groups]
+    down_refs = refs[groups + 1 : 2 * groups]
+    placed_ref, scale_ref, me_ref = refs[2 * groups : 2 * groups + 3]
+    out_refs = refs[2 * groups + 3 :]
+    total_slots = placed_ref.shape[0]
+    piece = message_refs[0].shape[1] // 2
+    summed = message_refs[0][...].astype(F32)
+    for ref in message_refs[1:]:
+        summed = summed + ref[...].astype(F32)
+    stats = summed[total_slots:, :total_slots]
+    power = stats[0:1] + (stats[1:2] + stats[2:3])
+    eye = iota((total_slots, total_slots), 0) == iota((total_slots, total_slots), 1)
+    power = jnp.sum(jnp.where(eye, power, 0.0), axis=1, keepdims=True)
+    gate_up = summed[:total_slots] * lax.rsqrt(power / D + EPS)
+    gate, up = gate_up[:, :piece], gate_up[:, piece:]
+    hidden = (gate / (1.0 + jnp.exp(-gate)) * up).astype(BF16)
+    experts = own_ref.shape[0]
+    slots = total_slots // experts
+    placed = placed_ref[...]
+    scale = scale_ref[...][:, :1]
+    begin = pl.multiple_of(me_ref[1] * piece, STAT)
+    width = own_ref.shape[2]
+    row_count = out_refs[0].shape[0]
+    for k in range(groups):
+        produced = []
+        for e in range(experts):
+            weight = own_ref[e, pl.ds(begin, piece), :] if k == 0 else down_refs[k - 1][e]
+            produced.append(
+                jnp.dot(
+                    hidden[e * slots : (e + 1) * slots], weight, preferred_element_type=F32
+                )
+            )
+        produced = (jnp.concatenate(produced, axis=0) * scale).astype(BF16)
+        total = lax.dot_general(
+            placed, produced, (((0,), (0,)), ((), ())), preferred_element_type=F32
+        )
+        column = pl.multiple_of((me_ref[1] ^ k) * width, STAT)
+        for j in range(groups):
+            out_refs[j][:, pl.ds(column, width)] = total[
+                j * row_count : (j + 1) * row_count
+            ].astype(BF16)
+
+
+def spread_kernel(groups, *refs):
+    total = refs[0][...].astype(F32)
+    for ref in refs[1:groups]:
+        total = total + ref[...].astype(F32)
+    out_ref = refs[groups]
+    width = out_ref.shape[2]
+    for s in range(out_ref.shape[0]):
+        out_ref[s] = total[:, s * width : (s + 1) * width].astype(BF16)
+
+
+def final_kernel(share_ref, arrived_ref, out_ref):
+    total = share_ref[...]
+    for s in range(arrived_ref.shape[0]):
+        total = total + arrived_ref[s].astype(F32)
+    for r in range(out_ref.shape[0]):
+        out_ref[r] = total[r * NSTEP : (r + 1) * NSTEP].astype(BF16)
+
+
+def staged(
+    x_in,
+    attn_gain,
+    moe_gain,
+    w_qkv,
+    w_o,
+    cache_k,
+    cache_v,
+    page_map,
+    lengths,
+    routes,
+    route_weights,
+    w_gate_up,
+    w_down,
+):
+    requests = x_in.shape[0]
+    row_count = requests * NSTEP
+    members, groups = lax.axis_size("seq"), lax.axis_size("req")
+    chips = members // 2
+    me = jnp.stack([lax.axis_index("seq"), lax.axis_index("req")]).astype(jnp.int32)
+    heads = w_qkv.shape[1] // HD
+    width = w_o.shape[1]
+
+    position = (lengths[:, None] + jnp.arange(NSTEP, dtype=jnp.int32)[None, :]).astype(F32)
+    half = HD // 2
+    rates = jnp.exp(jnp.arange(half, dtype=F32) * (-2.0 * math.log(10000.0) / HD))
+    angle = position.reshape(row_count, 1) * jnp.tile(rates, STAT // half)[None, :]
+    sign = jnp.where(jnp.arange(STAT) % HD < half, -1.0, 1.0).astype(F32)
+    cosine, sine = jnp.cos(angle), jnp.sin(angle) * sign[None, :]
+
+    own_heads, *packs = kernel_call(
+        project_kernel,
+        [jax.ShapeDtypeStruct((heads, row_count, 2 * HD), BF16)]
+        + [jax.ShapeDtypeStruct((row_count, 2 * width + STAT), BF16)] * groups,
+        [VMEM] * 7 + [SMEM],
+    )(x_in, attn_gain[None], w_qkv, cosine, sine, routes, route_weights, me)
+    near = [own_heads] + [swap(own_heads, "seq", 2 * k) for k in range(1, chips)]
+    far = [swap(piece, "seq", 1) for piece in near]
+
+    packs = [packs[0]] + [swap(packs[k], "req", k) for k in range(1, groups)]
+    moved = w_o
+    place = ("seq", "req")
+    arriving = [
+        lax.ppermute(
+            w_o,
+            place,
+            [
+                ((2 * z + c) * groups + z, (2 * (z ^ k) + c) * groups + z)
+                for z in range(groups)
+                for c in range(2)
+            ],
+        )
+        for k in range(1, chips)
+    ]
+    total = arriving[0]
+    for piece in arriving[1:]:
+        total = total + piece
+    near_w_o = jnp.where(me[0] // 2 == me[1], w_o, total)
+    far_w_o = swap(near_w_o, "seq", 1)
+    depth = w_down.shape[1] // groups
+    downs = [
+        swap(lax.dynamic_slice_in_dim(w_down, (me[1] ^ k) * depth, depth, 1), "req", k)
+        for k in range(1, groups)
+    ]
+
+    head_scratch = [
+        pltpu.VMEM((2, chips, heads, row_count, 2 * HD), BF16),
+        pltpu.VMEM((GROUP, row_count, KVD), F32),
+        pltpu.VMEM((GROUP * row_count, WIDE), F32),
+    ]
+    part = kernel_call(
+        lambda *refs: attend_kernel(chips, *refs),
+        jax.ShapeDtypeStruct((GROUP * row_count, WIDE), BF16),
+        [VMEM] * (2 * chips) + [SMEM] * 3 + [VMEM] * 2,
+        head_scratch,
+    )(*near, *far, me, page_map, lengths, cache_k, cache_v)
+    fresh = kernel_call(
+        lambda *refs: fresh_kernel(chips, *refs),
+        jax.ShapeDtypeStruct((GROUP * row_count, WIDE), F32),
+        [VMEM] * (2 * chips) + [SMEM],
+        head_scratch,
+    )(*near, *far, me)
+    parts = [part] + [swap(part, "seq", 2 * k) for k in range(1, chips)]
+    parts = parts + [swap(piece, "seq", 1) for piece in parts]
+    attended, share = kernel_call(
+        lambda *refs: merge_kernel(members, *refs),
+        [
+            jax.ShapeDtypeStruct((GROUP * row_count, KVD), BF16),
+            jax.ShapeDtypeStruct((row_count, width), F32),
+        ],
+        [VMEM] * (members + 3) + [SMEM],
+    )(*parts, fresh, x_in, w_o, me)
+    everyone = [attended] + [swap(attended, "req", k) for k in range(1, groups)]
+
+    experts = w_gate_up.shape[0]
+    total_slots = experts * groups * CAP
+    piece = FFE // groups
+    *messages, placed, scale = kernel_call(
+        lambda *refs: gate_kernel(groups, *refs),
+        [jax.ShapeDtypeStruct((total_slots + 16, 2 * piece), BF16)] * groups
+        + [
+            jax.ShapeDtypeStruct((total_slots, groups * row_count), BF16),
+            jax.ShapeDtypeStruct((total_slots, STAT), F32),
+        ],
+        [VMEM] * (2 * groups + 4) + [SMEM],
+        [pltpu.VMEM((total_slots, 2 * FFE), F32)],
+    )(*everyone, *packs, near_w_o, far_w_o, moe_gain[None], w_gate_up, me)
+    messages = [messages[0]] + [swap(messages[k], "req", k) for k in range(1, groups)]
+    outs = kernel_call(
+        lambda *refs: down_kernel(groups, *refs),
+        [jax.ShapeDtypeStruct((row_count, D), BF16)] * groups,
+        [VMEM] * (2 * groups + 2) + [SMEM],
+    )(*messages, w_down, *downs, placed, scale, me)
+    outs = [outs[0]] + [swap(outs[k], "req", k) for k in range(1, groups)]
+    spread = kernel_call(
+        lambda *refs: spread_kernel(groups, *refs),
+        jax.ShapeDtypeStruct((members, row_count, width), BF16),
+        [VMEM] * groups,
+    )(*outs)
+    arrived = lax.all_to_all(spread, "seq", 0, 0, tiled=True)
+    return kernel_call(
+        final_kernel, jax.ShapeDtypeStruct((requests, NSTEP, width), BF16), [VMEM] * 2
+    )(share, arrived)
+
+
+def local(*args):
+    w_qkv, w_o, page_map, w_gate_up = args[3], args[4], args[7], args[11]
+    members, groups = lax.axis_size("seq"), lax.axis_size("req")
+    fits = (
+        members == 2 * groups
+        and groups & (groups - 1) == 0
+        and w_qkv.shape[1] % HD == 0
+        and (FFE // groups) % STAT == 0
+        and (2 * w_o.shape[1]) % STAT == 0
+        and w_gate_up.shape[0] * groups * CAP <= 2 * (FFE // groups)
+    )
+    return staged(*args) if fits else plain(*args)
+
+
 def solution(mesh):
     in_specs = (
         P("req", None, None),

time: 315 us -> 155 us (0.49)
  waiting for transfers between devices: 135 us -> 45.8 us
  starting transfers between devices: 3.61 us -> 55.3 us
  local copies, waits for them, and re-layouts: 77.9 us -> 29.9 us
  other arithmetic: 28.6 us -> 1.6 us
  matrix products: 24.1 us -> 0 us
  blocking collectives: 29.3 us -> 7.79 us
  between operations: 13.5 us -> 0.3 us
  Pallas kernels: 0 us -> 12.5 us
    ppermute x0 -> x33, starting transfers between devices: none -> 55.3 us  [the longest x30 45.1 us: swap(): return lax.ppermute(value, axis, xor_pairs(lax.axis_size(axis), mask))]
    all_gather x3 -> x0, waiting for transfers between devices: 48.7 us -> none  [the longest x1 48.7 us: local(): lax.all_gather(w_qkv, 'seq', axis=1, tiled=True)]
    ppermute x0 -> x33, waiting for transfers between devices: none -> 45.8 us  [the longest x30 28.7 us: swap(): return lax.ppermute(value, axis, xor_pairs(lax.axis_size(axis), mask))]
    psum x1 -> x0, waiting for transfers between devices: 41.9 us -> none  [local(): gate_up = lax.psum(partial_values, 'req')]
    unnamed x6 -> x0, waiting for transfers between devices: 35.5 us -> none
    dot_general x10 -> x0, matrix products: 24.1 us -> none  [the longest x2 9.39 us: project_with(): return jnp.dot(left, piece, preferred_element_type=jnp.float32)]
    add x16 -> x0, other arithmetic: 18.7 us -> none  [the longest x7 12.7 us: softmax_join(): joined = (left_part + right_part).reshape(row_count, -1)]
    all_gather x2 -> x0, blocking collectives: 17.9 us -> none  [combined_all(): pieces = jax.tree.map(lambda part: lax.all_gather(part, axis), value)]
  transfers between devices with their start and end apart: 6 -> 33, of which waited for: 4 -> 17; matrix products, arithmetic and copies ran while one was open for 26% -> 5% of each run, Pallas kernels for 0% -> 6%
where the time goes in v1:
time: 155 us; the launch traced here: 153 us
  starting transfers between devices  55.3 us (36%)
  waiting for transfers between devices  45.8 us (30%)
  local copies, waits for them, and re-layouts  29.9 us (19%)
  Pallas kernels  12.5 us (8%)
  blocking collectives  7.79 us (5%)
  other arithmetic  1.6 us (1%)
    ppermute x30, starting transfers between devices, swap(): return lax.ppermute(value, axis, xor_pairs(lax.axis_size(axis), mask))  45.1 us
    ppermute x30, waiting for transfers between devices, swap(): return lax.ppermute(value, axis, xor_pairs(lax.axis_size(axis), mask))  28.7 us
    unnamed x88, local copies, waits for them, and re-layouts  21.7 us
    ppermute x3, waiting for transfers between devices, staged(): lax.ppermute(w_o, place, [((2 * z + c) * groups + z, (2 * (z ^ k) + c) *...  17.1 us
    ppermute x3, starting transfers between devices, staged(): lax.ppermute(w_o, place, [((2 * z + c) * groups + z, (2 * (z ^ k) + c) *...  10.2 us
    all_to_all x1, blocking collectives, staged(): arrived = lax.all_to_all(spread, 'seq', 0, 0, tiled=True)  7.79 us
    ppermute x3, local copies, waits for them, and re-layouts, staged(): lax.ppermute(w_o, place, [((2 * z + c) * groups + z, (2 * (z ^ k) + c) *...  3.82 us
  transfers between devices with their start and end apart: 33, of which 17 were waited for; matrix products, arithmetic and copies ran while one was open for 5% of the time, Pallas kernels for 6%

profile of v1, /device:TPU:0, one launch (start us, length us, event | category | flops | bytes accessed | tf_op | source)
XLA Modules:
  0.0 153.1 jit_solution(12950508226913544439)
XLA Ops:
  0.0 6.0 %collective-permute-start.22 = (bf16[1536,192]{0,1:T(8,128)(2,1)}, bf16[1536,192]{0,1:T(8,128)(2,1)S(1)}, u32[]{:S(2)}, u32[]{:S(2)}) collective-permute-start(bf16[1536,192]{0,1:T(8,128)(2,1)} %param.17), channel_id=1, source_target_pairs={{0,24},{4,28},{9,17},{13,21},{18,10},{22,14},{27,3},{31,7}} | collective-permute-start | bytes 1769480 | tf_op jit(solution)/shard_map/ppermute | solution.py:628
  6.0 2.1 %collective-permute-start.20 = (bf16[1536,192]{0,1:T(8,128)(2,1)}, bf16[1536,192]{0,1:T(8,128)(2,1)}, u32[]{:S(2)}, u32[]{:S(2)}) collective-permute-start(bf16[1536,192]{0,1:T(8,128)(2,1)} %param.17), channel_id=1, source_target_pairs={{0,8},{4,12},{9,1},{13,5},{18,26},{22,30},{27,19},{31,23}} | collective-permute-start | bytes 1769480 | tf_op jit(solution)/shard_map/ppermute | solution.py:628
  8.1 2.1 %collective-permute-start.21 = (bf16[1536,192]{0,1:T(8,128)(2,1)}, bf16[1536,192]{0,1:T(8,128)(2,1)}, u32[]{:S(2)}, u32[]{:S(2)}) collective-permute-start(bf16[1536,192]{0,1:T(8,128)(2,1)} %param.17), channel_id=1, source_target_pairs={{0,16},{4,20},{9,25},{13,29},{18,2},{22,6},{27,11},{31,15}} | collective-permute-start | bytes 1769480 | tf_op jit(solution)/shard_map/ppermute | solution.py:628
  14.1 5.9 %collective-permute-done.22 = bf16[1536,192]{0,1:T(8,128)(2,1)S(1)} collective-permute-done((bf16[1536,192]{0,1:T(8,128)(2,1)}, bf16[1536,192]{0,1:T(8,128)(2,1)S(1)}, u32[]{:S(2)}, u32[]{:S(2)}) %collective-permute-start.22) | collective-permute-done | bytes 589856 | tf_op jit(solution)/shard_map/ppermute | solution.py:628
  20.2 11.2 %collective-permute-done.20 = bf16[1536,192]{0,1:T(8,128)(2,1)} collective-permute-done((bf16[1536,192]{0,1:T(8,128)(2,1)}, bf16[1536,192]{0,1:T(8,128)(2,1)}, u32[]{:S(2)}, u32[]{:S(2)}) %collective-permute-start.20) | collective-permute-done | bytes 589856 | tf_op jit(solution)/shard_map/ppermute | solution.py:628
  32.8 2.2 %copy.29 = bf16[1536,192]{1,0:T(8,128)(2,1)} copy(bf16[1536,192]{0,1:T(8,128)(2,1)} %collective-permute-done.21) | data formatting | bytes 1179648 | tf_op jit(solution)/shard_map/ppermute | solution.py:628
  41.1 2.5 %collective-permute-start = (bf16[5,24,128]{2,1,0:T(8,128)(2,1)S(1)}, bf16[5,24,128]{2,1,0:T(8,128)(2,1)S(1)}, u32[]{:S(2)}, u32[]{:S(2)}) collective-permute-start(bf16[5,24,128]{2,1,0:T(8,128)(2,1)S(1)} %get-tuple-element.22.refs_0_), channel_id=1, source_target_pairs={{0,8},{4,12},{8,0},{12,4},{16,24},{20,28},{24,16},{28,20},{1,9},{5... | collective-permute-start | bytes 92168 | tf_op jit(solution)/shard_map/ppermute | solution.py:236
  45.6 2.2 %collective-permute-done.1.refs_2_ = bf16[5,24,128]{2,1,0:T(8,128)(2,1)S(1)} collective-permute-done((bf16[5,24,128]{2,1,0:T(8,128)(2,1)S(1)}, bf16[5,24,128]{2,1,0:T(8,128)(2,1)S(1)}, u32[]{:S(2)}, u32[]{:S(2)}) %collective-permute-start.1) | collective-permute-done | bytes 30752 | tf_op jit(solution)/shard_map/ppermute | solution.py:236
  49.1 2.6 %collective-permute-start.18 = (bf16[24,512]{1,0:T(8,128)(2,1)S(1)}, bf16[24,512]{1,0:T(8,128)(2,1)S(1)}, u32[]{:S(2)}, u32[]{:S(2)}) collective-permute-start(bf16[24,512]{1,0:T(8,128)(2,1)S(1)} %get-tuple-element.27), channel_id=1, source_target_pairs={{0,2},{1,3},{2,0},{3,1},{4,6},{5,7},{6,4},{7,5},{8,10},{9,11},{10,... | collective-permute-start | bytes 73736 | tf_op jit(solution)/shard_map/ppermute | solution.py:236
  55.6 2.1 %collective-permute-start.7 = (bf16[72,640]{1,0:T(8,128)(2,1)S(1)}, bf16[72,640]{1,0:T(8,128)(2,1)S(1)}, u32[]{:S(2)}, u32[]{:S(2)}) collective-permute-start(bf16[72,640]{1,0:T(8,128)(2,1)S(1)} %shard_map.128.refs_0_), channel_id=1, source_target_pairs={{0,8},{4,12},{8,0},{12,4},{16,24},{20,28},{24,16},{28,20},{1,9},{5... | collective-permute-start | bytes 276488 | tf_op jit(solution)/shard_map/ppermute | solution.py:236
  65.2 2.0 %collective-permute-start.29 = (bf16[4,128,384]{2,1,0:T(8,128)(2,1)}, bf16[4,128,384]{2,1,0:T(8,128)(2,1)}, u32[]{:S(2)}, u32[]{:S(2)}) collective-permute-start(bf16[4,128,384]{2,1,0:T(8,128)(2,1)} %get-tuple-element.39), channel_id=1, source_target_pairs={{0,3},{1,2},{2,1},{3,0},{4,7},{5,6},{6,5},{7,4},{8,11},{9,10},{10,... | collective-permute-start | bytes 1179656 | tf_op jit(solution)/shard_map/ppermute | solution.py:236
  77.9 2.7 %shard_map.130 = (bf16[72,512]{1,0:T(8,128)(2,1)}, f32[24,192]{1,0:T(8,128)S(1)}) custom-call(bf16[72,640]{1,0:T(8,128)(2,1)S(1)} %shard_map.128.refs_0_, bf16[72,640]{1,0:T(8,128)(2,1)S(1)} %collective-permute-done.7.refs_1_, bf16[72,640]{1,0:T(8,128)(2,1)S(1)} %collective-permute-done.8.refs_2_, bf16[72,640]{1,0:T(8,128)(2,1)S(1)} %collective-permute-done.9.refs_3_, ...), custom_call_target="tpu_custom_call" | custom-call | tf_op jit(solution)/shard_map/pallas_call | solution.py:669
  81.3 8.1 %collective-permute-done.19.refs_7_ = bf16[24,512]{1,0:T(8,128)(2,1)S(1)} collective-permute-done((bf16[24,512]{1,0:T(8,128)(2,1)S(1)}, bf16[24,512]{1,0:T(8,128)(2,1)S(1)}, u32[]{:S(2)}, u32[]{:S(2)}) %collective-permute-start.19) | collective-permute-done | bytes 24608 | tf_op jit(solution)/shard_map/ppermute | solution.py:236
  90.0 14.1 %collective-permute-start.14 = (bf16[72,512]{1,0:T(8,128)(2,1)}, bf16[72,512]{1,0:T(8,128)(2,1)S(1)}, u32[]{:S(2)}, u32[]{:S(2)}) collective-permute-start(bf16[72,512]{1,0:T(8,128)(2,1)} %get-tuple-element.24.refs_0_), channel_id=1, source_target_pairs={{0,1},{1,0},{2,3},{3,2},{4,5},{5,4},{6,7},{7,6},{8,9},{9,8},{10,11... | collective-permute-start | bytes 221192 | tf_op jit(solution)/shard_map/ppermute | solution.py:236
  104.1 2.5 %collective-permute-done.14.refs_1_ = bf16[72,512]{1,0:T(8,128)(2,1)S(1)} collective-permute-done((bf16[72,512]{1,0:T(8,128)(2,1)}, bf16[72,512]{1,0:T(8,128)(2,1)S(1)}, u32[]{:S(2)}, u32[]{:S(2)}) %collective-permute-start.14) | collective-permute-done | bytes 73760 | tf_op jit(solution)/shard_map/ppermute | solution.py:236
  108.8 2.9 %collective-permute-start.16 = (bf16[72,512]{1,0:T(8,128)(2,1)}, bf16[72,512]{1,0:T(8,128)(2,1)}, u32[]{:S(2)}, u32[]{:S(2)}) collective-permute-start(bf16[72,512]{1,0:T(8,128)(2,1)} %get-tuple-element.24.refs_0_), channel_id=1, source_target_pairs={{0,3},{1,2},{2,1},{3,0},{4,7},{5,6},{6,5},{7,4},{8,11},{9,10},{10,... | collective-permute-start | bytes 221192 | tf_op jit(solution)/shard_map/ppermute | solution.py:236
  115.3 1.9 %copy-done.2 = bf16[4,384,1024]{2,1,0:T(8,128)(2,1)S(1)} copy-done((bf16[4,384,1024]{2,1,0:T(8,128)(2,1)S(1)}, bf16[4,384,1024]{2,1,0:T(8,128)(2,1)}, u32[]{:S(2)}) %copy-start.2) | copy-done | bytes 3145752
  121.0 2.4 %shard_map.131 = (bf16[208,256]{1,0:T(8,128)(2,1)S(1)}, bf16[208,256]{1,0:T(8,128)(2,1)S(1)}, bf16[208,256]{1,0:T(8,128)(2,1)S(1)}, bf16[208,256]{1,0:T(8,128)(2...) custom-call(bf16[72,512]{1,0:T(8,128)(2,1)} %get-tuple-element.24.refs_0_, bf16[72,512]{1,0:T(8,128)(2,1)S(1)} %copy-done.24, ...), custom_call_target="tpu_custom_call" | custom-call | tf_op jit(solution)/shard_map/pallas_call | solution.py:682
  124.6 2.3 %collective-permute-start.25 = (bf16[208,256]{1,0:T(8,128)(2,1)S(1)}, bf16[208,256]{1,0:T(8,128)(2,1)S(1)}, u32[]{:S(2)}, u32[]{:S(2)}) collective-permute-start(bf16[208,256]{1,0:T(8,128)(2,1)S(1)} %get-tuple-element.31), channel_id=1, source_target_pairs={{0,2},{1,3},{2,0},{3,1},{4,6},{5,7},{6,4},{7,5},{8,10},{9,11},{10,... | collective-permute-start | bytes 319496 | tf_op jit(solution)/shard_map/ppermute | solution.py:236
  128.5 3.6 %collective-permute-done.25.refs_2_ = bf16[208,256]{1,0:T(8,128)(2,1)S(1)} collective-permute-done((bf16[208,256]{1,0:T(8,128)(2,1)S(1)}, bf16[208,256]{1,0:T(8,128)(2,1)S(1)}, u32[]{:S(2)}, u32[]{:S(2)}) %collective-permute-start.25) | collective-permute-done | bytes 106528 | tf_op jit(solution)/shard_map/ppermute | solution.py:236
  133.5 2.3 %shard_map.132 = (bf16[24,1536]{1,0:T(8,128)(2,1)S(1)}, bf16[24,1536]{1,0:T(8,128)(2,1)S(1)}, bf16[24,1536]{1,0:T(8,128)(2,1)S(1)}, bf16[24,1536]{1,0:T(8,128)(2,1)S(1)}) custom-call(bf16[208,256]{1,0:T(8,128)(2,1)S(1)} %get-tuple-element.29.refs_0_, bf16[208,256]{1,0:T(8,128)(2,1)S(1)} %collective-permute-done.24.refs_1_, ...), custom_call_target="tpu_custom_call" | custom-call | tf_op jit(solution)/shard_map/pallas_call | solution.py:693
  138.3 1.9 %collective-permute-start.32 = (bf16[24,1536]{1,0:T(8,128)(2,1)S(1)}, bf16[24,1536]{1,0:T(8,128)(2,1)S(1)}, u32[]{:S(2)}, u32[]{:S(2)}) collective-permute-start(bf16[24,1536]{1,0:T(8,128)(2,1)S(1)} %get-tuple-element.38), channel_id=1, source_target_pairs={{0,3},{1,2},{2,1},{3,0},{4,7},{5,6},{6,5},{7,4},{8,11},{9,10},{10,... | collective-permute-start | bytes 221192 | tf_op jit(solution)/shard_map/ppermute | solution.py:236
  140.2 3.1 %collective-permute-done.31.refs_2_ = bf16[24,1536]{1,0:T(8,128)(2,1)S(1)} collective-permute-done((bf16[24,1536]{1,0:T(8,128)(2,1)S(1)}, bf16[24,1536]{1,0:T(8,128)(2,1)S(1)}, u32[]{:S(2)}, u32[]{:S(2)}) %collective-permute-start.31) | collective-permute-done | bytes 73760 | tf_op jit(solution)/shard_map/ppermute | solution.py:236
  144.7 7.8 %all_to_all.5.arrived_ref = bf16[8,24,192]{2,1,0:T(8,128)(2,1)S(1)} all-to-all(bf16[8,24,192]{2,1,0:T(8,128)(2,1)S(1)} %shard_map.133), channel_id=1, replica_groups=mesh['seq'=8,'req'=4] {'seq'}, dimensions={0} | all-to-all | bytes 147456 | tf_op jit(solution)/shard_map/all_to_all | solution.py:704
  (156 shorter events, 56.4 us)
Async XLA Ops:
  0.0 20.0 %collective-permute-start.22 = (bf16[1536,192]{0,1:T(8,128)(2,1)}, bf16[1536,192]{0,1:T(8,128)(2,1)S(1)}, u32[]{:S(2)}, u32[]{:S(2)}) collective-permute-start(bf16[1536,192]{0,1:T(8,128)(2,1)} %param.17), channel_id=1, source_target_pairs={{0,24},{4,28},{9,17},{13,21},{18,10},{22,14},{27,3},{31,7}} | collective-permute-start | bytes 1769480 | tf_op jit(solution)/shard_map/ppermute | solution.py:628
  6.0 25.5 %collective-permute-start.20 = (bf16[1536,192]{0,1:T(8,128)(2,1)}, bf16[1536,192]{0,1:T(8,128)(2,1)}, u32[]{:S(2)}, u32[]{:S(2)}) collective-permute-start(bf16[1536,192]{0,1:T(8,128)(2,1)} %param.17), channel_id=1, source_target_pairs={{0,8},{4,12},{9,1},{13,5},{18,26},{22,30},{27,19},{31,23}} | collective-permute-start | bytes 1769480 | tf_op jit(solution)/shard_map/ppermute | solution.py:628
  8.1 24.7 %collective-permute-start.21 = (bf16[1536,192]{0,1:T(8,128)(2,1)}, bf16[1536,192]{0,1:T(8,128)(2,1)}, u32[]{:S(2)}, u32[]{:S(2)}) collective-permute-start(bf16[1536,192]{0,1:T(8,128)(2,1)} %param.17), channel_id=1, source_target_pairs={{0,16},{4,20},{9,25},{13,29},{18,2},{22,6},{27,11},{31,15}} | collective-permute-start | bytes 1769480 | tf_op jit(solution)/shard_map/ppermute | solution.py:628
  37.4 71.4 %collective-permute-start.23 = (bf16[1536,192]{0,1:T(8,128)(2,1)}, bf16[1536,192]{0,1:T(8,128)(2,1)}, u32[]{:S(2)}, u32[]{:S(2)}) collective-permute-start(bf16[1536,192]{0,1:T(8,128)(2,1)} %copy.32), channel_id=1, source_target_pairs={{0,4},{4,0},{8,12},{12,8},{16,20},{20,16},{24,28},{28,24},{1,5},{5... | collective-permute-start | bytes 1769480 | tf_op jit(solution)/shard_map/ppermute | solution.py:236
  41.1 4.5 %collective-permute-start = (bf16[5,24,128]{2,1,0:T(8,128)(2,1)S(1)}, bf16[5,24,128]{2,1,0:T(8,128)(2,1)S(1)}, u32[]{:S(2)}, u32[]{:S(2)}) collective-permute-start(bf16[5,24,128]{2,1,0:T(8,128)(2,1)S(1)} %get-tuple-element.22.refs_0_), channel_id=1, source_target_pairs={{0,8},{4,12},{8,0},{12,4},{16,24},{20,28},{24,16},{28,20},{1,9},{5... | collective-permute-start | bytes 92168 | tf_op jit(solution)/shard_map/ppermute | solution.py:236
  43.6 4.8 %collective-permute-start.2 = (bf16[5,24,128]{2,1,0:T(8,128)(2,1)S(1)}, bf16[5,24,128]{2,1,0:T(8,128)(2,1)S(1)}, u32[]{:S(2)}, u32[]{:S(2)}) collective-permute-start(bf16[5,24,128]{2,1,0:T(8,128)(2,1)S(1)} %get-tuple-element.22.refs_0_), channel_id=1, source_target_pairs={{0,24},{4,28},{8,16},{12,20},{16,8},{20,12},{24,0},{28,4},{1,25},{... | collective-permute-start | bytes 92168 | tf_op jit(solution)/shard_map/ppermute | solution.py:236
  48.4 9.3 %collective-permute-start.17 = (bf16[24,512]{1,0:T(8,128)(2,1)S(1)}, bf16[24,512]{1,0:T(8,128)(2,1)S(1)}, u32[]{:S(2)}, u32[]{:S(2)}) collective-permute-start(bf16[24,512]{1,0:T(8,128)(2,1)S(1)} %get-tuple-element.26), channel_id=1, source_target_pairs={{0,1},{1,0},{2,3},{3,2},{4,5},{5,4},{6,7},{7,6},{8,9},{9,8},{10,11... | collective-permute-start | bytes 73736 | tf_op jit(solution)/shard_map/ppermute | solution.py:236
  49.1 11.3 %collective-permute-start.18 = (bf16[24,512]{1,0:T(8,128)(2,1)S(1)}, bf16[24,512]{1,0:T(8,128)(2,1)S(1)}, u32[]{:S(2)}, u32[]{:S(2)}) collective-permute-start(bf16[24,512]{1,0:T(8,128)(2,1)S(1)} %get-tuple-element.27), channel_id=1, source_target_pairs={{0,2},{1,3},{2,0},{3,1},{4,6},{5,7},{6,4},{7,5},{8,10},{9,11},{10,... | collective-permute-start | bytes 73736 | tf_op jit(solution)/shard_map/ppermute | solution.py:236
  55.6 7.2 %collective-permute-start.7 = (bf16[72,640]{1,0:T(8,128)(2,1)S(1)}, bf16[72,640]{1,0:T(8,128)(2,1)S(1)}, u32[]{:S(2)}, u32[]{:S(2)}) collective-permute-start(bf16[72,640]{1,0:T(8,128)(2,1)S(1)} %shard_map.128.refs_0_), channel_id=1, source_target_pairs={{0,8},{4,12},{8,0},{12,4},{16,24},{20,28},{24,16},{28,20},{1,9},{5... | collective-permute-start | bytes 276488 | tf_op jit(solution)/shard_map/ppermute | solution.py:236
  57.7 6.1 %collective-permute-start.8 = (bf16[72,640]{1,0:T(8,128)(2,1)S(1)}, bf16[72,640]{1,0:T(8,128)(2,1)S(1)}, u32[]{:S(2)}, u32[]{:S(2)}) collective-permute-start(bf16[72,640]{1,0:T(8,128)(2,1)S(1)} %shard_map.128.refs_0_), channel_id=1, source_target_pairs={{0,16},{4,20},{8,24},{12,28},{16,0},{20,4},{24,8},{28,12},{1,17},{... | collective-permute-start | bytes 276488 | tf_op jit(solution)/shard_map/ppermute | solution.py:236
  57.7 6.1 %collective-permute-start.9 = (bf16[72,640]{1,0:T(8,128)(2,1)S(1)}, bf16[72,640]{1,0:T(8,128)(2,1)S(1)}, u32[]{:S(2)}, u32[]{:S(2)}) collective-permute-start(bf16[72,640]{1,0:T(8,128)(2,1)S(1)} %shard_map.128.refs_0_), channel_id=1, source_target_pairs={{0,24},{4,28},{8,16},{12,20},{16,8},{20,12},{24,0},{28,4},{1,25},{... | collective-permute-start | bytes 276488 | tf_op jit(solution)/shard_map/ppermute | solution.py:236
  61.0 65.9 %collective-permute-start.27 = (bf16[4,128,384]{2,1,0:T(8,128)(2,1)}, bf16[4,128,384]{2,1,0:T(8,128)(2,1)S(1)}, u32[]{:S(2)}, u32[]{:S(2)}) collective-permute-start(bf16[4,128,384]{2,1,0:T(8,128)(2,1)} %get-tuple-element.41), channel_id=1, source_target_pairs={{0,1},{1,0},{2,3},{3,2},{4,5},{5,4},{6,7},{7,6},{8,9},{9,8},{10,11... | collective-permute-start | bytes 1179656 | tf_op jit(solution)/shard_map/ppermute | solution.py:236
  64.4 63.5 %collective-permute-start.28 = (bf16[4,128,384]{2,1,0:T(8,128)(2,1)}, bf16[4,128,384]{2,1,0:T(8,128)(2,1)}, u32[]{:S(2)}, u32[]{:S(2)}) collective-permute-start(bf16[4,128,384]{2,1,0:T(8,128)(2,1)} %get-tuple-element.40), channel_id=1, source_target_pairs={{0,2},{1,3},{2,0},{3,1},{4,6},{5,7},{6,4},{7,5},{8,10},{9,11},{10,... | collective-permute-start | bytes 1179656 | tf_op jit(solution)/shard_map/ppermute | solution.py:236
  65.2 62.7 %collective-permute-start.29 = (bf16[4,128,384]{2,1,0:T(8,128)(2,1)}, bf16[4,128,384]{2,1,0:T(8,128)(2,1)}, u32[]{:S(2)}, u32[]{:S(2)}) collective-permute-start(bf16[4,128,384]{2,1,0:T(8,128)(2,1)} %get-tuple-element.39), channel_id=1, source_target_pairs={{0,3},{1,2},{2,1},{3,0},{4,7},{5,6},{6,5},{7,4},{8,11},{9,10},{10,... | collective-permute-start | bytes 1179656 | tf_op jit(solution)/shard_map/ppermute | solution.py:236
  68.5 20.9 %collective-permute-start.19 = (bf16[24,512]{1,0:T(8,128)(2,1)S(1)}, bf16[24,512]{1,0:T(8,128)(2,1)S(1)}, u32[]{:S(2)}, u32[]{:S(2)}) collective-permute-start(bf16[24,512]{1,0:T(8,128)(2,1)S(1)} %copy-done.40), channel_id=1, source_target_pairs={{0,3},{1,2},{2,1},{3,0},{4,7},{5,6},{6,5},{7,4},{8,11},{9,10},{10,... | collective-permute-start | bytes 73736 | tf_op jit(solution)/shard_map/ppermute | solution.py:236
  90.0 16.7 %collective-permute-start.14 = (bf16[72,512]{1,0:T(8,128)(2,1)}, bf16[72,512]{1,0:T(8,128)(2,1)S(1)}, u32[]{:S(2)}, u32[]{:S(2)}) collective-permute-start(bf16[72,512]{1,0:T(8,128)(2,1)} %get-tuple-element.24.refs_0_), channel_id=1, source_target_pairs={{0,1},{1,0},{2,3},{3,2},{4,5},{5,4},{6,7},{7,6},{8,9},{9,8},{10,11... | collective-permute-start | bytes 221192 | tf_op jit(solution)/shard_map/ppermute | solution.py:236
  107.3 6.2 %collective-permute-start.15 = (bf16[72,512]{1,0:T(8,128)(2,1)}, bf16[72,512]{1,0:T(8,128)(2,1)}, u32[]{:S(2)}, u32[]{:S(2)}) collective-permute-start(bf16[72,512]{1,0:T(8,128)(2,1)} %get-tuple-element.24.refs_0_), channel_id=1, source_target_pairs={{0,2},{1,3},{2,0},{3,1},{4,6},{5,7},{6,4},{7,5},{8,10},{9,11},{10,... | collective-permute-start | bytes 221192 | tf_op jit(solution)/shard_map/ppermute | solution.py:236
  108.8 6.5 %collective-permute-start.16 = (bf16[72,512]{1,0:T(8,128)(2,1)}, bf16[72,512]{1,0:T(8,128)(2,1)}, u32[]{:S(2)}, u32[]{:S(2)}) collective-permute-start(bf16[72,512]{1,0:T(8,128)(2,1)} %get-tuple-element.24.refs_0_), channel_id=1, source_target_pairs={{0,3},{1,2},{2,1},{3,0},{4,7},{5,6},{6,5},{7,4},{8,11},{9,10},{10,... | collective-permute-start | bytes 221192 | tf_op jit(solution)/shard_map/ppermute | solution.py:236
  123.4 5.1 %collective-permute-start.24 = (bf16[208,256]{1,0:T(8,128)(2,1)S(1)}, bf16[208,256]{1,0:T(8,128)(2,1)S(1)}, u32[]{:S(2)}, u32[]{:S(2)}) collective-permute-start(bf16[208,256]{1,0:T(8,128)(2,1)S(1)} %get-tuple-element.30), channel_id=1, source_target_pairs={{0,1},{1,0},{2,3},{3,2},{4,5},{5,4},{6,7},{7,6},{8,9},{9,8},{10,11... | collective-permute-start | bytes 319496 | tf_op jit(solution)/shard_map/ppermute | solution.py:236
  124.6 7.4 %collective-permute-start.25 = (bf16[208,256]{1,0:T(8,128)(2,1)S(1)}, bf16[208,256]{1,0:T(8,128)(2,1)S(1)}, u32[]{:S(2)}, u32[]{:S(2)}) collective-permute-start(bf16[208,256]{1,0:T(8,128)(2,1)S(1)} %get-tuple-element.31), channel_id=1, source_target_pairs={{0,2},{1,3},{2,0},{3,1},{4,6},{5,7},{6,4},{7,5},{8,10},{9,11},{10,... | collective-permute-start | bytes 319496 | tf_op jit(solution)/shard_map/ppermute | solution.py:236
  126.9 6.6 %collective-permute-start.26 = (bf16[208,256]{1,0:T(8,128)(2,1)S(1)}, bf16[208,256]{1,0:T(8,128)(2,1)S(1)}, u32[]{:S(2)}, u32[]{:S(2)}) collective-permute-start(bf16[208,256]{1,0:T(8,128)(2,1)S(1)} %get-tuple-element.32), channel_id=1, source_target_pairs={{0,3},{1,2},{2,1},{3,0},{4,7},{5,6},{6,5},{7,4},{8,11},{9,10},{10,... | collective-permute-start | bytes 319496 | tf_op jit(solution)/shard_map/ppermute | solution.py:236
  135.8 4.5 %collective-permute-start.30 = (bf16[24,1536]{1,0:T(8,128)(2,1)S(1)}, bf16[24,1536]{1,0:T(8,128)(2,1)S(1)}, u32[]{:S(2)}, u32[]{:S(2)}) collective-permute-start(bf16[24,1536]{1,0:T(8,128)(2,1)S(1)} %get-tuple-element.36), channel_id=1, source_target_pairs={{0,1},{1,0},{2,3},{3,2},{4,5},{5,4},{6,7},{7,6},{8,9},{9,8},{10,11... | collective-permute-start | bytes 221192 | tf_op jit(solution)/shard_map/ppermute | solution.py:236
  137.3 6.0 %collective-permute-start.31 = (bf16[24,1536]{1,0:T(8,128)(2,1)S(1)}, bf16[24,1536]{1,0:T(8,128)(2,1)S(1)}, u32[]{:S(2)}, u32[]{:S(2)}) collective-permute-start(bf16[24,1536]{1,0:T(8,128)(2,1)S(1)} %get-tuple-element.37), channel_id=1, source_target_pairs={{0,2},{1,3},{2,0},{3,1},{4,6},{5,7},{6,4},{7,5},{8,10},{9,11},{10,... | collective-permute-start | bytes 221192 | tf_op jit(solution)/shard_map/ppermute | solution.py:236
  138.3 6.3 %collective-permute-start.32 = (bf16[24,1536]{1,0:T(8,128)(2,1)S(1)}, bf16[24,1536]{1,0:T(8,128)(2,1)S(1)}, u32[]{:S(2)}, u32[]{:S(2)}) collective-permute-start(bf16[24,1536]{1,0:T(8,128)(2,1)S(1)} %get-tuple-element.38), channel_id=1, source_target_pairs={{0,3},{1,2},{2,1},{3,0},{4,7},{5,6},{6,5},{7,4},{8,11},{9,10},{10,... | collective-permute-start | bytes 221192 | tf_op jit(solution)/shard_map/ppermute | solution.py:236
  (52 other events, 309.6 us)

commit v2 on v1

v2 whole, which is shorter than its diff:
```python
import math

import jax
import jax.numpy as jnp
from jax import lax
from jax.experimental import pallas as pl
from jax.experimental.pallas import tpu as pltpu
from jax.sharding import PartitionSpec as P

D = 1536
HEADS = 24
KVH = 8
HD = 64
FFE = 512
TOP = 8
NSTEP = 4
PAGE = 16
ATT = 1536
KVD = 512
GROUP = 3
CAP = 12


EPS = 1e-05
NEG = -1e30


def combined_all(value, axis, join):
    pieces = jax.tree.map(lambda part: lax.all_gather(part, axis), value)
    head = jax.tree.map(lambda part: part[0], pieces)
    tail = jax.tree.map(lambda part: part[1:], pieces)
    so_far, _ = lax.scan(lambda so_far, piece: (join(so_far, piece), None), head, tail)
    return so_far


def normalize(values, gain):
    power = jnp.mean(values * values, axis=-1, keepdims=True)
    return values * lax.rsqrt(power + EPS) * gain


def rotate(values, position):
    half = values.shape[-1] // 2
    rates = jnp.exp(
        jnp.arange(half, dtype=jnp.float32) * (-2.0 * math.log(10000.0) / values.shape[-1])
    )
    angle = position[..., None, None] * rates
    cosine = jnp.cos(angle)
    sine = jnp.sin(angle)
    first_half = values[..., :half]
    second_half = values[..., half:]
    return jnp.concatenate(
        [first_half * cosine - second_half * sine, second_half * cosine + first_half * sine],
        axis=-1,
    )


def softmax_join(left, right):
    left_top, left_total, left_sums = left
    right_top, right_total, right_sums = right
    highest = jnp.maximum(left_top, right_top)
    left_factor = jnp.exp(left_top - highest)
    right_factor = jnp.exp(right_top - highest)
    row_count, head_count = highest.shape
    left_part = left_sums.reshape(row_count, head_count, -1) * left_factor[:, :, None]
    right_part = right_sums.reshape(row_count, head_count, -1) * right_factor[:, :, None]
    joined = (left_part + right_part).reshape(row_count, -1)
    return (highest, left_total * left_factor + right_total * right_factor, joined)


def project_with(left, piece):
    return jnp.dot(left, piece, preferred_element_type=jnp.float32)


def plain(
    x_in,
    attn_gain,
    moe_gain,
    w_qkv,
    w_o,
    cache_k,
    cache_v,
    page_map,
    lengths,
    routes,
    route_weights,
    w_gate_up,
    w_down,
):
    local_requests = x_in.shape[0]
    row_count = local_requests * NSTEP
    inputs = x_in.astype(jnp.float32).reshape(row_count, D)
    normed = normalize(inputs, attn_gain).astype(jnp.bfloat16)
    projected = project_with(normed, lax.all_gather(w_qkv, "seq", axis=1, tiled=True))
    queries = projected[:, :ATT].reshape(local_requests, NSTEP, HEADS, HD)
    keys_new = projected[:, ATT : ATT + KVD].reshape(local_requests, NSTEP, KVH, HD)
    values_new = (
        projected[:, ATT + KVD :].reshape(local_requests, NSTEP, KVH, HD).astype(jnp.bfloat16)
    )
    position = (lengths[:, None] + jnp.arange(NSTEP, dtype=jnp.int32)[None, :]).astype(jnp.float32)
    queries = (
        rotate(queries, position)
        .astype(jnp.bfloat16)
        .reshape(local_requests, NSTEP, KVH, GROUP, HD)
    )
    keys_new = rotate(keys_new, position).astype(jnp.bfloat16)
    scale = HD ** (-0.5)
    slot_count = cache_k.shape[1]
    cached_keys = cache_k.reshape(local_requests, slot_count, KVH, HD)
    cached_values = cache_v.reshape(local_requests, slot_count, KVH, HD)
    slot_position = (
        page_map[:, :, None] * PAGE + jnp.arange(PAGE, dtype=jnp.int32)[None, None, :]
    ).reshape(local_requests, slot_count)
    live = (slot_position < lengths[:, None])[:, None, None, None, :]
    scores = (
        jnp.einsum("rskgd,rtkd->rskgt", queries, cached_keys, preferred_element_type=jnp.float32)
        * scale
    )
    scores = jnp.where(live, scores, NEG)
    local_top = jnp.max(scores, axis=-1)
    exp_scores = jnp.where(live, jnp.exp(scores - local_top[..., None]), 0.0)
    local_total = jnp.sum(exp_scores, axis=-1).reshape(row_count, HEADS)
    local_sums = jnp.einsum(
        "rskgt,rtkd->rskgd",
        exp_scores.astype(jnp.bfloat16),
        cached_values,
        preferred_element_type=jnp.float32,
    ).reshape(row_count, ATT)
    local_top = local_top.reshape(row_count, HEADS)
    cache_top, cache_total, cache_sums = combined_all(
        (local_top, local_total, local_sums), "seq", softmax_join
    )
    causal = (
        jnp.arange(NSTEP, dtype=jnp.int32)[:, None] >= jnp.arange(NSTEP, dtype=jnp.int32)[None, :]
    )[None, :, None, None, :]
    fresh = (
        jnp.einsum("rskgd,rukd->rskgu", queries, keys_new, preferred_element_type=jnp.float32)
        * scale
    )
    fresh = jnp.where(causal, fresh, NEG).reshape(row_count, HEADS, NSTEP)
    highest = jnp.maximum(cache_top, jnp.max(fresh, axis=-1))
    fresh_exp = jnp.exp(fresh - highest[:, :, None])
    carried = jnp.exp(cache_top - highest)
    denominator = cache_total * carried + jnp.sum(fresh_exp, axis=-1)
    fresh_probs = fresh_exp.reshape(local_requests, NSTEP, KVH, GROUP, NSTEP).astype(jnp.bfloat16)
    fresh_sums = jnp.einsum(
        "rskgu,rukd->rskgd", fresh_probs, values_new, preferred_element_type=jnp.float32
    ).reshape(row_count, HEADS, HD)
    numerator = cache_sums.reshape(row_count, HEADS, HD) * carried[:, :, None] + fresh_sums
    attended = (numerator / denominator[:, :, None]).reshape(row_count, ATT).astype(jnp.bfloat16)
    attn_mixed = project_with(attended, lax.all_gather(w_o, "seq", axis=1, tiled=True))
    resid = inputs + attn_mixed
    mixed_in = normalize(resid, moe_gain).astype(jnp.bfloat16)
    local_experts = w_gate_up.shape[0]
    groups = lax.axis_size("req")
    owned = lax.axis_index("seq") * local_experts + jnp.arange(local_experts, dtype=jnp.int32)
    chosen = routes.reshape(row_count, TOP)
    gates = route_weights.reshape(row_count, TOP)
    matches = chosen[None, :, :] == owned[:, None, None]
    routed = jnp.any(matches, axis=-1)
    route_scale = jnp.sum(jnp.where(matches, gates[None, :, :], 0.0), axis=-1)
    ordinal = jnp.cumsum(routed.astype(jnp.int32), axis=1) - 1
    placed = routed[:, :, None] & (
        ordinal[:, :, None] == jnp.arange(CAP, dtype=jnp.int32)[None, None, :]
    )
    outgoing = jnp.einsum(
        "erc,rd->ecd", placed.astype(jnp.bfloat16), mixed_in, preferred_element_type=jnp.float32
    ).astype(jnp.bfloat16)
    arrived = lax.all_to_all(outgoing[:, None], "req", split_axis=3, concat_axis=1, tiled=True)
    slice_width = arrived.shape[3]
    arrived = arrived.reshape(local_experts, groups * CAP, slice_width)
    partial_values = jnp.einsum(
        "end,edf->enf", arrived, w_gate_up, preferred_element_type=jnp.float32
    )
    gate_up = lax.psum(partial_values, "req")
    hidden = (jax.nn.silu(gate_up[..., :FFE]) * gate_up[..., FFE:]).astype(jnp.bfloat16)
    produced = jnp.einsum("enf,efd->end", hidden, w_down, preferred_element_type=jnp.float32)
    returned = lax.all_to_all(
        produced.reshape(local_experts, groups, CAP, slice_width),
        "req",
        split_axis=1,
        concat_axis=3,
        tiled=True,
    )[:, 0]
    weighted = placed.astype(jnp.float32) * route_scale[:, :, None]
    expert_total = jnp.einsum("erc,ecd->rd", weighted, returned, precision=lax.Precision.HIGHEST)
    own_share = lax.psum_scatter(expert_total, "seq", scatter_dimension=1, tiled=True)
    share_width = own_share.shape[1]
    resid_share = lax.dynamic_slice_in_dim(
        resid, lax.axis_index("seq") * share_width, share_width, 1
    )
    return (
        (resid_share + own_share).astype(jnp.bfloat16).reshape(local_requests, NSTEP, share_width)
    )


F32 = jnp.float32
BF16 = jnp.bfloat16
STAT = 128
WIDE = KVD + STAT
VMEM = pl.BlockSpec(memory_space=pltpu.VMEM)
HBM = pl.BlockSpec(memory_space=pltpu.HBM)


def kernel_call(body, out_shape, in_specs, scratch=(), out_specs=None, vmem_mib=8, cost=0.5):
    return pl.pallas_call(
        body,
        out_shape=out_shape,
        in_specs=in_specs,
        out_specs=out_specs or ([VMEM] * len(out_shape) if isinstance(out_shape, list) else VMEM),
        scratch_shapes=list(scratch),
        compiler_params=pltpu.CompilerParams(vmem_limit_bytes=vmem_mib * 2**20),
        cost_estimate=pl.CostEstimate(
            flops=int(cost * 1e9), bytes_accessed=int(cost * 3e6), transcendentals=0
        ),
    )


def iota(shape, dim):
    return lax.broadcasted_iota(jnp.int32, shape, dim)


def split3(value):
    high = value.astype(BF16).astype(F32)
    rest = value - high
    middle = rest.astype(BF16).astype(F32)
    return high, middle, rest - middle


def rows_of(ref):
    return jnp.concatenate([ref[r].astype(F32) for r in range(ref.shape[0])], axis=0)


def dot_nt(left, right):
    return lax.dot_general(left, right, (((1,), (1,)), ((), ())), preferred_element_type=F32)


def swap(value, axis, mask):
    pairs = [(i, i ^ mask) for i in range(lax.axis_size(axis))]
    return lax.ppermute(value, axis, pairs)


def after(value, *others):
    return lax.optimization_barrier((value, *others))[0]


def project_kernel(groups, *refs):
    x_hbm, attn_hbm, moe_hbm, w_hbm, lengths_hbm, pages_hbm, routes_hbm, weights_hbm = refs[:8]
    heads_ref, x_ref, live_ref, routing_ref, gain_ref = refs[8:13]
    x_in, attn_gain, moe_gain, w_in, lengths, pages, routes, weights, sem = refs[13:]
    loads = [
        pltpu.make_async_copy(source, target, sem.at[i])
        for i, (source, target) in enumerate(
            [
                (lengths_hbm, lengths),
                (x_hbm, x_in),
                (attn_hbm, attn_gain),
                (w_hbm, w_in),
                (pages_hbm, pages),
                (routes_hbm, routes),
                (weights_hbm, weights),
                (moe_hbm, moe_gain),
            ]
        )
    ]
    for load in loads:
        load.start()
    requests = x_in.shape[0]
    row_count = requests * NSTEP
    shape = (row_count, STAT)
    loads[0].wait()
    row, lane = iota(shape, 0), iota(shape, 1)
    position = row % NSTEP
    for r in range(requests):
        position = position + jnp.where(row // NSTEP == r, lengths[r], 0)
    rates = jnp.exp((lane % (HD // 2)).astype(F32) * (-2.0 * math.log(10000.0) / HD))
    angle = position.astype(F32) * rates
    cosine = jnp.cos(angle)
    sine = jnp.where(lane % HD < HD // 2, -jnp.sin(angle), jnp.sin(angle))
    loads[1].wait()
    x = rows_of(x_in)
    x_ref[...] = x
    power = jnp.mean(x * x, axis=-1, keepdims=True)
    loads[2].wait()
    normed = (x * lax.rsqrt(power + EPS) * attn_gain[...].reshape(1, D)).astype(BF16)
    loads[3].wait()
    projected = dot_nt(normed, w_in[...])
    heads = w_in.shape[0] // HD
    first = lax.axis_index("seq") * heads
    for i in range(heads):
        one = projected[:, i * HD : (i + 1) * HD]
        both = jnp.concatenate([one, one], axis=1)
        turned = both * cosine + pltpu.roll(both, HD // 2, 1) * sine
        heads_ref[i] = jnp.where(first + i < HEADS + KVH, turned, both).astype(BF16)
    for load in loads[4:]:
        load.wait()
    slots = live_ref.shape[1]
    slot = iota((1, slots), 1)
    for r in range(requests):
        page = jnp.zeros((1, slots), jnp.int32)
        for j in range(slots // PAGE):
            page = jnp.where(slot // PAGE == j, pages[r, j], page)
        live = page * PAGE + slot % PAGE < lengths[r]
        live_ref[r : r + 1, :] = jnp.where(live, 1.0, 0.0)
    high, middle, low = split3(rows_of(weights))
    routing_ref[...] = jnp.concatenate(
        [rows_of(routes), high, middle, low, jnp.zeros((row_count, STAT - 4 * TOP), F32)], axis=1
    )
    gain_ref[...] = moe_gain[...].reshape(1, D)


def cut_kernel(groups, down_ref, *refs):
    cut_refs, sem = refs[:-1], refs[-1]
    depth = cut_refs[0].shape[1]
    copies = []
    for k in range(1, groups):
        start = pl.multiple_of((lax.axis_index("req") ^ k) * depth, depth)
        source = down_ref.at[:, pl.ds(start, depth), :]
        copies.append(pltpu.make_async_copy(source, cut_refs[k - 1], sem.at[k - 1]))
        copies[-1].start()
    for copy in copies:
        copy.wait()


def gather_pieces(near_refs, far_refs, all_ref):
    core = lax.axis_index("seq") % 2
    for k in range(len(near_refs)):
        all_ref[core, k] = near_refs[k][...]
        all_ref[1 - core, k] = far_refs[k][...]


def paired(head, left, right):
    a = head(left)
    return jnp.where(iota(a.shape, 1) < HD, a, head(right))


def expanded(q_ref, r):
    rows = [q_ref[g, r * NSTEP : (r + 1) * NSTEP, :] for g in range(GROUP)]
    base = jnp.concatenate(rows + [jnp.zeros((NSTEP, KVD), F32)], axis=0)
    owner = iota(base.shape, 1) // HD
    return jnp.concatenate(
        [jnp.where(owner == k, base, 0.0) for k in range(KVH)], axis=0
    ).astype(BF16)


def attend_part(query, keys, values, live):
    scores = jnp.where(live, dot_nt(query, keys) * (HD ** (-0.5)), NEG)
    top = jnp.max(scores, axis=1, keepdims=True)
    exp_scores = jnp.where(live, jnp.exp(scores - top), 0.0)
    total = jnp.sum(exp_scores, axis=1, keepdims=True)
    return top, total, jnp.dot(exp_scores.astype(BF16), values, preferred_element_type=F32)


def place_rows(part_ref, r, row_count, top, total, sums):
    block = (GROUP + 1) * NSTEP
    owner = iota((block, KVD), 1) // HD
    lane = iota((block, STAT), 1)
    own_sums = jnp.zeros((block, KVD), F32)
    stats = jnp.zeros((block, STAT), F32)
    for k in range(KVH):
        rows = slice(k * block, (k + 1) * block)
        own_sums = jnp.where(owner == k, sums[rows], own_sums)
        value = jnp.where(lane < 3 * KVH, top[rows], total[rows])
        stats = jnp.where(lane % KVH == k, value, stats)
    high, middle, low = split3(stats)
    part = (lane // KVH) % 3
    stats = jnp.where(part == 0, high, jnp.where(part == 1, middle, low))
    for g in range(GROUP):
        rows = slice(g * row_count + r * NSTEP, g * row_count + (r + 1) * NSTEP)
        part_ref[rows, :KVD] = own_sums[g * NSTEP : (g + 1) * NSTEP]
        part_ref[rows, KVD:] = stats[g * NSTEP : (g + 1) * NSTEP]


def head_of(all_ref):
    chip = lax.axis_index("seq") // 2
    heads = all_ref.shape[2]

    def head(h):
        owner = h // heads
        return all_ref[owner % 2, chip ^ (owner // 2), h % heads].astype(F32)

    return head


def query_rows(head, q_ref):
    for g in range(GROUP):
        for m in range(KVH // 2):
            q_ref[g, :, m * STAT : (m + 1) * STAT] = paired(
                head, GROUP * 2 * m + g, GROUP * (2 * m + 1) + g
            )


def attend_kernel(chips, *refs):
    near_refs, far_refs = refs[:chips], refs[chips : 2 * chips]
    live_ref, k_ref, v_ref, out_ref, all_ref, q_ref, part_ref = refs[2 * chips :]
    requests = k_ref.shape[0]
    gather_pieces(near_refs, far_refs, all_ref)
    query_rows(head_of(all_ref), q_ref)
    for r in range(requests):
        live = live_ref[r : r + 1, :] > 0.5
        place_rows(
            part_ref,
            r,
            requests * NSTEP,
            *attend_part(expanded(q_ref, r), k_ref[r], v_ref[r], live),
        )
    out_ref[...] = part_ref[...].astype(BF16)


def fresh_kernel(chips, *refs):
    near_refs, far_refs = refs[:chips], refs[chips : 2 * chips]
    out_ref, all_ref, q_ref, part_ref = refs[2 * chips :]
    gather_pieces(near_refs, far_refs, all_ref)
    head = head_of(all_ref)
    query_rows(head, q_ref)
    row_count = q_ref.shape[1]
    pad = jnp.zeros((STAT - row_count, KVD), F32)

    def new_rows(first):
        pieces = [paired(head, first + 2 * m, first + 2 * m + 1) for m in range(KVH // 2)]
        return jnp.concatenate([jnp.concatenate(pieces, axis=1), pad], axis=0).astype(BF16)

    keys, values = new_rows(HEADS), new_rows(HEADS + KVH)
    shape = ((GROUP + 1) * NSTEP * KVH, STAT)
    slot, step = iota(shape, 1), iota(shape, 0) % NSTEP
    for r in range(row_count // NSTEP):
        live = (slot // NSTEP == r) & (slot % NSTEP <= step)
        place_rows(
            part_ref, r, row_count, *attend_part(expanded(q_ref, r), keys, values, live)
        )
    out_ref[...] = part_ref[...].astype(BF16)


def merge_kernel(count, *refs):
    part_refs = refs[:count]
    x_ref, w_ref, share_ref, resid_ref = refs[count:]
    parts = [ref[...].astype(F32) for ref in part_refs]
    tops, totals = [], []
    for part in parts:
        stats = part[:, KVD:]
        full = stats + (
            pltpu.roll(stats, STAT - KVH, 1) + pltpu.roll(stats, STAT - 2 * KVH, 1)
        )
        tops.append(full)
        totals.append(pltpu.roll(full, STAT - 3 * KVH, 1))
    highest = tops[0]
    for top in tops[1:]:
        highest = jnp.maximum(highest, top)
    factors = [jnp.exp(top - highest) for top in tops]
    denominator = factors[0] * totals[0]
    for factor, total in zip(factors[1:], totals[1:]):
        denominator = denominator + factor * total
    inverse = 1.0 / denominator
    row_total = parts[0].shape[0]
    row_count = row_total // GROUP
    left = iota((row_total, STAT), 1) < HD
    columns = []
    for m in range(KVH // 2):
        value = jnp.zeros((row_total, STAT), F32)
        for part, factor in zip(parts, factors):
            spread = jnp.where(left, factor[:, 2 * m : 2 * m + 1], factor[:, 2 * m + 1 : 2 * m + 2])
            value = value + spread * part[:, m * STAT : (m + 1) * STAT]
        spread = jnp.where(left, inverse[:, 2 * m : 2 * m + 1], inverse[:, 2 * m + 1 : 2 * m + 2])
        columns.append(value * spread)

    def head(h, side):
        k, g = h // GROUP, h % GROUP
        rows = columns[k // 2][g * row_count : (g + 1) * row_count]
        return rows if k % 2 == side else pltpu.roll(rows, HD, 1)

    left = iota((row_count, STAT), 1) < HD
    attended = jnp.concatenate(
        [jnp.where(left, head(2 * n, 0), head(2 * n + 1, 1)) for n in range(HEADS // 2)], axis=1
    ).astype(BF16)
    share = dot_nt(attended, w_ref[...])
    share_ref[...] = share
    width = w_ref.shape[0]
    member = lax.axis_index("seq")
    chunk = x_ref[:, pl.ds(pl.multiple_of((member // 2) * (2 * width), STAT), 2 * width)]
    resid_ref[...] = share + jnp.where(member % 2 == 0, chunk[:, :width], chunk[:, width:])


def mix_kernel(chips, groups, *refs):
    near_refs, far_refs = refs[:chips], refs[chips : 2 * chips]
    x_ref, gain_ref, routing_ref = refs[2 * chips : 2 * chips + 3]
    pack_refs, all_ref, mixed_ref = refs[2 * chips + 3 : -2], refs[-2], refs[-1]
    gather_pieces(near_refs, far_refs, all_ref)
    chip = lax.axis_index("seq") // 2
    attn = jnp.concatenate([all_ref[s % 2, chip ^ (s // 2)] for s in range(2 * chips)], axis=1)
    resid = x_ref[...] + attn
    power = jnp.mean(resid * resid, axis=-1, keepdims=True)
    mixed_ref[...] = resid * lax.rsqrt(power + EPS) * gain_ref[...]
    routing = routing_ref[...]
    width = D // groups
    for k in range(groups):
        start = pl.multiple_of((lax.axis_index("req") ^ k) * width, STAT)
        part = mixed_ref[:, pl.ds(start, width)]
        pack_refs[k][...] = jnp.concatenate([part, routing], axis=1).astype(BF16)


def across(column, eye):
    return jnp.sum(jnp.where(eye, column, 0.0), axis=0, keepdims=True)


def gate_kernel(groups, *refs):
    pack_refs = refs[:groups]
    w_ref = refs[groups]
    message_refs = refs[groups + 1 : 2 * groups + 1]
    placed_ref, scale_ref, full_ref = refs[2 * groups + 1 :]
    first = lax.axis_index("seq") * w_ref.shape[0]
    me = lax.axis_index("req")
    packs = [ref[...].astype(F32) for ref in pack_refs]
    row_count = packs[0].shape[0]
    tokens = groups * row_count
    width = w_ref.shape[1]
    mixed = jnp.concatenate([pack[:, :width] for pack in packs], axis=0).astype(BF16)
    routing = jnp.concatenate([pack[:, width:] for pack in packs], axis=0)
    chosen = routing[:, :TOP]
    gates = routing[:, TOP : 2 * TOP] + (
        routing[:, 2 * TOP : 3 * TOP] + routing[:, 3 * TOP : 4 * TOP]
    )
    experts = w_ref.shape[0]
    square = (tokens, tokens)
    eye = iota(square, 0) == iota(square, 1)
    earlier = (iota(square, 0) < iota(square, 1)) & (
        iota(square, 0) // row_count == iota(square, 1) // row_count
    )
    slots = groups * CAP
    shape = (slots, tokens)
    home = (iota(shape, 1) // row_count) ^ me
    slot = iota(shape, 0)
    same_group = slot // CAP == home
    ordinal_of_slot = (slot % CAP).astype(F32)
    placed, scales = [], []
    for e in range(experts):
        match = chosen == (first + e).astype(F32)
        routed = jnp.max(jnp.where(match, 1.0, 0.0), axis=1, keepdims=True)
        scale = jnp.sum(jnp.where(match, gates, 0.0), axis=1, keepdims=True)
        ordinal = across(routed, earlier)
        here = same_group & (across(routed, eye) > 0.5) & (ordinal_of_slot == ordinal)
        placed.append(jnp.where(here, 1.0, 0.0))
        scales.append(jnp.sum(jnp.where(here, across(scale, eye), 0.0), axis=1, keepdims=True))
    placed = jnp.concatenate(placed, axis=0).astype(BF16)
    placed_ref[...] = placed
    scale_ref[...] = jnp.broadcast_to(jnp.concatenate(scales, axis=0), scale_ref.shape)
    taken = jnp.dot(placed, mixed, preferred_element_type=F32).astype(BF16)
    for e in range(experts):
        full_ref[e * slots : (e + 1) * slots, :] = jnp.dot(
            taken[e * slots : (e + 1) * slots], w_ref[e], preferred_element_type=F32
        )
    piece = FFE // groups
    for k in range(groups):
        begin = pl.multiple_of((me ^ k) * piece, STAT)
        message_refs[k][:, :piece] = full_ref[:, pl.ds(begin, piece)].astype(BF16)
        message_refs[k][:, piece:] = full_ref[:, pl.ds(begin + FFE, piece)].astype(BF16)


def down_kernel(groups, *refs):
    message_refs = refs[:groups]
    own_ref = refs[groups]
    down_refs = refs[groups + 1 : 2 * groups]
    placed_ref, scale_ref = refs[2 * groups : 2 * groups + 2]
    out_refs = refs[2 * groups + 2 :]
    me = lax.axis_index("req")
    piece = message_refs[0].shape[1] // 2
    gate_up = message_refs[0][...].astype(F32)
    for ref in message_refs[1:]:
        gate_up = gate_up + ref[...].astype(F32)
    gate, up = gate_up[:, :piece], gate_up[:, piece:]
    hidden = (gate / (1.0 + jnp.exp(-gate)) * up).astype(BF16)
    experts = own_ref.shape[0]
    slots = placed_ref.shape[0] // experts
    placed = placed_ref[...]
    scale = scale_ref[...][:, :1]
    begin = pl.multiple_of(me * piece, STAT)
    width = own_ref.shape[2]
    row_count = out_refs[0].shape[0]
    for k in range(groups):
        produced = []
        for e in range(experts):
            weight = own_ref[e, pl.ds(begin, piece), :] if k == 0 else down_refs[k - 1][e]
            produced.append(
                jnp.dot(
                    hidden[e * slots : (e + 1) * slots], weight, preferred_element_type=F32
                )
            )
        produced = (jnp.concatenate(produced, axis=0) * scale).astype(BF16)
        total = lax.dot_general(
            placed, produced, (((0,), (0,)), ((), ())), preferred_element_type=F32
        )
        column = pl.multiple_of((me ^ k) * width, STAT)
        for j in range(groups):
            out_refs[j][:, pl.ds(column, width)] = total[
                j * row_count : (j + 1) * row_count
            ].astype(BF16)


def spread_kernel(groups, *refs):
    total = refs[0][...].astype(F32)
    for ref in refs[1:groups]:
        total = total + ref[...].astype(F32)
    out_ref = refs[groups]
    width = out_ref.shape[2]
    for s in range(out_ref.shape[0]):
        out_ref[s] = total[:, s * width : (s + 1) * width].astype(BF16)


def final_kernel(resid_ref, arrived_ref, out_ref):
    total = resid_ref[...]
    for s in range(arrived_ref.shape[0]):
        total = total + arrived_ref[s].astype(F32)
    for r in range(out_ref.shape[0]):
        out_ref[r] = total[r * NSTEP : (r + 1) * NSTEP].astype(BF16)


def staged(
    x_in,
    attn_gain,
    moe_gain,
    w_qkv,
    w_o,
    cache_k,
    cache_v,
    page_map,
    lengths,
    routes,
    route_weights,
    w_gate_up,
    w_down,
):
    requests = x_in.shape[0]
    row_count = requests * NSTEP
    members, groups = lax.axis_size("seq"), lax.axis_size("req")
    chips = members // 2
    heads = w_qkv.shape[1] // HD
    width = w_o.shape[1]
    depth = w_down.shape[1] // groups
    slots = cache_k.shape[1]

    own_heads, x, live, routing, gain = kernel_call(
        lambda *refs: project_kernel(groups, *refs),
        [
            jax.ShapeDtypeStruct((heads, row_count, 2 * HD), BF16),
            jax.ShapeDtypeStruct((row_count, D), F32),
            jax.ShapeDtypeStruct((requests, slots), F32),
            jax.ShapeDtypeStruct((row_count, STAT), F32),
            jax.ShapeDtypeStruct((1, D), F32),
        ],
        [HBM] * 8,
        [
            pltpu.VMEM(x_in.shape, BF16),
            pltpu.VMEM((D,), F32),
            pltpu.VMEM((D,), F32),
            pltpu.VMEM((w_qkv.shape[1], D), BF16),
            pltpu.SMEM(lengths.shape, jnp.int32),
            pltpu.SMEM(page_map.shape, jnp.int32),
            pltpu.VMEM(routes.shape, jnp.int32),
            pltpu.VMEM(route_weights.shape, F32),
            pltpu.SemaphoreType.DMA((8,)),
        ],
        vmem_mib=60,
    )(x_in, attn_gain, moe_gain, w_qkv.T, lengths, page_map, routes, route_weights)
    cuts = kernel_call(
        lambda *refs: cut_kernel(groups, *refs),
        [jax.ShapeDtypeStruct((w_down.shape[0], depth, w_down.shape[2]), BF16)] * (groups - 1),
        [HBM],
        [pltpu.SemaphoreType.DMA((groups - 1,))],
        [HBM] * (groups - 1),
    )(w_down)
    downs = [swap(cuts[k - 1], "req", k) for k in range(1, groups)]

    def gathered(own):
        near = [own] + [swap(own, "seq", 2 * k) for k in range(1, chips)]
        return near, [swap(piece, "seq", 1) for piece in near]

    near, far = gathered(own_heads)
    part_shape = jax.ShapeDtypeStruct((GROUP * row_count, WIDE), BF16)
    head_scratch = [
        pltpu.VMEM((2, chips, heads, row_count, 2 * HD), BF16),
        pltpu.VMEM((GROUP, row_count, KVD), F32),
        pltpu.VMEM((GROUP * row_count, WIDE), F32),
    ]
    part = kernel_call(
        lambda *refs: attend_kernel(chips, *refs),
        part_shape,
        [VMEM] * (2 * chips + 3),
        head_scratch,
    )(*near, *far, live, cache_k, cache_v)
    fresh = kernel_call(
        lambda *refs: fresh_kernel(chips, *refs),
        part_shape,
        [VMEM] * (2 * chips),
        head_scratch,
        cost=0.5,
    )(*near, *far)
    near, far = gathered(part)
    x = after(x, downs[2])
    share, resid = kernel_call(
        lambda *refs: merge_kernel(members + 1, *refs),
        [jax.ShapeDtypeStruct((row_count, width), F32)] * 2,
        [VMEM] * (members + 3),
    )(*near, *far, fresh, x, w_o.T)
    near, far = gathered(share)
    routing = after(routing, downs[1])
    packs = kernel_call(
        lambda *refs: mix_kernel(chips, groups, *refs),
        [jax.ShapeDtypeStruct((row_count, 2 * width + STAT), BF16)] * groups,
        [VMEM] * (2 * chips + 3),
        [pltpu.VMEM((2, chips, row_count, width), F32), pltpu.VMEM((row_count, D), F32)],
    )(*near, *far, x, gain, routing)

    def exchanged(pieces):
        return [pieces[0]] + [swap(pieces[k], "req", k) for k in range(1, groups)]

    experts = w_gate_up.shape[0]
    total_slots = experts * groups * CAP
    *messages, placed, scale = kernel_call(
        lambda *refs: gate_kernel(groups, *refs),
        [jax.ShapeDtypeStruct((total_slots, 2 * FFE // groups), BF16)] * groups
        + [
            jax.ShapeDtypeStruct((total_slots, groups * row_count), BF16),
            jax.ShapeDtypeStruct((total_slots, STAT), F32),
        ],
        [VMEM] * (groups + 1),
        [pltpu.VMEM((total_slots, 2 * FFE), F32)],
    )(*exchanged(packs), after(w_gate_up, downs[0]))
    outs = kernel_call(
        lambda *refs: down_kernel(groups, *refs),
        [jax.ShapeDtypeStruct((row_count, D), BF16)] * groups,
        [VMEM] * (2 * groups + 2),
    )(*exchanged(messages), w_down, *downs, placed, scale)
    spread = kernel_call(
        lambda *refs: spread_kernel(groups, *refs),
        jax.ShapeDtypeStruct((members, row_count, width), BF16),
        [VMEM] * groups,
    )(*exchanged(outs))
    arrived = lax.all_to_all(spread, "seq", 0, 0, tiled=True)
    return kernel_call(
        final_kernel, jax.ShapeDtypeStruct((requests, NSTEP, width), BF16), [VMEM] * 2
    )(resid, arrived)


def local(*args):
    w_qkv, w_o = args[3], args[4]
    members, groups = lax.axis_size("seq"), lax.axis_size("req")
    fits = (
        members == 2 * groups
        and groups & (groups - 1) == 0
        and w_qkv.shape[1] % HD == 0
        and (FFE // groups) % STAT == 0
        and (2 * w_o.shape[1]) % STAT == 0
    )
    return staged(*args) if fits else plain(*args)


def solution(mesh):
    in_specs = (
        P("req", None, None),
        P(),
        P(),
        P(None, "seq"),
        P(None, "seq"),
        P("req", "seq", None),
        P("req", "seq", None),
        P("req", "seq"),
        P("req"),
        P("req", None, None),
        P("req", None, None),
        P("seq", "req", None),
        P("seq", None, "req"),
    )
    out_specs = P("req", None, "seq")
    return jax.shard_map(local, mesh=mesh, in_specs=in_specs, out_specs=out_specs, check_vma=False)
```

time: 155 us -> 81.1 us (0.52); the launches traced: 153 us -> 80.8 us
  local copies, waits for them, and re-layouts: 29.9 us -> 2.88 us
  starting transfers between devices: 55.3 us -> 31 us
  waiting for transfers between devices: 45.8 us -> 28.9 us
  Pallas kernels: 12.5 us -> 9.69 us
  other arithmetic: 1.6 us -> 0 us
    ppermute x33, starting transfers between devices: 55.3 us -> 31 us  [swap(): return lax.ppermute(value, axis, pairs)]
    unnamed x88 -> x22, local copies, waits for them, and re-layouts: 21.7 us -> 2.88 us
    ppermute x33, waiting for transfers between devices: 45.8 us -> 28.9 us  [swap(): return lax.ppermute(value, axis, pairs)]
    ppermute x4 -> x0, local copies, waits for them, and re-layouts: 5.16 us -> none  [the longest x3 3.82 us: staged(): lax.ppermute(w_o, place, [((2 * z + c) * groups + z, (2 * (z ^ k) + c) *...]
    pallas_call x4 -> x6, Pallas kernels: 7.07 us -> 6.88 us  [the longest x1 2.58 us: staged(): kernel_call(lambda *refs: project_kernel(groups, *refs), [jax.ShapeDtypeS...]
  transfers between devices with their start and end apart: 33 -> 33, of which waited for: 17 -> 19; matrix products, arithmetic and copies ran while one was open for 5% -> 0% of each run, Pallas kernels for 6% -> 8%
where the time goes in v2:
time: 81.1 us; the launch traced here: 80.8 us
  starting transfers between devices  31 us (38%)
  waiting for transfers between devices  28.9 us (36%)
  Pallas kernels  9.69 us (12%)
  blocking collectives  8.12 us (10%)
  local copies, waits for them, and re-layouts  2.88 us (4%)
    ppermute x33, starting transfers between devices, swap(): return lax.ppermute(value, axis, pairs)  31 us
    ppermute x33, waiting for transfers between devices, swap(): return lax.ppermute(value, axis, pairs)  28.9 us
    all_to_all x1, blocking collectives, staged(): arrived = lax.all_to_all(spread, 'seq', 0, 0, tiled=True)  8.12 us
    unnamed x22, local copies, waits for them, and re-layouts  2.88 us
    pallas_call x1, Pallas kernels, staged(): kernel_call(lambda *refs: project_kernel(groups, *refs), [jax.ShapeDtypeS...  2.58 us
    pallas_call x1, Pallas kernels, staged(): kernel_call(lambda *refs: merge_kernel(members + 1, *refs), [jax.ShapeDty...  1.74 us
  transfers between devices with their start and end apart: 33, of which 19 were waited for; matrix products, arithmetic and copies ran while one was open for 0% of the time, Pallas kernels for 8%

profile of v2, /device:TPU:0, one launch (start us, length us, event | category | flops | bytes accessed | tf_op | source)
XLA Modules:
  0.0 80.8 jit_solution(15376218356001125819)
XLA Ops:
  0.0 1.4 %copy-done.1 = bf16[4,512,384]{2,1,0:T(8,128)(2,1)S(1)} copy-done((bf16[4,512,384]{2,1,0:T(8,128)(2,1)S(1)}, bf16[4,512,384]{2,1,0:T(8,128)(2,1)}, u32[]{:S(2)}) %copy-start.1) | copy-done | bytes 1572888
  1.6 5.1 %collective-permute-start.14 = (bf16[4,128,384]{2,1,0:T(8,128)(2,1)S(1)}, bf16[4,128,384]{2,1,0:T(8,128)(2,1)S(1)}, u32[]{:S(2)}, u32[]{:S(2)}) collective-permute-start(bf16[4,128,384]{2,1,0:T(8,128)(2,1)S(1)} %get-tuple-element.35), channel_id=1, source_target_pairs={{0,3},{1,2},{2,1},{3,0},{4,7},{5,6},{6,5},{7,4},{8,11},{9,10},{10,... | collective-permute-start | bytes 1179656 | tf_op jit(solution)/shard_map/ppermute | solution.py:239
  6.8 2.6 %shard_map.127 = (bf16[5,24,128]{2,1,0:T(8,128)(2,1)}, f32[24,1536]{1,0:T(8,128)}, f32[6,128]{1,0:T(8,128)}, f32[24,128]{1,0:T(8,128)}, f32[1,1536]{1,0:T(1,128)}) custom-call(bf16[6,4,1536]{2,1,0:T(4,128)(2,1)} %refs_0_.2, f32[1536]{0:T(1024)} %refs_1_.1, f32[1536]{0:T(1024)} %refs_2_.1, bf16[320,1536]{1,0:T(8,128)(2,1)} %bitcast.3, s32[6]{0:T(128)} %refs_4_.2, ...), custom_call_target="tpu_custom_call" | custom-call | flops 500000000 | bytes 1500000 | tf_op jit(solution)/shard_map/pallas_call | solution.py:639
  9.3 2.5 %collective-permute-start.2 = (bf16[5,24,128]{2,1,0:T(8,128)(2,1)}, bf16[5,24,128]{2,1,0:T(8,128)(2,1)S(1)}, u32[]{:S(2)}, u32[]{:S(2)}) collective-permute-start(bf16[5,24,128]{2,1,0:T(8,128)(2,1)} %get-tuple-element.32.refs_0_), channel_id=1, source_target_pairs={{0,24},{4,28},{8,16},{12,20},{16,8},{20,12},{24,0},{28,4},{1,25},{... | collective-permute-start | bytes 92168 | tf_op jit(solution)/shard_map/ppermute | solution.py:239
  12.9 1.6 %collective-permute-done.2.refs_3_ = bf16[5,24,128]{2,1,0:T(8,128)(2,1)S(1)} collective-permute-done((bf16[5,24,128]{2,1,0:T(8,128)(2,1)}, bf16[5,24,128]{2,1,0:T(8,128)(2,1)S(1)}, u32[]{:S(2)}, u32[]{:S(2)}) %collective-permute-start.2) | collective-permute-done | bytes 30752 | tf_op jit(solution)/shard_map/ppermute | solution.py:239
  14.5 1.4 %collective-permute-done.1.refs_2_ = bf16[5,24,128]{2,1,0:T(8,128)(2,1)S(1)} collective-permute-done((bf16[5,24,128]{2,1,0:T(8,128)(2,1)}, bf16[5,24,128]{2,1,0:T(8,128)(2,1)S(1)}, u32[]{:S(2)}, u32[]{:S(2)}) %collective-permute-start.1) | collective-permute-done | bytes 30752 | tf_op jit(solution)/shard_map/ppermute | solution.py:239
  20.4 1.5 %collective-permute-start.9 = (bf16[72,640]{1,0:T(8,128)(2,1)S(1)}, bf16[72,640]{1,0:T(8,128)(2,1)S(1)}, u32[]{:S(2)}, u32[]{:S(2)}) collective-permute-start(bf16[72,640]{1,0:T(8,128)(2,1)S(1)} %shard_map.128.refs_0_), channel_id=1, source_target_pairs={{0,24},{4,28},{8,16},{12,20},{16,8},{20,12},{24,0},{28,4},{1,25},{... | collective-permute-start | bytes 276488 | tf_op jit(solution)/shard_map/ppermute | solution.py:239
  23.1 3.3 %collective-permute-done.9.refs_3_ = bf16[72,640]{1,0:T(8,128)(2,1)S(1)} collective-permute-done((bf16[72,640]{1,0:T(8,128)(2,1)S(1)}, bf16[72,640]{1,0:T(8,128)(2,1)S(1)}, u32[]{:S(2)}, u32[]{:S(2)}) %collective-permute-start.9) | collective-permute-done | bytes 92192 | tf_op jit(solution)/shard_map/ppermute | solution.py:239
  28.2 2.7 %collective-permute-done.7.refs_1_ = bf16[72,640]{1,0:T(8,128)(2,1)S(1)} collective-permute-done((bf16[72,640]{1,0:T(8,128)(2,1)S(1)}, bf16[72,640]{1,0:T(8,128)(2,1)S(1)}, u32[]{:S(2)}, u32[]{:S(2)}) %collective-permute-start.7) | collective-permute-done | bytes 92192 | tf_op jit(solution)/shard_map/ppermute | solution.py:239
  32.6 1.7 %shard_map.131 = (f32[24,192]{1,0:T(8,128)S(1)}, f32[24,192]{1,0:T(8,128)S(1)}) custom-call(bf16[72,640]{1,0:T(8,128)(2,1)S(1)} %shard_map.128.refs_0_, bf16[72,640]{1,0:T(8,128)(2,1)S(1)} %collective-permute-done.7.refs_1_, bf16[72,640]{1,0:T(8,128)(2,1)S(1)} %collective-permute-done.8.refs_2_, bf16[72,640]{1,0:T(8,128)(2,1)S(1)} %collective-permute-done.9.refs_3_, ...), custom_call_target="tpu_custom_call" | custom-call | flops 500000000 | bytes 1500000 | tf_op jit(solution)/shard_map/pallas_call | solution.py:697
  34.3 1.6 %collective-permute-start.17 = (f32[24,192]{1,0:T(8,128)S(1)}, f32[24,192]{1,0:T(8,128)S(1)}, u32[]{:S(2)}, u32[]{:S(2)}) collective-permute-start(f32[24,192]{1,0:T(8,128)S(1)} %get-tuple-element.38.refs_0_), channel_id=1, source_target_pairs={{0,24},{4,28},{8,16},{12,20},{16,8},{20,12},{24,0},{28,4},{1,25},{... | collective-permute-start | bytes 55304 | tf_op jit(solution)/shard_map/ppermute | solution.py:239
  36.3 1.5 %collective-permute-start.15 = (f32[24,192]{1,0:T(8,128)S(1)}, f32[24,192]{1,0:T(8,128)S(1)}, u32[]{:S(2)}, u32[]{:S(2)}) collective-permute-start(f32[24,192]{1,0:T(8,128)S(1)} %get-tuple-element.38.refs_0_), channel_id=1, source_target_pairs={{0,8},{4,12},{8,0},{12,4},{16,24},{20,28},{24,16},{28,20},{1,9},{5... | collective-permute-start | bytes 55304 | tf_op jit(solution)/shard_map/ppermute | solution.py:239
  37.9 2.5 %collective-permute-done.22.refs_6_ = bf16[4,128,384]{2,1,0:T(8,128)(2,1)S(1)} collective-permute-done((bf16[4,128,384]{2,1,0:T(8,128)(2,1)S(1)}, bf16[4,128,384]{2,1,0:T(8,128)(2,1)S(1)}, u32[]{:S(2)}, u32[]{:S(2)}) %collective-permute-start.22) | collective-permute-done | bytes 393248 | tf_op jit(solution)/shard_map/ppermute | solution.py:239
  42.5 2.3 %collective-permute-start.23 = (bf16[24,512]{1,0:T(8,128)(2,1)S(1)}, bf16[24,512]{1,0:T(8,128)(2,1)S(1)}, u32[]{:S(2)}, u32[]{:S(2)}) collective-permute-start(bf16[24,512]{1,0:T(8,128)(2,1)S(1)} %get-tuple-element.44), channel_id=1, source_target_pairs={{0,1},{1,0},{2,3},{3,2},{4,5},{5,4},{6,7},{7,6},{8,9},{9,8},{10,11... | collective-permute-start | bytes 73736 | tf_op jit(solution)/shard_map/ppermute | solution.py:239
  47.5 2.4 %collective-permute-done.24.refs_2_ = bf16[24,512]{1,0:T(8,128)(2,1)S(1)} collective-permute-done((bf16[24,512]{1,0:T(8,128)(2,1)S(1)}, bf16[24,512]{1,0:T(8,128)(2,1)S(1)}, u32[]{:S(2)}, u32[]{:S(2)}) %collective-permute-start.24) | collective-permute-done | bytes 24608 | tf_op jit(solution)/shard_map/ppermute | solution.py:239
  49.9 1.8 %collective-permute-done.25.refs_3_ = bf16[24,512]{1,0:T(8,128)(2,1)S(1)} collective-permute-done((bf16[24,512]{1,0:T(8,128)(2,1)S(1)}, bf16[24,512]{1,0:T(8,128)(2,1)S(1)}, u32[]{:S(2)}, u32[]{:S(2)}) %collective-permute-start.25) | collective-permute-done | bytes 24608 | tf_op jit(solution)/shard_map/ppermute | solution.py:239
  53.0 1.8 %collective-permute-start.28 = (bf16[192,256]{1,0:T(8,128)(2,1)S(1)}, bf16[192,256]{1,0:T(8,128)(2,1)S(1)}, u32[]{:S(2)}, u32[]{:S(2)}) collective-permute-start(bf16[192,256]{1,0:T(8,128)(2,1)S(1)} %get-tuple-element.51), channel_id=1, source_target_pairs={{0,2},{1,3},{2,0},{3,1},{4,6},{5,7},{6,4},{7,5},{8,10},{9,11},{10,... | collective-permute-start | bytes 294920 | tf_op jit(solution)/shard_map/ppermute | solution.py:239
  54.8 2.4 %collective-permute-start.29 = (bf16[192,256]{1,0:T(8,128)(2,1)S(1)}, bf16[192,256]{1,0:T(8,128)(2,1)S(1)}, u32[]{:S(2)}, u32[]{:S(2)}) collective-permute-start(bf16[192,256]{1,0:T(8,128)(2,1)S(1)} %get-tuple-element.52), channel_id=1, source_target_pairs={{0,3},{1,2},{2,1},{3,0},{4,7},{5,6},{6,5},{7,4},{8,11},{9,10},{10,... | collective-permute-start | bytes 294920 | tf_op jit(solution)/shard_map/ppermute | solution.py:239
  57.4 5.1 %collective-permute-done.28.refs_2_ = bf16[192,256]{1,0:T(8,128)(2,1)S(1)} collective-permute-done((bf16[192,256]{1,0:T(8,128)(2,1)S(1)}, bf16[192,256]{1,0:T(8,128)(2,1)S(1)}, u32[]{:S(2)}, u32[]{:S(2)}) %collective-permute-start.28) | collective-permute-done | bytes 98336 | tf_op jit(solution)/shard_map/ppermute | solution.py:239
  63.6 1.7 %collective-permute-start.30 = (bf16[24,1536]{1,0:T(8,128)(2,1)S(1)}, bf16[24,1536]{1,0:T(8,128)(2,1)S(1)}, u32[]{:S(2)}, u32[]{:S(2)}) collective-permute-start(bf16[24,1536]{1,0:T(8,128)(2,1)S(1)} %get-tuple-element.56), channel_id=1, source_target_pairs={{0,1},{1,0},{2,3},{3,2},{4,5},{5,4},{6,7},{7,6},{8,9},{9,8},{10,11... | collective-permute-start | bytes 221192 | tf_op jit(solution)/shard_map/ppermute | solution.py:239
  65.6 2.4 %collective-permute-start.32 = (bf16[24,1536]{1,0:T(8,128)(2,1)S(1)}, bf16[24,1536]{1,0:T(8,128)(2,1)S(1)}, u32[]{:S(2)}, u32[]{:S(2)}) collective-permute-start(bf16[24,1536]{1,0:T(8,128)(2,1)S(1)} %get-tuple-element.58), channel_id=1, source_target_pairs={{0,3},{1,2},{2,1},{3,0},{4,7},{5,6},{6,5},{7,4},{8,11},{9,10},{10,... | collective-permute-start | bytes 221192 | tf_op jit(solution)/shard_map/ppermute | solution.py:239
  68.0 1.5 %collective-permute-done.30.refs_1_ = bf16[24,1536]{1,0:T(8,128)(2,1)S(1)} collective-permute-done((bf16[24,1536]{1,0:T(8,128)(2,1)S(1)}, bf16[24,1536]{1,0:T(8,128)(2,1)S(1)}, u32[]{:S(2)}, u32[]{:S(2)}) %collective-permute-start.30) | collective-permute-done | bytes 73760 | tf_op jit(solution)/shard_map/ppermute | solution.py:239
  69.5 2.4 %collective-permute-done.31.refs_2_ = bf16[24,1536]{1,0:T(8,128)(2,1)S(1)} collective-permute-done((bf16[24,1536]{1,0:T(8,128)(2,1)S(1)}, bf16[24,1536]{1,0:T(8,128)(2,1)S(1)}, u32[]{:S(2)}, u32[]{:S(2)}) %collective-permute-start.31) | collective-permute-done | bytes 73760 | tf_op jit(solution)/shard_map/ppermute | solution.py:239
  72.0 8.1 %all_to_all.5.arrived_ref = bf16[8,24,192]{2,1,0:T(8,128)(2,1)S(1)} all-to-all(bf16[8,24,192]{2,1,0:T(8,128)(2,1)S(1)} %shard_map.135), channel_id=1, replica_groups=mesh['seq'=8,'req'=4] {'seq'}, dimensions={0} | all-to-all | bytes 147456 | tf_op jit(solution)/shard_map/all_to_all | solution.py:736
  (75 shorter events, 19.2 us)
Async XLA Ops:
  1.6 29.3 %collective-permute-start.14 = (bf16[4,128,384]{2,1,0:T(8,128)(2,1)S(1)}, bf16[4,128,384]{2,1,0:T(8,128)(2,1)S(1)}, u32[]{:S(2)}, u32[]{:S(2)}) collective-permute-start(bf16[4,128,384]{2,1,0:T(8,128)(2,1)S(1)} %get-tuple-element.35), channel_id=1, source_target_pairs={{0,3},{1,2},{2,1},{3,0},{4,7},{5,6},{6,5},{7,4},{8,11},{9,10},{10,... | collective-permute-start | bytes 1179656 | tf_op jit(solution)/shard_map/ppermute | solution.py:239
  9.3 5.2 %collective-permute-start.2 = (bf16[5,24,128]{2,1,0:T(8,128)(2,1)}, bf16[5,24,128]{2,1,0:T(8,128)(2,1)S(1)}, u32[]{:S(2)}, u32[]{:S(2)}) collective-permute-start(bf16[5,24,128]{2,1,0:T(8,128)(2,1)} %get-tuple-element.32.refs_0_), channel_id=1, source_target_pairs={{0,24},{4,28},{8,16},{12,20},{16,8},{20,12},{24,0},{28,4},{1,25},{... | collective-permute-start | bytes 92168 | tf_op jit(solution)/shard_map/ppermute | solution.py:239
  11.9 4.1 %collective-permute-start.1 = (bf16[5,24,128]{2,1,0:T(8,128)(2,1)}, bf16[5,24,128]{2,1,0:T(8,128)(2,1)S(1)}, u32[]{:S(2)}, u32[]{:S(2)}) collective-permute-start(bf16[5,24,128]{2,1,0:T(8,128)(2,1)} %get-tuple-element.32.refs_0_), channel_id=1, source_target_pairs={{0,16},{4,20},{8,24},{12,28},{16,0},{20,4},{24,8},{28,12},{1,17},{... | collective-permute-start | bytes 92168 | tf_op jit(solution)/shard_map/ppermute | solution.py:239
  12.4 4.1 %collective-permute-start = (bf16[5,24,128]{2,1,0:T(8,128)(2,1)}, bf16[5,24,128]{2,1,0:T(8,128)(2,1)S(1)}, u32[]{:S(2)}, u32[]{:S(2)}) collective-permute-start(bf16[5,24,128]{2,1,0:T(8,128)(2,1)} %get-tuple-element.32.refs_0_), channel_id=1, source_target_pairs={{0,8},{4,12},{8,0},{12,4},{16,24},{20,28},{24,16},{28,20},{1,9},{5... | collective-permute-start | bytes 92168 | tf_op jit(solution)/shard_map/ppermute | solution.py:239
  12.9 3.6 %collective-permute-start.3 = (bf16[5,24,128]{2,1,0:T(8,128)(2,1)}, bf16[5,24,128]{2,1,0:T(8,128)(2,1)S(1)}, u32[]{:S(2)}, u32[]{:S(2)}) collective-permute-start(bf16[5,24,128]{2,1,0:T(8,128)(2,1)} %get-tuple-element.32.refs_0_), channel_id=1, source_target_pairs={{0,4},{4,0},{8,12},{12,8},{16,20},{20,16},{24,28},{28,24},{1,5},{5... | collective-permute-start | bytes 92168 | tf_op jit(solution)/shard_map/ppermute | solution.py:239
  14.5 2.0 %collective-permute-start.6 = (bf16[5,24,128]{2,1,0:T(8,128)(2,1)S(1)}, bf16[5,24,128]{2,1,0:T(8,128)(2,1)S(1)}, u32[]{:S(2)}, u32[]{:S(2)}) collective-permute-start(bf16[5,24,128]{2,1,0:T(8,128)(2,1)S(1)} %collective-permute-done.2.refs_3_), channel_id=1, source_target_pairs={{0,4},{4,0},{8,12},{12,8},{16,20},{20,16},{24,28},{28,24},{1,5},{5... | collective-permute-start | bytes 92168 | tf_op jit(solution)/shard_map/ppermute | solution.py:239
  16.5 23.9 %collective-permute-start.22 = (bf16[4,128,384]{2,1,0:T(8,128)(2,1)S(1)}, bf16[4,128,384]{2,1,0:T(8,128)(2,1)S(1)}, u32[]{:S(2)}, u32[]{:S(2)}) collective-permute-start(bf16[4,128,384]{2,1,0:T(8,128)(2,1)S(1)} %get-tuple-element.41), channel_id=1, source_target_pairs={{0,2},{1,3},{2,0},{3,1},{4,6},{5,7},{6,4},{7,5},{8,10},{9,11},{10,... | collective-permute-start | bytes 1179656 | tf_op jit(solution)/shard_map/ppermute | solution.py:239
  20.4 5.9 %collective-permute-start.9 = (bf16[72,640]{1,0:T(8,128)(2,1)S(1)}, bf16[72,640]{1,0:T(8,128)(2,1)S(1)}, u32[]{:S(2)}, u32[]{:S(2)}) collective-permute-start(bf16[72,640]{1,0:T(8,128)(2,1)S(1)} %shard_map.128.refs_0_), channel_id=1, source_target_pairs={{0,24},{4,28},{8,16},{12,20},{16,8},{20,12},{24,0},{28,4},{1,25},{... | collective-permute-start | bytes 276488 | tf_op jit(solution)/shard_map/ppermute | solution.py:239
  21.9 25.5 %collective-permute-start.26 = (bf16[4,128,384]{2,1,0:T(8,128)(2,1)S(1)}, bf16[4,128,384]{2,1,0:T(8,128)(2,1)S(1)}, u32[]{:S(2)}, u32[]{:S(2)}) collective-permute-start(bf16[4,128,384]{2,1,0:T(8,128)(2,1)S(1)} %get-tuple-element.47), channel_id=1, source_target_pairs={{0,1},{1,0},{2,3},{3,2},{4,5},{5,4},{6,7},{7,6},{8,9},{9,8},{10,11... | collective-permute-start | bytes 1179656 | tf_op jit(solution)/shard_map/ppermute | solution.py:239
  21.9 6.3 %collective-permute-start.8 = (bf16[72,640]{1,0:T(8,128)(2,1)S(1)}, bf16[72,640]{1,0:T(8,128)(2,1)S(1)}, u32[]{:S(2)}, u32[]{:S(2)}) collective-permute-start(bf16[72,640]{1,0:T(8,128)(2,1)S(1)} %shard_map.128.refs_0_), channel_id=1, source_target_pairs={{0,16},{4,20},{8,24},{12,28},{16,0},{20,4},{24,8},{28,12},{1,17},{... | collective-permute-start | bytes 276488 | tf_op jit(solution)/shard_map/ppermute | solution.py:239
  26.3 4.6 %collective-permute-start.7 = (bf16[72,640]{1,0:T(8,128)(2,1)S(1)}, bf16[72,640]{1,0:T(8,128)(2,1)S(1)}, u32[]{:S(2)}, u32[]{:S(2)}) collective-permute-start(bf16[72,640]{1,0:T(8,128)(2,1)S(1)} %shard_map.128.refs_0_), channel_id=1, source_target_pairs={{0,8},{4,12},{8,0},{12,4},{16,24},{20,28},{24,16},{28,20},{1,9},{5... | collective-permute-start | bytes 276488 | tf_op jit(solution)/shard_map/ppermute | solution.py:239
  28.2 4.3 %collective-permute-start.13 = (bf16[72,640]{1,0:T(8,128)(2,1)S(1)}, bf16[72,640]{1,0:T(8,128)(2,1)S(1)}, u32[]{:S(2)}, u32[]{:S(2)}) collective-permute-start(bf16[72,640]{1,0:T(8,128)(2,1)S(1)} %collective-permute-done.9.refs_3_), channel_id=1, source_target_pairs={{0,4},{4,0},{8,12},{12,8},{16,20},{20,16},{24,28},{28,24},{1,5},{5... | collective-permute-start | bytes 276488 | tf_op jit(solution)/shard_map/ppermute | solution.py:239
  34.3 6.1 %collective-permute-start.17 = (f32[24,192]{1,0:T(8,128)S(1)}, f32[24,192]{1,0:T(8,128)S(1)}, u32[]{:S(2)}, u32[]{:S(2)}) collective-permute-start(f32[24,192]{1,0:T(8,128)S(1)} %get-tuple-element.38.refs_0_), channel_id=1, source_target_pairs={{0,24},{4,28},{8,16},{12,20},{16,8},{20,12},{24,0},{28,4},{1,25},{... | collective-permute-start | bytes 55304 | tf_op jit(solution)/shard_map/ppermute | solution.py:239
  35.9 5.1 %collective-permute-start.16 = (f32[24,192]{1,0:T(8,128)S(1)}, f32[24,192]{1,0:T(8,128)S(1)}, u32[]{:S(2)}, u32[]{:S(2)}) collective-permute-start(f32[24,192]{1,0:T(8,128)S(1)} %get-tuple-element.38.refs_0_), channel_id=1, source_target_pairs={{0,16},{4,20},{8,24},{12,28},{16,0},{20,4},{24,8},{28,12},{1,17},{... | collective-permute-start | bytes 55304 | tf_op jit(solution)/shard_map/ppermute | solution.py:239
  36.3 4.7 %collective-permute-start.15 = (f32[24,192]{1,0:T(8,128)S(1)}, f32[24,192]{1,0:T(8,128)S(1)}, u32[]{:S(2)}, u32[]{:S(2)}) collective-permute-start(f32[24,192]{1,0:T(8,128)S(1)} %get-tuple-element.38.refs_0_), channel_id=1, source_target_pairs={{0,8},{4,12},{8,0},{12,4},{16,24},{20,28},{24,16},{28,20},{1,9},{5... | collective-permute-start | bytes 55304 | tf_op jit(solution)/shard_map/ppermute | solution.py:239
  42.5 4.9 %collective-permute-start.23 = (bf16[24,512]{1,0:T(8,128)(2,1)S(1)}, bf16[24,512]{1,0:T(8,128)(2,1)S(1)}, u32[]{:S(2)}, u32[]{:S(2)}) collective-permute-start(bf16[24,512]{1,0:T(8,128)(2,1)S(1)} %get-tuple-element.44), channel_id=1, source_target_pairs={{0,1},{1,0},{2,3},{3,2},{4,5},{5,4},{6,7},{7,6},{8,9},{9,8},{10,11... | collective-permute-start | bytes 73736 | tf_op jit(solution)/shard_map/ppermute | solution.py:239
  44.8 5.1 %collective-permute-start.24 = (bf16[24,512]{1,0:T(8,128)(2,1)S(1)}, bf16[24,512]{1,0:T(8,128)(2,1)S(1)}, u32[]{:S(2)}, u32[]{:S(2)}) collective-permute-start(bf16[24,512]{1,0:T(8,128)(2,1)S(1)} %get-tuple-element.45), channel_id=1, source_target_pairs={{0,2},{1,3},{2,0},{3,1},{4,6},{5,7},{6,4},{7,5},{8,10},{9,11},{10,... | collective-permute-start | bytes 73736 | tf_op jit(solution)/shard_map/ppermute | solution.py:239
  46.1 5.6 %collective-permute-start.25 = (bf16[24,512]{1,0:T(8,128)(2,1)S(1)}, bf16[24,512]{1,0:T(8,128)(2,1)S(1)}, u32[]{:S(2)}, u32[]{:S(2)}) collective-permute-start(bf16[24,512]{1,0:T(8,128)(2,1)S(1)} %get-tuple-element.46), channel_id=1, source_target_pairs={{0,3},{1,2},{2,1},{3,0},{4,7},{5,6},{6,5},{7,4},{8,11},{9,10},{10,... | collective-permute-start | bytes 73736 | tf_op jit(solution)/shard_map/ppermute | solution.py:239
  52.7 4.7 %collective-permute-start.27 = (bf16[192,256]{1,0:T(8,128)(2,1)S(1)}, bf16[192,256]{1,0:T(8,128)(2,1)S(1)}, u32[]{:S(2)}, u32[]{:S(2)}) collective-permute-start(bf16[192,256]{1,0:T(8,128)(2,1)S(1)} %get-tuple-element.50), channel_id=1, source_target_pairs={{0,1},{1,0},{2,3},{3,2},{4,5},{5,4},{6,7},{7,6},{8,9},{9,8},{10,11... | collective-permute-start | bytes 294920 | tf_op jit(solution)/shard_map/ppermute | solution.py:239
  53.0 9.5 %collective-permute-start.28 = (bf16[192,256]{1,0:T(8,128)(2,1)S(1)}, bf16[192,256]{1,0:T(8,128)(2,1)S(1)}, u32[]{:S(2)}, u32[]{:S(2)}) collective-permute-start(bf16[192,256]{1,0:T(8,128)(2,1)S(1)} %get-tuple-element.51), channel_id=1, source_target_pairs={{0,2},{1,3},{2,0},{3,1},{4,6},{5,7},{6,4},{7,5},{8,10},{9,11},{10,... | collective-permute-start | bytes 294920 | tf_op jit(solution)/shard_map/ppermute | solution.py:239
  54.8 7.7 %collective-permute-start.29 = (bf16[192,256]{1,0:T(8,128)(2,1)S(1)}, bf16[192,256]{1,0:T(8,128)(2,1)S(1)}, u32[]{:S(2)}, u32[]{:S(2)}) collective-permute-start(bf16[192,256]{1,0:T(8,128)(2,1)S(1)} %get-tuple-element.52), channel_id=1, source_target_pairs={{0,3},{1,2},{2,1},{3,0},{4,7},{5,6},{6,5},{7,4},{8,11},{9,10},{10,... | collective-permute-start | bytes 294920 | tf_op jit(solution)/shard_map/ppermute | solution.py:239
  63.6 5.9 %collective-permute-start.30 = (bf16[24,1536]{1,0:T(8,128)(2,1)S(1)}, bf16[24,1536]{1,0:T(8,128)(2,1)S(1)}, u32[]{:S(2)}, u32[]{:S(2)}) collective-permute-start(bf16[24,1536]{1,0:T(8,128)(2,1)S(1)} %get-tuple-element.56), channel_id=1, source_target_pairs={{0,1},{1,0},{2,3},{3,2},{4,5},{5,4},{6,7},{7,6},{8,9},{9,8},{10,11... | collective-permute-start | bytes 221192 | tf_op jit(solution)/shard_map/ppermute | solution.py:239
  65.2 6.7 %collective-permute-start.31 = (bf16[24,1536]{1,0:T(8,128)(2,1)S(1)}, bf16[24,1536]{1,0:T(8,128)(2,1)S(1)}, u32[]{:S(2)}, u32[]{:S(2)}) collective-permute-start(bf16[24,1536]{1,0:T(8,128)(2,1)S(1)} %get-tuple-element.57), channel_id=1, source_target_pairs={{0,2},{1,3},{2,0},{3,1},{4,6},{5,7},{6,4},{7,5},{8,10},{9,11},{10,... | collective-permute-start | bytes 221192 | tf_op jit(solution)/shard_map/ppermute | solution.py:239
  65.6 6.3 %collective-permute-start.32 = (bf16[24,1536]{1,0:T(8,128)(2,1)S(1)}, bf16[24,1536]{1,0:T(8,128)(2,1)S(1)}, u32[]{:S(2)}, u32[]{:S(2)}) collective-permute-start(bf16[24,1536]{1,0:T(8,128)(2,1)S(1)} %get-tuple-element.58), channel_id=1, source_target_pairs={{0,3},{1,2},{2,1},{3,0},{4,7},{5,6},{6,5},{7,4},{8,11},{9,10},{10,... | collective-permute-start | bytes 221192 | tf_op jit(solution)/shard_map/ppermute | solution.py:239
  (20 other events, 199.9 us)

commit v3 on v2

--- a/solution.py
+++ b/solution.py
@@ -198,7 +198,7 @@
 STAT = 128
 WIDE = KVD + STAT
 VMEM = pl.BlockSpec(memory_space=pltpu.VMEM)
-HBM = pl.BlockSpec(memory_space=pltpu.HBM)
+SMEM = pl.BlockSpec(memory_space=pltpu.SMEM)
 
 
 def kernel_call(body, out_shape, in_specs, scratch=(), out_specs=None, vmem_mib=8, cost=0.5):
@@ -243,31 +243,12 @@
     return lax.optimization_barrier((value, *others))[0]
 
 
-def project_kernel(groups, *refs):
-    x_hbm, attn_hbm, moe_hbm, w_hbm, lengths_hbm, pages_hbm, routes_hbm, weights_hbm = refs[:8]
-    heads_ref, x_ref, live_ref, routing_ref, gain_ref = refs[8:13]
-    x_in, attn_gain, moe_gain, w_in, lengths, pages, routes, weights, sem = refs[13:]
-    loads = [
-        pltpu.make_async_copy(source, target, sem.at[i])
-        for i, (source, target) in enumerate(
-            [
-                (lengths_hbm, lengths),
-                (x_hbm, x_in),
-                (attn_hbm, attn_gain),
-                (w_hbm, w_in),
-                (pages_hbm, pages),
-                (routes_hbm, routes),
-                (weights_hbm, weights),
-                (moe_hbm, moe_gain),
-            ]
-        )
-    ]
-    for load in loads:
-        load.start()
+def project_kernel(*refs):
+    x_in, attn_gain, moe_gain, w_in, lengths, pages, routes, weights = refs[:8]
+    heads_ref, x_ref, live_ref, routing_ref, gain_ref = refs[8:]
     requests = x_in.shape[0]
     row_count = requests * NSTEP
     shape = (row_count, STAT)
-    loads[0].wait()
     row, lane = iota(shape, 0), iota(shape, 1)
     position = row % NSTEP
     for r in range(requests):
@@ -276,13 +257,10 @@
     angle = position.astype(F32) * rates
     cosine = jnp.cos(angle)
     sine = jnp.where(lane % HD < HD // 2, -jnp.sin(angle), jnp.sin(angle))
-    loads[1].wait()
     x = rows_of(x_in)
     x_ref[...] = x
     power = jnp.mean(x * x, axis=-1, keepdims=True)
-    loads[2].wait()
     normed = (x * lax.rsqrt(power + EPS) * attn_gain[...].reshape(1, D)).astype(BF16)
-    loads[3].wait()
     projected = dot_nt(normed, w_in[...])
     heads = w_in.shape[0] // HD
     first = lax.axis_index("seq") * heads
@@ -291,8 +269,6 @@
         both = jnp.concatenate([one, one], axis=1)
         turned = both * cosine + pltpu.roll(both, HD // 2, 1) * sine
         heads_ref[i] = jnp.where(first + i < HEADS + KVH, turned, both).astype(BF16)
-    for load in loads[4:]:
-        load.wait()
     slots = live_ref.shape[1]
     slot = iota((1, slots), 1)
     for r in range(requests):
@@ -306,19 +282,6 @@
         [rows_of(routes), high, middle, low, jnp.zeros((row_count, STAT - 4 * TOP), F32)], axis=1
     )
     gain_ref[...] = moe_gain[...].reshape(1, D)
-
-
-def cut_kernel(groups, down_ref, *refs):
-    cut_refs, sem = refs[:-1], refs[-1]
-    depth = cut_refs[0].shape[1]
-    copies = []
-    for k in range(1, groups):
-        start = pl.multiple_of((lax.axis_index("req") ^ k) * depth, depth)
-        source = down_ref.at[:, pl.ds(start, depth), :]
-        copies.append(pltpu.make_async_copy(source, cut_refs[k - 1], sem.at[k - 1]))
-        copies[-1].start()
-    for copy in copies:
-        copy.wait()
 
 
 def gather_pieces(near_refs, far_refs, all_ref):
@@ -539,57 +502,40 @@
         here = same_group & (across(routed, eye) > 0.5) & (ordinal_of_slot == ordinal)
         placed.append(jnp.where(here, 1.0, 0.0))
         scales.append(jnp.sum(jnp.where(here, across(scale, eye), 0.0), axis=1, keepdims=True))
-    placed = jnp.concatenate(placed, axis=0).astype(BF16)
-    placed_ref[...] = placed
-    scale_ref[...] = jnp.broadcast_to(jnp.concatenate(scales, axis=0), scale_ref.shape)
-    taken = jnp.dot(placed, mixed, preferred_element_type=F32).astype(BF16)
+    all_placed = jnp.concatenate(placed, axis=0).astype(BF16)
+    taken = jnp.dot(all_placed, mixed, preferred_element_type=F32).astype(BF16)
     for e in range(experts):
-        full_ref[e * slots : (e + 1) * slots, :] = jnp.dot(
-            taken[e * slots : (e + 1) * slots], w_ref[e], preferred_element_type=F32
-        )
-    piece = FFE // groups
+        rows = slice(e * slots, (e + 1) * slots)
+        placed_ref[e] = all_placed[rows]
+        scale_ref[e] = jnp.broadcast_to(scales[e], scale_ref.shape[1:])
+        full_ref[e] = jnp.dot(taken[rows], w_ref[e], preferred_element_type=F32).astype(BF16)
     for k in range(groups):
-        begin = pl.multiple_of((me ^ k) * piece, STAT)
-        message_refs[k][:, :piece] = full_ref[:, pl.ds(begin, piece)].astype(BF16)
-        message_refs[k][:, piece:] = full_ref[:, pl.ds(begin + FFE, piece)].astype(BF16)
+        message_refs[k][...] = full_ref[me ^ k]
 
 
 def down_kernel(groups, *refs):
     message_refs = refs[:groups]
-    own_ref = refs[groups]
-    down_refs = refs[groups + 1 : 2 * groups]
-    placed_ref, scale_ref = refs[2 * groups : 2 * groups + 2]
-    out_refs = refs[2 * groups + 2 :]
+    down_ref, placed_ref, scale_ref = refs[groups : groups + 3]
+    out_refs = refs[groups + 3 :]
     me = lax.axis_index("req")
-    piece = message_refs[0].shape[1] // 2
     gate_up = message_refs[0][...].astype(F32)
     for ref in message_refs[1:]:
         gate_up = gate_up + ref[...].astype(F32)
-    gate, up = gate_up[:, :piece], gate_up[:, piece:]
+    gate, up = gate_up[:, :FFE], gate_up[:, FFE:]
     hidden = (gate / (1.0 + jnp.exp(-gate)) * up).astype(BF16)
-    experts = own_ref.shape[0]
-    slots = placed_ref.shape[0] // experts
-    placed = placed_ref[...]
-    scale = scale_ref[...][:, :1]
-    begin = pl.multiple_of(me * piece, STAT)
-    width = own_ref.shape[2]
+    placed, scale = placed_ref[me], scale_ref[me][:, :1]
+    width = down_ref.shape[2]
     row_count = out_refs[0].shape[0]
     for k in range(groups):
-        produced = []
-        for e in range(experts):
-            weight = own_ref[e, pl.ds(begin, piece), :] if k == 0 else down_refs[k - 1][e]
-            produced.append(
-                jnp.dot(
-                    hidden[e * slots : (e + 1) * slots], weight, preferred_element_type=F32
-                )
-            )
-        produced = (jnp.concatenate(produced, axis=0) * scale).astype(BF16)
+        produced = jnp.dot(hidden, down_ref[k], preferred_element_type=F32)
         total = lax.dot_general(
-            placed, produced, (((0,), (0,)), ((), ())), preferred_element_type=F32
+            placed,
+            (produced * scale).astype(BF16),
+            (((0,), (0,)), ((), ())),
+            preferred_element_type=F32,
         )
-        column = pl.multiple_of((me ^ k) * width, STAT)
         for j in range(groups):
-            out_refs[j][:, pl.ds(column, width)] = total[
+            out_refs[j][:, k * width : (k + 1) * width] = total[
                 j * row_count : (j + 1) * row_count
             ].astype(BF16)
 
@@ -633,46 +579,26 @@
     chips = members // 2
     heads = w_qkv.shape[1] // HD
     width = w_o.shape[1]
-    depth = w_down.shape[1] // groups
-    slots = cache_k.shape[1]
 
     own_heads, x, live, routing, gain = kernel_call(
-        lambda *refs: project_kernel(groups, *refs),
+        project_kernel,
         [
             jax.ShapeDtypeStruct((heads, row_count, 2 * HD), BF16),
             jax.ShapeDtypeStruct((row_count, D), F32),
-            jax.ShapeDtypeStruct((requests, slots), F32),
+            jax.ShapeDtypeStruct((requests, cache_k.shape[1]), F32),
             jax.ShapeDtypeStruct((row_count, STAT), F32),
             jax.ShapeDtypeStruct((1, D), F32),
         ],
-        [HBM] * 8,
-        [
-            pltpu.VMEM(x_in.shape, BF16),
-            pltpu.VMEM((D,), F32),
-            pltpu.VMEM((D,), F32),
-            pltpu.VMEM((w_qkv.shape[1], D), BF16),
-            pltpu.SMEM(lengths.shape, jnp.int32),
-            pltpu.SMEM(page_map.shape, jnp.int32),
-            pltpu.VMEM(routes.shape, jnp.int32),
-            pltpu.VMEM(route_weights.shape, F32),
-            pltpu.SemaphoreType.DMA((8,)),
-        ],
-        vmem_mib=60,
+        [VMEM] * 4 + [SMEM] * 2 + [VMEM] * 2,
     )(x_in, attn_gain, moe_gain, w_qkv.T, lengths, page_map, routes, route_weights)
-    cuts = kernel_call(
-        lambda *refs: cut_kernel(groups, *refs),
-        [jax.ShapeDtypeStruct((w_down.shape[0], depth, w_down.shape[2]), BF16)] * (groups - 1),
-        [HBM],
-        [pltpu.SemaphoreType.DMA((groups - 1,))],
-        [HBM] * (groups - 1),
-    )(w_down)
-    downs = [swap(cuts[k - 1], "req", k) for k in range(1, groups)]
-
-    def gathered(own):
-        near = [own] + [swap(own, "seq", 2 * k) for k in range(1, chips)]
+    def gathered(own, *first):
+        near = [swap(own, "seq", 2 * k) for k in range(chips - 1, 0, -1)]
+        near = [own] + near[::-1]
+        near[1] = after(near[1], *first) if first else near[1]
         return near, [swap(piece, "seq", 1) for piece in near]
 
     near, far = gathered(own_heads)
+    down = lax.all_to_all(w_down, "req", 0, 0, tiled=True)
     part_shape = jax.ShapeDtypeStruct((GROUP * row_count, WIDE), BF16)
     head_scratch = [
         pltpu.VMEM((2, chips, heads, row_count, 2 * HD), BF16),
@@ -692,15 +618,13 @@
         head_scratch,
         cost=0.5,
     )(*near, *far)
-    near, far = gathered(part)
-    x = after(x, downs[2])
+    near, far = gathered(part, fresh)
     share, resid = kernel_call(
         lambda *refs: merge_kernel(members + 1, *refs),
         [jax.ShapeDtypeStruct((row_count, width), F32)] * 2,
         [VMEM] * (members + 3),
     )(*near, *far, fresh, x, w_o.T)
     near, far = gathered(share)
-    routing = after(routing, downs[1])
     packs = kernel_call(
         lambda *refs: mix_kernel(chips, groups, *refs),
         [jax.ShapeDtypeStruct((row_count, 2 * width + STAT), BF16)] * groups,
@@ -712,22 +636,22 @@
         return [pieces[0]] + [swap(pieces[k], "req", k) for k in range(1, groups)]
 
     experts = w_gate_up.shape[0]
-    total_slots = experts * groups * CAP
+    slots = groups * CAP
     *messages, placed, scale = kernel_call(
         lambda *refs: gate_kernel(groups, *refs),
-        [jax.ShapeDtypeStruct((total_slots, 2 * FFE // groups), BF16)] * groups
+        [jax.ShapeDtypeStruct((slots, 2 * FFE), BF16)] * groups
         + [
-            jax.ShapeDtypeStruct((total_slots, groups * row_count), BF16),
-            jax.ShapeDtypeStruct((total_slots, STAT), F32),
+            jax.ShapeDtypeStruct((experts, slots, groups * row_count), BF16),
+            jax.ShapeDtypeStruct((experts, slots, STAT), F32),
         ],
         [VMEM] * (groups + 1),
-        [pltpu.VMEM((total_slots, 2 * FFE), F32)],
-    )(*exchanged(packs), after(w_gate_up, downs[0]))
+        [pltpu.VMEM((experts, slots, 2 * FFE), BF16)],
+    )(*exchanged(packs), w_gate_up)
     outs = kernel_call(
         lambda *refs: down_kernel(groups, *refs),
         [jax.ShapeDtypeStruct((row_count, D), BF16)] * groups,
-        [VMEM] * (2 * groups + 2),
-    )(*exchanged(messages), w_down, *downs, placed, scale)
+        [VMEM] * (groups + 3),
+    )(*exchanged(messages), down, placed, scale)
     spread = kernel_call(
         lambda *refs: spread_kernel(groups, *refs),
         jax.ShapeDtypeStruct((members, row_count, width), BF16),
@@ -740,13 +664,13 @@
 
 
 def local(*args):
-    w_qkv, w_o = args[3], args[4]
+    w_qkv, w_o, w_gate_up = args[3], args[4], args[11]
     members, groups = lax.axis_size("seq"), lax.axis_size("req")
     fits = (
         members == 2 * groups
         and groups & (groups - 1) == 0
         and w_qkv.shape[1] % HD == 0
-        and (FFE // groups) % STAT == 0
+        and w_gate_up.shape[0] == groups
         and (2 * w_o.shape[1]) % STAT == 0
     )
     return staged(*args) if fits else plain(*args)

time: 81.1 us -> 75.5 us (0.931)
  local copies, waits for them, and re-layouts: 2.88 us -> 0.05 us
  Pallas kernels: 9.69 us -> 7.84 us
    all_to_all x0 -> x1, starting transfers between devices: none -> 6.48 us  [staged(): down = lax.all_to_all(w_down, 'req', 0, 0, tiled=True)]
    ppermute x33 -> x30, starting transfers between devices: 31 us -> 24.9 us  [swap(): return lax.ppermute(value, axis, pairs)]
    unnamed x22 -> x24, local copies, waits for them, and re-layouts: 2.88 us -> 0.05 us
    pallas_call x2 -> x1, Pallas kernels: 2.79 us -> 1.21 us  [staged(): kernel_call(project_kernel, [jax.ShapeDtypeStruct((heads, row_count, 2 *...]
    ppermute x33 -> x30, waiting for transfers between devices: 28.9 us -> 28.2 us  [swap(): return lax.ppermute(value, axis, pairs)]
  transfers between devices with their start and end apart: 33 -> 31, of which waited for: 19 -> 19; matrix products, arithmetic and copies ran while one was open for 0% -> 0% of each run, Pallas kernels for 8% -> 8%
where the time goes in v3:
time: 75.5 us; the launch traced here: 75.3 us
  starting transfers between devices  31.4 us (42%)
  waiting for transfers between devices  28.3 us (37%)
  Pallas kernels  7.84 us (10%)
  blocking collectives  7.58 us (10%)
    ppermute x30, waiting for transfers between devices, swap(): return lax.ppermute(value, axis, pairs)  28.2 us
    ppermute x30, starting transfers between devices, swap(): return lax.ppermute(value, axis, pairs)  24.9 us
    all_to_all x1, blocking collectives, staged(): arrived = lax.all_to_all(spread, 'seq', 0, 0, tiled=True)  7.58 us
    all_to_all x1, starting transfers between devices, staged(): down = lax.all_to_all(w_down, 'req', 0, 0, tiled=True)  6.48 us
    pallas_call x1, Pallas kernels, staged(): kernel_call(lambda *refs: merge_kernel(members + 1, *refs), [jax.ShapeDty...  1.76 us
  transfers between devices with their start and end apart: 31, of which 19 were waited for; matrix products, arithmetic and copies ran while one was open for 0% of the time, Pallas kernels for 8%

profile of v3, /device:TPU:0, one launch (start us, length us, event | category | flops | bytes accessed | tf_op | source)
XLA Modules:
  0.0 75.3 jit_solution(9370481827053683400)
XLA Ops:
  0.0 6.5 %all-to-all-start = ((bf16[4,512,384]{2,1,0:T(8,128)(2,1)}), bf16[4,512,384]{2,1,0:T(8,128)(2,1)S(1)}, u32[]{:S(2)}, u32[]{:S(2)}) async-start(bf16[4,512,384]{2,1,0:T(8,128)(2,1)} %param.25), calls=%async_computation | async-start | bytes 3145728 | tf_op jit(solution)/shard_map/all_to_all | solution.py:601
  7.8 1.6 %collective-permute-start = (bf16[5,24,128]{2,1,0:T(8,128)(2,1)S(1)}, bf16[5,24,128]{2,1,0:T(8,128)(2,1)S(1)}, u32[]{:S(2)}, u32[]{:S(2)}) collective-permute-start(bf16[5,24,128]{2,1,0:T(8,128)(2,1)S(1)} %get-tuple-element.27.refs_0_), channel_id=1, source_target_pairs={{0,8},{4,12},{8,0},{12,4},{16,24},{20,28},{24,16},{28,20},{1,9},{5... | collective-permute-start | bytes 92168 | tf_op jit(solution)/shard_map/ppermute | solution.py:239
  9.4 1.5 %collective-permute-start.1 = (bf16[5,24,128]{2,1,0:T(8,128)(2,1)S(1)}, bf16[5,24,128]{2,1,0:T(8,128)(2,1)S(1)}, u32[]{:S(2)}, u32[]{:S(2)}) collective-permute-start(bf16[5,24,128]{2,1,0:T(8,128)(2,1)S(1)} %get-tuple-element.27.refs_0_), channel_id=1, source_target_pairs={{0,16},{4,20},{8,24},{12,28},{16,0},{20,4},{24,8},{28,12},{1,17},{... | collective-permute-start | bytes 92168 | tf_op jit(solution)/shard_map/ppermute | solution.py:239
  11.9 1.4 %collective-permute-done.1.refs_2_ = bf16[5,24,128]{2,1,0:T(8,128)(2,1)S(1)} collective-permute-done((bf16[5,24,128]{2,1,0:T(8,128)(2,1)S(1)}, bf16[5,24,128]{2,1,0:T(8,128)(2,1)S(1)}, u32[]{:S(2)}, u32[]{:S(2)}) %collective-permute-start.1) | collective-permute-done | bytes 30752 | tf_op jit(solution)/shard_map/ppermute | solution.py:239
  13.3 2.4 %collective-permute-done.2.refs_3_ = bf16[5,24,128]{2,1,0:T(8,128)(2,1)S(1)} collective-permute-done((bf16[5,24,128]{2,1,0:T(8,128)(2,1)S(1)}, bf16[5,24,128]{2,1,0:T(8,128)(2,1)S(1)}, u32[]{:S(2)}, u32[]{:S(2)}) %collective-permute-start.2) | collective-permute-done | bytes 30752 | tf_op jit(solution)/shard_map/ppermute | solution.py:239
  19.1 2.4 %collective-permute-start.9 = (bf16[72,640]{1,0:T(8,128)(2,1)S(1)}, bf16[72,640]{1,0:T(8,128)(2,1)S(1)}, u32[]{:S(2)}, u32[]{:S(2)}) collective-permute-start(bf16[72,640]{1,0:T(8,128)(2,1)S(1)} %shard_map.128.refs_0_), channel_id=1, source_target_pairs={{0,24},{4,28},{8,16},{12,20},{16,8},{20,12},{24,0},{28,4},{1,25},{... | collective-permute-start | bytes 276488 | tf_op jit(solution)/shard_map/ppermute | solution.py:239
  23.3 1.7 %collective-permute-done.8.refs_2_ = bf16[72,640]{1,0:T(8,128)(2,1)S(1)} collective-permute-done((bf16[72,640]{1,0:T(8,128)(2,1)S(1)}, bf16[72,640]{1,0:T(8,128)(2,1)S(1)}, u32[]{:S(2)}, u32[]{:S(2)}) %collective-permute-start.8) | collective-permute-done | bytes 92192 | tf_op jit(solution)/shard_map/ppermute | solution.py:239
  26.5 1.8 %shard_map.130 = (f32[24,192]{1,0:T(8,128)S(1)}, f32[24,192]{1,0:T(8,128)S(1)}) custom-call(bf16[72,640]{1,0:T(8,128)(2,1)S(1)} %shard_map.128.refs_0_, bf16[72,640]{1,0:T(8,128)(2,1)S(1)} %collective-permute-done.7.refs_1_, bf16[72,640]{1,0:T(8,128)(2,1)S(1)} %collective-permute-done.8.refs_2_, bf16[72,640]{1,0:T(8,128)(2,1)S(1)} %collective-permute-done.9.refs_3_, ...), custom_call_target="tpu_custom_call" | custom-call | flops 500000000 | bytes 1500000 | tf_op jit(solution)/shard_map/pallas_call | solution.py:622
  28.3 1.6 %collective-permute-start.14 = (f32[24,192]{1,0:T(8,128)S(1)}, f32[24,192]{1,0:T(8,128)S(1)}, u32[]{:S(2)}, u32[]{:S(2)}) collective-permute-start(f32[24,192]{1,0:T(8,128)S(1)} %get-tuple-element.32.refs_0_), channel_id=1, source_target_pairs={{0,8},{4,12},{8,0},{12,4},{16,24},{20,28},{24,16},{28,20},{1,9},{5... | collective-permute-start | bytes 55304 | tf_op jit(solution)/shard_map/ppermute | solution.py:239
  32.4 1.3 %collective-permute-done.15.refs_2_ = f32[24,192]{1,0:T(8,128)S(1)} collective-permute-done((f32[24,192]{1,0:T(8,128)S(1)}, f32[24,192]{1,0:T(8,128)S(1)}, u32[]{:S(2)}, u32[]{:S(2)}) %collective-permute-start.15) | collective-permute-done | bytes 18464 | tf_op jit(solution)/shard_map/ppermute | solution.py:239
  33.7 1.7 %collective-permute-done.16.refs_3_ = f32[24,192]{1,0:T(8,128)S(1)} collective-permute-done((f32[24,192]{1,0:T(8,128)S(1)}, f32[24,192]{1,0:T(8,128)S(1)}, u32[]{:S(2)}, u32[]{:S(2)}) %collective-permute-start.16) | collective-permute-done | bytes 18464 | tf_op jit(solution)/shard_map/ppermute | solution.py:239
  36.8 2.1 %collective-permute-start.21 = (bf16[24,512]{1,0:T(8,128)(2,1)S(1)}, bf16[24,512]{1,0:T(8,128)(2,1)S(1)}, u32[]{:S(2)}, u32[]{:S(2)}) collective-permute-start(bf16[24,512]{1,0:T(8,128)(2,1)S(1)} %get-tuple-element.36), channel_id=1, source_target_pairs={{0,1},{1,0},{2,3},{3,2},{4,5},{5,4},{6,7},{7,6},{8,9},{9,8},{10,11... | collective-permute-start | bytes 73736 | tf_op jit(solution)/shard_map/ppermute | solution.py:239
  38.9 2.4 %collective-permute-start.22 = (bf16[24,512]{1,0:T(8,128)(2,1)S(1)}, bf16[24,512]{1,0:T(8,128)(2,1)S(1)}, u32[]{:S(2)}, u32[]{:S(2)}) collective-permute-start(bf16[24,512]{1,0:T(8,128)(2,1)S(1)} %get-tuple-element.37), channel_id=1, source_target_pairs={{0,2},{1,3},{2,0},{3,1},{4,6},{5,7},{6,4},{7,5},{8,10},{9,11},{10,... | collective-permute-start | bytes 73736 | tf_op jit(solution)/shard_map/ppermute | solution.py:239
  41.3 1.9 %collective-permute-done.21.refs_1_ = bf16[24,512]{1,0:T(8,128)(2,1)S(1)} collective-permute-done((bf16[24,512]{1,0:T(8,128)(2,1)S(1)}, bf16[24,512]{1,0:T(8,128)(2,1)S(1)}, u32[]{:S(2)}, u32[]{:S(2)}) %collective-permute-start.21) | collective-permute-done | bytes 24608 | tf_op jit(solution)/shard_map/ppermute | solution.py:239
  43.3 1.6 %collective-permute-done.22.refs_2_ = bf16[24,512]{1,0:T(8,128)(2,1)S(1)} collective-permute-done((bf16[24,512]{1,0:T(8,128)(2,1)S(1)}, bf16[24,512]{1,0:T(8,128)(2,1)S(1)}, u32[]{:S(2)}, u32[]{:S(2)}) %collective-permute-start.22) | collective-permute-done | bytes 24608 | tf_op jit(solution)/shard_map/ppermute | solution.py:239
  44.8 2.0 %collective-permute-done.23.refs_3_ = bf16[24,512]{1,0:T(8,128)(2,1)S(1)} collective-permute-done((bf16[24,512]{1,0:T(8,128)(2,1)S(1)}, bf16[24,512]{1,0:T(8,128)(2,1)S(1)}, u32[]{:S(2)}, u32[]{:S(2)}) %collective-permute-start.23) | collective-permute-done | bytes 24608 | tf_op jit(solution)/shard_map/ppermute | solution.py:239
  48.7 3.6 %collective-permute-start.26 = (bf16[48,1024]{1,0:T(8,128)(2,1)S(1)}, bf16[48,1024]{1,0:T(8,128)(2,1)S(1)}, u32[]{:S(2)}, u32[]{:S(2)}) collective-permute-start(bf16[48,1024]{1,0:T(8,128)(2,1)S(1)} %get-tuple-element.42), channel_id=1, source_target_pairs={{0,3},{1,2},{2,1},{3,0},{4,7},{5,6},{6,5},{7,4},{8,11},{9,10},{10,... | collective-permute-start | bytes 294920 | tf_op jit(solution)/shard_map/ppermute | solution.py:239
  52.3 1.5 %collective-permute-done.24.refs_1_ = bf16[48,1024]{1,0:T(8,128)(2,1)S(1)} collective-permute-done((bf16[48,1024]{1,0:T(8,128)(2,1)S(1)}, bf16[48,1024]{1,0:T(8,128)(2,1)S(1)}, u32[]{:S(2)}, u32[]{:S(2)}) %collective-permute-start.24) | collective-permute-done | bytes 98336 | tf_op jit(solution)/shard_map/ppermute | solution.py:239
  53.8 3.5 %collective-permute-done.25.refs_2_ = bf16[48,1024]{1,0:T(8,128)(2,1)S(1)} collective-permute-done((bf16[48,1024]{1,0:T(8,128)(2,1)S(1)}, bf16[48,1024]{1,0:T(8,128)(2,1)S(1)}, u32[]{:S(2)}, u32[]{:S(2)}) %collective-permute-start.25) | collective-permute-done | bytes 98336 | tf_op jit(solution)/shard_map/ppermute | solution.py:239
  58.2 1.7 %collective-permute-start.27 = (bf16[24,1536]{1,0:T(8,128)(2,1)S(1)}, bf16[24,1536]{1,0:T(8,128)(2,1)S(1)}, u32[]{:S(2)}, u32[]{:S(2)}) collective-permute-start(bf16[24,1536]{1,0:T(8,128)(2,1)S(1)} %get-tuple-element.46), channel_id=1, source_target_pairs={{0,1},{1,0},{2,3},{3,2},{4,5},{5,4},{6,7},{7,6},{8,9},{9,8},{10,11... | collective-permute-start | bytes 221192 | tf_op jit(solution)/shard_map/ppermute | solution.py:239
  60.3 2.3 %collective-permute-start.29 = (bf16[24,1536]{1,0:T(8,128)(2,1)S(1)}, bf16[24,1536]{1,0:T(8,128)(2,1)S(1)}, u32[]{:S(2)}, u32[]{:S(2)}) collective-permute-start(bf16[24,1536]{1,0:T(8,128)(2,1)S(1)} %get-tuple-element.48), channel_id=1, source_target_pairs={{0,3},{1,2},{2,1},{3,0},{4,7},{5,6},{6,5},{7,4},{8,11},{9,10},{10,... | collective-permute-start | bytes 221192 | tf_op jit(solution)/shard_map/ppermute | solution.py:239
  62.6 1.5 %collective-permute-done.27.refs_1_ = bf16[24,1536]{1,0:T(8,128)(2,1)S(1)} collective-permute-done((bf16[24,1536]{1,0:T(8,128)(2,1)S(1)}, bf16[24,1536]{1,0:T(8,128)(2,1)S(1)}, u32[]{:S(2)}, u32[]{:S(2)}) %collective-permute-start.27) | collective-permute-done | bytes 73760 | tf_op jit(solution)/shard_map/ppermute | solution.py:239
  64.2 2.8 %collective-permute-done.28.refs_2_ = bf16[24,1536]{1,0:T(8,128)(2,1)S(1)} collective-permute-done((bf16[24,1536]{1,0:T(8,128)(2,1)S(1)}, bf16[24,1536]{1,0:T(8,128)(2,1)S(1)}, u32[]{:S(2)}, u32[]{:S(2)}) %collective-permute-start.28) | collective-permute-done | bytes 73760 | tf_op jit(solution)/shard_map/ppermute | solution.py:239
  67.1 7.6 %all_to_all.10.arrived_ref = bf16[8,24,192]{2,1,0:T(8,128)(2,1)S(1)} all-to-all(bf16[8,24,192]{2,1,0:T(8,128)(2,1)S(1)} %shard_map.134), channel_id=1, replica_groups=mesh['seq'=8,'req'=4] {'seq'}, dimensions={0} | all-to-all | bytes 147456 | tf_op jit(solution)/shard_map/all_to_all | solution.py:660
  (72 shorter events, 16.7 us)
Async XLA Ops:
  0.0 57.3 %all-to-all-start = ((bf16[4,512,384]{2,1,0:T(8,128)(2,1)}), bf16[4,512,384]{2,1,0:T(8,128)(2,1)S(1)}, u32[]{:S(2)}, u32[]{:S(2)}) async-start(bf16[4,512,384]{2,1,0:T(8,128)(2,1)} %param.25), calls=%async_computation | async-start | bytes 3145728 | tf_op jit(solution)/shard_map/all_to_all | solution.py:601
  7.8 4.0 %collective-permute-start = (bf16[5,24,128]{2,1,0:T(8,128)(2,1)S(1)}, bf16[5,24,128]{2,1,0:T(8,128)(2,1)S(1)}, u32[]{:S(2)}, u32[]{:S(2)}) collective-permute-start(bf16[5,24,128]{2,1,0:T(8,128)(2,1)S(1)} %get-tuple-element.27.refs_0_), channel_id=1, source_target_pairs={{0,8},{4,12},{8,0},{12,4},{16,24},{20,28},{24,16},{28,20},{1,9},{5... | collective-permute-start | bytes 92168 | tf_op jit(solution)/shard_map/ppermute | solution.py:239
  9.4 3.9 %collective-permute-start.1 = (bf16[5,24,128]{2,1,0:T(8,128)(2,1)S(1)}, bf16[5,24,128]{2,1,0:T(8,128)(2,1)S(1)}, u32[]{:S(2)}, u32[]{:S(2)}) collective-permute-start(bf16[5,24,128]{2,1,0:T(8,128)(2,1)S(1)} %get-tuple-element.27.refs_0_), channel_id=1, source_target_pairs={{0,16},{4,20},{8,24},{12,28},{16,0},{20,4},{24,8},{28,12},{1,17},{... | collective-permute-start | bytes 92168 | tf_op jit(solution)/shard_map/ppermute | solution.py:239
  10.9 4.8 %collective-permute-start.2 = (bf16[5,24,128]{2,1,0:T(8,128)(2,1)S(1)}, bf16[5,24,128]{2,1,0:T(8,128)(2,1)S(1)}, u32[]{:S(2)}, u32[]{:S(2)}) collective-permute-start(bf16[5,24,128]{2,1,0:T(8,128)(2,1)S(1)} %get-tuple-element.27.refs_0_), channel_id=1, source_target_pairs={{0,24},{4,28},{8,16},{12,20},{16,8},{20,12},{24,0},{28,4},{1,25},{... | collective-permute-start | bytes 92168 | tf_op jit(solution)/shard_map/ppermute | solution.py:239
  11.4 4.3 %collective-permute-start.3 = (bf16[5,24,128]{2,1,0:T(8,128)(2,1)S(1)}, bf16[5,24,128]{2,1,0:T(8,128)(2,1)S(1)}, u32[]{:S(2)}, u32[]{:S(2)}) collective-permute-start(bf16[5,24,128]{2,1,0:T(8,128)(2,1)S(1)} %get-tuple-element.27.refs_0_), channel_id=1, source_target_pairs={{0,4},{4,0},{8,12},{12,8},{16,20},{20,16},{24,28},{28,24},{1,5},{5... | collective-permute-start | bytes 92168 | tf_op jit(solution)/shard_map/ppermute | solution.py:239
  11.8 3.9 %collective-permute-start.4 = (bf16[5,24,128]{2,1,0:T(8,128)(2,1)S(1)}, bf16[5,24,128]{2,1,0:T(8,128)(2,1)S(1)}, u32[]{:S(2)}, u32[]{:S(2)}) collective-permute-start(bf16[5,24,128]{2,1,0:T(8,128)(2,1)S(1)} %collective-permute-done.refs_1_), channel_id=1, source_target_pairs={{0,4},{4,0},{8,12},{12,8},{16,20},{20,16},{24,28},{28,24},{1,5},{5... | collective-permute-start | bytes 92168 | tf_op jit(solution)/shard_map/ppermute | solution.py:239
  18.0 5.4 %collective-permute-start.7 = (bf16[72,640]{1,0:T(8,128)(2,1)S(1)}, bf16[72,640]{1,0:T(8,128)(2,1)S(1)}, u32[]{:S(2)}, u32[]{:S(2)}) collective-permute-start(bf16[72,640]{1,0:T(8,128)(2,1)S(1)} %shard_map.128.refs_0_), channel_id=1, source_target_pairs={{0,8},{4,12},{8,0},{12,4},{16,24},{20,28},{24,16},{28,20},{1,9},{5... | collective-permute-start | bytes 276488 | tf_op jit(solution)/shard_map/ppermute | solution.py:239
  18.6 6.5 %collective-permute-start.8 = (bf16[72,640]{1,0:T(8,128)(2,1)S(1)}, bf16[72,640]{1,0:T(8,128)(2,1)S(1)}, u32[]{:S(2)}, u32[]{:S(2)}) collective-permute-start(bf16[72,640]{1,0:T(8,128)(2,1)S(1)} %shard_map.128.refs_0_), channel_id=1, source_target_pairs={{0,16},{4,20},{8,24},{12,28},{16,0},{20,4},{24,8},{28,12},{1,17},{... | collective-permute-start | bytes 276488 | tf_op jit(solution)/shard_map/ppermute | solution.py:239
  19.1 6.0 %collective-permute-start.9 = (bf16[72,640]{1,0:T(8,128)(2,1)S(1)}, bf16[72,640]{1,0:T(8,128)(2,1)S(1)}, u32[]{:S(2)}, u32[]{:S(2)}) collective-permute-start(bf16[72,640]{1,0:T(8,128)(2,1)S(1)} %shard_map.128.refs_0_), channel_id=1, source_target_pairs={{0,24},{4,28},{8,16},{12,20},{16,8},{20,12},{24,0},{28,4},{1,25},{... | collective-permute-start | bytes 276488 | tf_op jit(solution)/shard_map/ppermute | solution.py:239
  21.5 4.1 %collective-permute-start.10 = (bf16[72,640]{1,0:T(8,128)(2,1)S(1)}, bf16[72,640]{1,0:T(8,128)(2,1)S(1)}, u32[]{:S(2)}, u32[]{:S(2)}) collective-permute-start(bf16[72,640]{1,0:T(8,128)(2,1)S(1)} %shard_map.128.refs_0_), channel_id=1, source_target_pairs={{0,4},{4,0},{8,12},{12,8},{16,20},{20,16},{24,28},{28,24},{1,5},{5... | collective-permute-start | bytes 276488 | tf_op jit(solution)/shard_map/ppermute | solution.py:239
  28.3 3.9 %collective-permute-start.14 = (f32[24,192]{1,0:T(8,128)S(1)}, f32[24,192]{1,0:T(8,128)S(1)}, u32[]{:S(2)}, u32[]{:S(2)}) collective-permute-start(f32[24,192]{1,0:T(8,128)S(1)} %get-tuple-element.32.refs_0_), channel_id=1, source_target_pairs={{0,8},{4,12},{8,0},{12,4},{16,24},{20,28},{24,16},{28,20},{1,9},{5... | collective-permute-start | bytes 55304 | tf_op jit(solution)/shard_map/ppermute | solution.py:239
  29.9 3.8 %collective-permute-start.15 = (f32[24,192]{1,0:T(8,128)S(1)}, f32[24,192]{1,0:T(8,128)S(1)}, u32[]{:S(2)}, u32[]{:S(2)}) collective-permute-start(f32[24,192]{1,0:T(8,128)S(1)} %get-tuple-element.32.refs_0_), channel_id=1, source_target_pairs={{0,16},{4,20},{8,24},{12,28},{16,0},{20,4},{24,8},{28,12},{1,17},{... | collective-permute-start | bytes 55304 | tf_op jit(solution)/shard_map/ppermute | solution.py:239
  30.7 4.7 %collective-permute-start.16 = (f32[24,192]{1,0:T(8,128)S(1)}, f32[24,192]{1,0:T(8,128)S(1)}, u32[]{:S(2)}, u32[]{:S(2)}) collective-permute-start(f32[24,192]{1,0:T(8,128)S(1)} %get-tuple-element.32.refs_0_), channel_id=1, source_target_pairs={{0,24},{4,28},{8,16},{12,20},{16,8},{20,12},{24,0},{28,4},{1,25},{... | collective-permute-start | bytes 55304 | tf_op jit(solution)/shard_map/ppermute | solution.py:239
  31.9 3.5 %collective-permute-start.17 = (f32[24,192]{1,0:T(8,128)S(1)}, f32[24,192]{1,0:T(8,128)S(1)}, u32[]{:S(2)}, u32[]{:S(2)}) collective-permute-start(f32[24,192]{1,0:T(8,128)S(1)} %get-tuple-element.32.refs_0_), channel_id=1, source_target_pairs={{0,4},{4,0},{8,12},{12,8},{16,20},{20,16},{24,28},{28,24},{1,5},{5... | collective-permute-start | bytes 55304 | tf_op jit(solution)/shard_map/ppermute | solution.py:239
  32.2 3.2 %collective-permute-start.18 = (f32[24,192]{1,0:T(8,128)S(1)}, f32[24,192]{1,0:T(8,128)S(1)}, u32[]{:S(2)}, u32[]{:S(2)}) collective-permute-start(f32[24,192]{1,0:T(8,128)S(1)} %collective-permute-done.14.refs_1_), channel_id=1, source_target_pairs={{0,4},{4,0},{8,12},{12,8},{16,20},{20,16},{24,28},{28,24},{1,5},{5... | collective-permute-start | bytes 55304 | tf_op jit(solution)/shard_map/ppermute | solution.py:239
  36.8 6.5 %collective-permute-start.21 = (bf16[24,512]{1,0:T(8,128)(2,1)S(1)}, bf16[24,512]{1,0:T(8,128)(2,1)S(1)}, u32[]{:S(2)}, u32[]{:S(2)}) collective-permute-start(bf16[24,512]{1,0:T(8,128)(2,1)S(1)} %get-tuple-element.36), channel_id=1, source_target_pairs={{0,1},{1,0},{2,3},{3,2},{4,5},{5,4},{6,7},{7,6},{8,9},{9,8},{10,11... | collective-permute-start | bytes 73736 | tf_op jit(solution)/shard_map/ppermute | solution.py:239
  38.9 5.9 %collective-permute-start.22 = (bf16[24,512]{1,0:T(8,128)(2,1)S(1)}, bf16[24,512]{1,0:T(8,128)(2,1)S(1)}, u32[]{:S(2)}, u32[]{:S(2)}) collective-permute-start(bf16[24,512]{1,0:T(8,128)(2,1)S(1)} %get-tuple-element.37), channel_id=1, source_target_pairs={{0,2},{1,3},{2,0},{3,1},{4,6},{5,7},{6,4},{7,5},{8,10},{9,11},{10,... | collective-permute-start | bytes 73736 | tf_op jit(solution)/shard_map/ppermute | solution.py:239
  41.3 5.6 %collective-permute-start.23 = (bf16[24,512]{1,0:T(8,128)(2,1)S(1)}, bf16[24,512]{1,0:T(8,128)(2,1)S(1)}, u32[]{:S(2)}, u32[]{:S(2)}) collective-permute-start(bf16[24,512]{1,0:T(8,128)(2,1)S(1)} %get-tuple-element.38), channel_id=1, source_target_pairs={{0,3},{1,2},{2,1},{3,0},{4,7},{5,6},{6,5},{7,4},{8,11},{9,10},{10,... | collective-permute-start | bytes 73736 | tf_op jit(solution)/shard_map/ppermute | solution.py:239
  47.8 6.0 %collective-permute-start.24 = (bf16[48,1024]{1,0:T(8,128)(2,1)S(1)}, bf16[48,1024]{1,0:T(8,128)(2,1)S(1)}, u32[]{:S(2)}, u32[]{:S(2)}) collective-permute-start(bf16[48,1024]{1,0:T(8,128)(2,1)S(1)} %get-tuple-element.40), channel_id=1, source_target_pairs={{0,1},{1,0},{2,3},{3,2},{4,5},{5,4},{6,7},{7,6},{8,9},{9,8},{10,11... | collective-permute-start | bytes 294920 | tf_op jit(solution)/shard_map/ppermute | solution.py:239
  47.9 9.4 %collective-permute-start.25 = (bf16[48,1024]{1,0:T(8,128)(2,1)S(1)}, bf16[48,1024]{1,0:T(8,128)(2,1)S(1)}, u32[]{:S(2)}, u32[]{:S(2)}) collective-permute-start(bf16[48,1024]{1,0:T(8,128)(2,1)S(1)} %get-tuple-element.41), channel_id=1, source_target_pairs={{0,2},{1,3},{2,0},{3,1},{4,6},{5,7},{6,4},{7,5},{8,10},{9,11},{10,... | collective-permute-start | bytes 294920 | tf_op jit(solution)/shard_map/ppermute | solution.py:239
  48.7 8.6 %collective-permute-start.26 = (bf16[48,1024]{1,0:T(8,128)(2,1)S(1)}, bf16[48,1024]{1,0:T(8,128)(2,1)S(1)}, u32[]{:S(2)}, u32[]{:S(2)}) collective-permute-start(bf16[48,1024]{1,0:T(8,128)(2,1)S(1)} %get-tuple-element.42), channel_id=1, source_target_pairs={{0,3},{1,2},{2,1},{3,0},{4,7},{5,6},{6,5},{7,4},{8,11},{9,10},{10,... | collective-permute-start | bytes 294920 | tf_op jit(solution)/shard_map/ppermute | solution.py:239
  58.2 6.0 %collective-permute-start.27 = (bf16[24,1536]{1,0:T(8,128)(2,1)S(1)}, bf16[24,1536]{1,0:T(8,128)(2,1)S(1)}, u32[]{:S(2)}, u32[]{:S(2)}) collective-permute-start(bf16[24,1536]{1,0:T(8,128)(2,1)S(1)} %get-tuple-element.46), channel_id=1, source_target_pairs={{0,1},{1,0},{2,3},{3,2},{4,5},{5,4},{6,7},{7,6},{8,9},{9,8},{10,11... | collective-permute-start | bytes 221192 | tf_op jit(solution)/shard_map/ppermute | solution.py:239
  59.9 7.1 %collective-permute-start.28 = (bf16[24,1536]{1,0:T(8,128)(2,1)S(1)}, bf16[24,1536]{1,0:T(8,128)(2,1)S(1)}, u32[]{:S(2)}, u32[]{:S(2)}) collective-permute-start(bf16[24,1536]{1,0:T(8,128)(2,1)S(1)} %get-tuple-element.47), channel_id=1, source_target_pairs={{0,2},{1,3},{2,0},{3,1},{4,6},{5,7},{6,4},{7,5},{8,10},{9,11},{10,... | collective-permute-start | bytes 221192 | tf_op jit(solution)/shard_map/ppermute | solution.py:239
  60.3 6.7 %collective-permute-start.29 = (bf16[24,1536]{1,0:T(8,128)(2,1)S(1)}, bf16[24,1536]{1,0:T(8,128)(2,1)S(1)}, u32[]{:S(2)}, u32[]{:S(2)}) collective-permute-start(bf16[24,1536]{1,0:T(8,128)(2,1)S(1)} %get-tuple-element.48), channel_id=1, source_target_pairs={{0,3},{1,2},{2,1},{3,0},{4,7},{5,6},{6,5},{7,4},{8,11},{9,10},{10,... | collective-permute-start | bytes 221192 | tf_op jit(solution)/shard_map/ppermute | solution.py:239
  (19 other events, 114.6 us)

commit v4 on v3

--- a/solution.py
+++ b/solution.py
@@ -198,7 +198,7 @@
 STAT = 128
 WIDE = KVD + STAT
 VMEM = pl.BlockSpec(memory_space=pltpu.VMEM)
-SMEM = pl.BlockSpec(memory_space=pltpu.SMEM)
+HBM = pl.BlockSpec(memory_space=pltpu.HBM)
 
 
 def kernel_call(body, out_shape, in_specs, scratch=(), out_specs=None, vmem_mib=8, cost=0.5):
@@ -244,11 +244,30 @@
 
 
 def project_kernel(*refs):
-    x_in, attn_gain, moe_gain, w_in, lengths, pages, routes, weights = refs[:8]
-    heads_ref, x_ref, live_ref, routing_ref, gain_ref = refs[8:]
+    x_hbm, attn_hbm, moe_hbm, w_hbm, lengths_hbm, pages_hbm, routes_hbm, weights_hbm = refs[:8]
+    heads_ref, x_ref, live_ref, routing_ref, gain_ref = refs[8:13]
+    x_in, attn_gain, moe_gain, w_in, lengths, pages, routes, weights, sem = refs[13:]
+    loads = [
+        pltpu.make_async_copy(source, target, sem.at[i])
+        for i, (source, target) in enumerate(
+            [
+                (lengths_hbm, lengths),
+                (x_hbm, x_in),
+                (attn_hbm, attn_gain),
+                (w_hbm, w_in),
+                (pages_hbm, pages),
+                (routes_hbm, routes),
+                (weights_hbm, weights),
+                (moe_hbm, moe_gain),
+            ]
+        )
+    ]
+    for load in loads:
+        load.start()
     requests = x_in.shape[0]
     row_count = requests * NSTEP
     shape = (row_count, STAT)
+    loads[0].wait()
     row, lane = iota(shape, 0), iota(shape, 1)
     position = row % NSTEP
     for r in range(requests):
@@ -257,10 +276,13 @@
     angle = position.astype(F32) * rates
     cosine = jnp.cos(angle)
     sine = jnp.where(lane % HD < HD // 2, -jnp.sin(angle), jnp.sin(angle))
+    loads[1].wait()
     x = rows_of(x_in)
     x_ref[...] = x
     power = jnp.mean(x * x, axis=-1, keepdims=True)
+    loads[2].wait()
     normed = (x * lax.rsqrt(power + EPS) * attn_gain[...].reshape(1, D)).astype(BF16)
+    loads[3].wait()
     projected = dot_nt(normed, w_in[...])
     heads = w_in.shape[0] // HD
     first = lax.axis_index("seq") * heads
@@ -269,6 +291,8 @@
         both = jnp.concatenate([one, one], axis=1)
         turned = both * cosine + pltpu.roll(both, HD // 2, 1) * sine
         heads_ref[i] = jnp.where(first + i < HEADS + KVH, turned, both).astype(BF16)
+    for load in loads[4:]:
+        load.wait()
     slots = live_ref.shape[1]
     slot = iota((1, slots), 1)
     for r in range(requests):
@@ -282,6 +306,13 @@
         [rows_of(routes), high, middle, low, jnp.zeros((row_count, STAT - 4 * TOP), F32)], axis=1
     )
     gain_ref[...] = moe_gain[...].reshape(1, D)
+
+
+def in_chip_order(near, far):
+    first = lax.axis_index("seq") % 2 == 0
+    return jnp.where(
+        first, jnp.concatenate([near, far], axis=1), jnp.concatenate([far, near], axis=1)
+    )
 
 
 def gather_pieces(near_refs, far_refs, all_ref):
@@ -395,7 +426,7 @@
 
 def merge_kernel(count, *refs):
     part_refs = refs[:count]
-    x_ref, w_ref, share_ref, resid_ref = refs[count:]
+    x_ref, gain_ref, routing_ref, near_w, far_w, out_ref, resid_ref = refs[count:]
     parts = [ref[...].astype(F32) for ref in part_refs]
     tops, totals = [], []
     for part in parts:
@@ -434,30 +465,18 @@
     attended = jnp.concatenate(
         [jnp.where(left, head(2 * n, 0), head(2 * n + 1, 1)) for n in range(HEADS // 2)], axis=1
     ).astype(BF16)
-    share = dot_nt(attended, w_ref[...])
-    share_ref[...] = share
-    width = w_ref.shape[0]
+    share = in_chip_order(dot_nt(attended, near_w[...]), dot_nt(attended, far_w[...]))
+    width = near_w.shape[0]
     member = lax.axis_index("seq")
-    chunk = x_ref[:, pl.ds(pl.multiple_of((member // 2) * (2 * width), STAT), 2 * width)]
-    resid_ref[...] = share + jnp.where(member % 2 == 0, chunk[:, :width], chunk[:, width:])
-
-
-def mix_kernel(chips, groups, *refs):
-    near_refs, far_refs = refs[:chips], refs[chips : 2 * chips]
-    x_ref, gain_ref, routing_ref = refs[2 * chips : 2 * chips + 3]
-    pack_refs, all_ref, mixed_ref = refs[2 * chips + 3 : -2], refs[-2], refs[-1]
-    gather_pieces(near_refs, far_refs, all_ref)
-    chip = lax.axis_index("seq") // 2
-    attn = jnp.concatenate([all_ref[s % 2, chip ^ (s // 2)] for s in range(2 * chips)], axis=1)
-    resid = x_ref[...] + attn
-    power = jnp.mean(resid * resid, axis=-1, keepdims=True)
-    mixed_ref[...] = resid * lax.rsqrt(power + EPS) * gain_ref[...]
-    routing = routing_ref[...]
-    width = D // groups
-    for k in range(groups):
-        start = pl.multiple_of((lax.axis_index("req") ^ k) * width, STAT)
-        part = mixed_ref[:, pl.ds(start, width)]
-        pack_refs[k][...] = jnp.concatenate([part, routing], axis=1).astype(BF16)
+    both = pl.ds(pl.multiple_of((member // 2) * (2 * width), STAT), 2 * width)
+    resid = x_ref[:, both] + share
+    resid_ref[...] = jnp.where(member % 2 == 0, resid[:, :width], resid[:, width:])
+    stats = routing_ref[...]
+    lane = iota(stats.shape, 1)
+    for i, value in enumerate(split3(jnp.sum(resid * resid, axis=1, keepdims=True))):
+        stats = jnp.where(lane == 4 * TOP + i, value, stats)
+    out_ref[:, : 2 * width] = (resid * gain_ref[:, both]).astype(BF16)
+    out_ref[:, 2 * width :] = stats.astype(BF16)
 
 
 def across(column, eye):
@@ -465,18 +484,18 @@
 
 
 def gate_kernel(groups, *refs):
-    pack_refs = refs[:groups]
-    w_ref = refs[groups]
+    piece_refs, w_ref = refs[:groups], refs[groups]
     message_refs = refs[groups + 1 : 2 * groups + 1]
     placed_ref, scale_ref, full_ref = refs[2 * groups + 1 :]
-    first = lax.axis_index("seq") * w_ref.shape[0]
-    me = lax.axis_index("req")
-    packs = [ref[...].astype(F32) for ref in pack_refs]
-    row_count = packs[0].shape[0]
+    member, me = lax.axis_index("seq"), lax.axis_index("req")
+    width = w_ref.shape[1]
+    row_count = piece_refs[0].shape[0]
     tokens = groups * row_count
-    width = w_ref.shape[1]
-    mixed = jnp.concatenate([pack[:, :width] for pack in packs], axis=0).astype(BF16)
-    routing = jnp.concatenate([pack[:, width:] for pack in packs], axis=0)
+    pieces = jnp.concatenate([ref[...].astype(F32) for ref in piece_refs], axis=0)
+    mixed, routing = pieces[:, :width].astype(BF16), pieces[:, width:]
+    power = routing[:, 4 * TOP : 4 * TOP + 1] + (
+        routing[:, 4 * TOP + 1 : 4 * TOP + 2] + routing[:, 4 * TOP + 2 : 4 * TOP + 3]
+    )
     chosen = routing[:, :TOP]
     gates = routing[:, TOP : 2 * TOP] + (
         routing[:, 2 * TOP : 3 * TOP] + routing[:, 3 * TOP : 4 * TOP]
@@ -489,71 +508,83 @@
     )
     slots = groups * CAP
     shape = (slots, tokens)
-    home = (iota(shape, 1) // row_count) ^ me
+    home = (iota(shape, 1) // row_count) ^ (member // 2)
     slot = iota(shape, 0)
     same_group = slot // CAP == home
     ordinal_of_slot = (slot % CAP).astype(F32)
-    placed, scales = [], []
+    placed, scales, powers = [], [], []
+    power_row = across(power, eye)
     for e in range(experts):
-        match = chosen == (first + e).astype(F32)
+        match = chosen == (member * experts + e).astype(F32)
         routed = jnp.max(jnp.where(match, 1.0, 0.0), axis=1, keepdims=True)
         scale = jnp.sum(jnp.where(match, gates, 0.0), axis=1, keepdims=True)
         ordinal = across(routed, earlier)
         here = same_group & (across(routed, eye) > 0.5) & (ordinal_of_slot == ordinal)
         placed.append(jnp.where(here, 1.0, 0.0))
         scales.append(jnp.sum(jnp.where(here, across(scale, eye), 0.0), axis=1, keepdims=True))
+        powers.append(jnp.sum(jnp.where(here, power_row, 0.0), axis=1, keepdims=True))
+    lane = iota((slots, STAT), 1)
     all_placed = jnp.concatenate(placed, axis=0).astype(BF16)
     taken = jnp.dot(all_placed, mixed, preferred_element_type=F32).astype(BF16)
     for e in range(experts):
         rows = slice(e * slots, (e + 1) * slots)
         placed_ref[e] = all_placed[rows]
         scale_ref[e] = jnp.broadcast_to(scales[e], scale_ref.shape[1:])
-        full_ref[e] = jnp.dot(taken[rows], w_ref[e], preferred_element_type=F32).astype(BF16)
+        full_ref[e, :, : 2 * FFE] = jnp.dot(
+            taken[rows], w_ref[e], preferred_element_type=F32
+        ).astype(BF16)
+        high, middle, low = split3(powers[e])
+        full_ref[e, :, 2 * FFE :] = jnp.where(
+            lane == 0, high, jnp.where(lane == 1, middle, jnp.where(lane == 2, low, 0.0))
+        ).astype(BF16)
     for k in range(groups):
         message_refs[k][...] = full_ref[me ^ k]
 
 
+def hidden_kernel(*refs):
+    gate_up = refs[0][...].astype(F32)
+    for ref in refs[1:-1]:
+        gate_up = gate_up + ref[...].astype(F32)
+    power = gate_up[:, 2 * FFE : 2 * FFE + 1] + (
+        gate_up[:, 2 * FFE + 1 : 2 * FFE + 2] + gate_up[:, 2 * FFE + 2 : 2 * FFE + 3]
+    )
+    gate_up = gate_up[:, : 2 * FFE] * lax.rsqrt(power / D + EPS)
+    gate, up = gate_up[:, :FFE], gate_up[:, FFE:]
+    refs[-1][...] = (gate / (1.0 + jnp.exp(-gate)) * up).astype(BF16)
+
+
 def down_kernel(groups, *refs):
-    message_refs = refs[:groups]
-    down_ref, placed_ref, scale_ref = refs[groups : groups + 3]
-    out_refs = refs[groups + 3 :]
-    me = lax.axis_index("req")
-    gate_up = message_refs[0][...].astype(F32)
-    for ref in message_refs[1:]:
-        gate_up = gate_up + ref[...].astype(F32)
-    gate, up = gate_up[:, :FFE], gate_up[:, FFE:]
-    hidden = (gate / (1.0 + jnp.exp(-gate)) * up).astype(BF16)
-    placed, scale = placed_ref[me], scale_ref[me][:, :1]
-    width = down_ref.shape[2]
-    row_count = out_refs[0].shape[0]
-    for k in range(groups):
-        produced = jnp.dot(hidden, down_ref[k], preferred_element_type=F32)
-        total = lax.dot_general(
-            placed,
-            (produced * scale).astype(BF16),
+    hidden_refs = refs[:groups]
+    w_ref, placed_ref, scale_ref, send_ref, keep_ref = refs[groups:]
+    me, core = lax.axis_index("req"), lax.axis_index("seq") % 2
+    total = jnp.zeros((placed_ref.shape[2], w_ref.shape[2]), F32)
+    for k, hidden_ref in enumerate(hidden_refs):
+        expert = me ^ k
+        produced = jnp.dot(hidden_ref[...], w_ref[expert], preferred_element_type=F32)
+        total = total + lax.dot_general(
+            placed_ref[expert],
+            (produced * scale_ref[expert][:, :1]).astype(BF16),
             (((0,), (0,)), ((), ())),
             preferred_element_type=F32,
         )
-        for j in range(groups):
-            out_refs[j][:, k * width : (k + 1) * width] = total[
-                j * row_count : (j + 1) * row_count
-            ].astype(BF16)
-
-
-def spread_kernel(groups, *refs):
-    total = refs[0][...].astype(F32)
-    for ref in refs[1:groups]:
+    width = w_ref.shape[2] // 2
+    left, right = total[:, :width], total[:, width:]
+    send_ref[...] = jnp.where(core == 0, left, right).astype(BF16)
+    keep_ref[...] = jnp.where(core == 0, right, left)
+
+
+def spread_kernel(keep_ref, arrived_ref, *out_refs):
+    total = keep_ref[...] + arrived_ref[...].astype(F32)
+    row_count = out_refs[0].shape[0]
+    for k, out_ref in enumerate(out_refs):
+        out_ref[...] = total[k * row_count : (k + 1) * row_count].astype(BF16)
+
+
+def final_kernel(resid_ref, *refs):
+    arrived_refs, out_ref = refs[:-1], refs[-1]
+    total = resid_ref[...]
+    for ref in arrived_refs:
         total = total + ref[...].astype(F32)
-    out_ref = refs[groups]
-    width = out_ref.shape[2]
-    for s in range(out_ref.shape[0]):
-        out_ref[s] = total[:, s * width : (s + 1) * width].astype(BF16)
-
-
-def final_kernel(resid_ref, arrived_ref, out_ref):
-    total = resid_ref[...]
-    for s in range(arrived_ref.shape[0]):
-        total = total + arrived_ref[s].astype(F32)
     for r in range(out_ref.shape[0]):
         out_ref[r] = total[r * NSTEP : (r + 1) * NSTEP].astype(BF16)
 
@@ -589,8 +620,35 @@
             jax.ShapeDtypeStruct((row_count, STAT), F32),
             jax.ShapeDtypeStruct((1, D), F32),
         ],
-        [VMEM] * 4 + [SMEM] * 2 + [VMEM] * 2,
+        [HBM] * 8,
+        [
+            pltpu.VMEM(x_in.shape, BF16),
+            pltpu.VMEM((D,), F32),
+            pltpu.VMEM((D,), F32),
+            pltpu.VMEM((w_qkv.shape[1], D), BF16),
+            pltpu.SMEM(lengths.shape, jnp.int32),
+            pltpu.SMEM(page_map.shape, jnp.int32),
+            pltpu.VMEM(routes.shape, jnp.int32),
+            pltpu.VMEM(route_weights.shape, F32),
+            pltpu.SemaphoreType.DMA((8,)),
+        ],
+        vmem_mib=60,
+        cost=5.0,
     )(x_in, attn_gain, moe_gain, w_qkv.T, lengths, page_map, routes, route_weights)
+    def gathered(own, *first):
+        near = [swap(own, "seq", 2 * k) for k in range(chips - 1, 0, -1)]
+        near = [own] + near[::-1]
+        near[1] = after(near[1], *first) if first else near[1]
+        return near, [swap(piece, "seq", 1) for piece in near]
+
+    near, far = gathered(own_heads)
+    def gathered(own, *first):
+        near = [swap(own, "seq", 2 * k) for k in range(chips - 1, 0, -1)]
+        near = [own] + near[::-1]
+        near[1] = after(near[1], *first) if first else near[1]
+        return near, [swap(piece, "seq", 1) for piece in near]
+
+    near, far = gathered(own_heads)
     def gathered(own, *first):
         near = [swap(own, "seq", 2 * k) for k in range(chips - 1, 0, -1)]
         near = [own] + near[::-1]
@@ -619,56 +677,70 @@
         cost=0.5,
     )(*near, *far)
     near, far = gathered(part, fresh)
-    share, resid = kernel_call(
+    packed, resid = kernel_call(
         lambda *refs: merge_kernel(members + 1, *refs),
-        [jax.ShapeDtypeStruct((row_count, width), F32)] * 2,
-        [VMEM] * (members + 3),
-    )(*near, *far, fresh, x, w_o.T)
-    near, far = gathered(share)
-    packs = kernel_call(
-        lambda *refs: mix_kernel(chips, groups, *refs),
-        [jax.ShapeDtypeStruct((row_count, 2 * width + STAT), BF16)] * groups,
-        [VMEM] * (2 * chips + 3),
-        [pltpu.VMEM((2, chips, row_count, width), F32), pltpu.VMEM((row_count, D), F32)],
-    )(*near, *far, x, gain, routing)
-
-    def exchanged(pieces):
-        return [pieces[0]] + [swap(pieces[k], "req", k) for k in range(1, groups)]
-
+        [
+            jax.ShapeDtypeStruct((row_count, 2 * width + STAT), BF16),
+            jax.ShapeDtypeStruct((row_count, width), F32),
+        ],
+        [VMEM] * (members + 6),
+    )(*near, *far, fresh, x, gain, routing, w_o.T, swap(w_o.T, "seq", 1))
+
+    def crossing(mask):
+        return [
+            ((2 * p + c) * groups + q, (2 * (q ^ mask) + 1 - c) * groups + p)
+            for p in range(chips)
+            for c in range(2)
+            for q in range(groups)
+        ]
+
+    place = ("seq", "req")
+    pieces = [lax.ppermute(packed, place, crossing(k)) for k in range(groups)]
     experts = w_gate_up.shape[0]
     slots = groups * CAP
     *messages, placed, scale = kernel_call(
         lambda *refs: gate_kernel(groups, *refs),
-        [jax.ShapeDtypeStruct((slots, 2 * FFE), BF16)] * groups
+        [jax.ShapeDtypeStruct((slots, 2 * FFE + STAT), BF16)] * groups
         + [
             jax.ShapeDtypeStruct((experts, slots, groups * row_count), BF16),
             jax.ShapeDtypeStruct((experts, slots, STAT), F32),
         ],
         [VMEM] * (groups + 1),
-        [pltpu.VMEM((experts, slots, 2 * FFE), BF16)],
-    )(*exchanged(packs), w_gate_up)
+        [pltpu.VMEM((experts, slots, 2 * FFE + STAT), BF16)],
+    )(*pieces, w_gate_up)
+    sums = [messages[0]] + [swap(messages[k], "req", k) for k in (3, 1, 2)]
+    hidden = kernel_call(
+        hidden_kernel, jax.ShapeDtypeStruct((slots, FFE), BF16), [VMEM] * groups
+    )(*sums)
+    hiddens = [hidden] + [swap(hidden, "req", k) for k in range(1, groups)]
+    send, keep = kernel_call(
+        lambda *refs: down_kernel(groups, *refs),
+        [
+            jax.ShapeDtypeStruct((groups * row_count, width), BF16),
+            jax.ShapeDtypeStruct((groups * row_count, width), F32),
+        ],
+        [VMEM] * (groups + 3),
+    )(*hiddens, w_down, placed, scale)
     outs = kernel_call(
-        lambda *refs: down_kernel(groups, *refs),
-        [jax.ShapeDtypeStruct((row_count, D), BF16)] * groups,
-        [VMEM] * (groups + 3),
-    )(*exchanged(messages), down, placed, scale)
-    spread = kernel_call(
-        lambda *refs: spread_kernel(groups, *refs),
-        jax.ShapeDtypeStruct((members, row_count, width), BF16),
-        [VMEM] * groups,
-    )(*exchanged(outs))
-    arrived = lax.all_to_all(spread, "seq", 0, 0, tiled=True)
+        spread_kernel, [jax.ShapeDtypeStruct((row_count, width), BF16)] * groups, [VMEM] * 2
+    )(keep, swap(send, "seq", 1))
+    arrived = [
+        lax.ppermute(out, place, [(target, source) for source, target in crossing(k)])
+        for k, out in enumerate(outs)
+    ]
     return kernel_call(
-        final_kernel, jax.ShapeDtypeStruct((requests, NSTEP, width), BF16), [VMEM] * 2
-    )(resid, arrived)
+        final_kernel,
+        jax.ShapeDtypeStruct((requests, NSTEP, width), BF16),
+        [VMEM] * (groups + 1),
+    )(resid, *arrived)
 
 
 def local(*args):
     w_qkv, w_o, w_gate_up = args[3], args[4], args[11]
     members, groups = lax.axis_size("seq"), lax.axis_size("req")
     fits = (
-        members == 2 * groups
-        and groups & (groups - 1) == 0
+        members == 8
+        and groups == 4
         and w_qkv.shape[1] % HD == 0
         and w_gate_up.shape[0] == groups
         and (2 * w_o.shape[1]) % STAT == 0

time: 75.5 us -> 73 us (0.967)
  blocking collectives: 7.58 us -> 0 us
  local copies, waits for them, and re-layouts: 0.05 us -> 2.36 us
  waiting for transfers between devices: 28.3 us -> 30.5 us
  starting transfers between devices: 31.4 us -> 29.6 us
  Pallas kernels: 7.84 us -> 9.55 us
    ppermute x0 -> x8, starting transfers between devices: none -> 9.15 us  [the longest x4 4.68 us: staged(): lax.ppermute(out, place, [(target, source) for source, target in crossing...]
    all_to_all x1 -> x0, blocking collectives: 7.58 us -> none  [staged(): arrived = lax.all_to_all(spread, 'seq', 0, 0, tiled=True)]
    ppermute x0 -> x8, waiting for transfers between devices: none -> 6.53 us  [the longest x4 3.48 us: staged(): pieces = [lax.ppermute(packed, place, crossing(k)) for k in range(groups)]]
    all_to_all x1 -> x0, starting transfers between devices: 6.48 us -> none  [staged(): down = lax.all_to_all(w_down, 'req', 0, 0, tiled=True)]
    ppermute x30 -> x22, starting transfers between devices: 24.9 us -> 20.4 us  [swap(): return lax.ppermute(value, axis, pairs)]
    ppermute x30 -> x22, waiting for transfers between devices: 28.2 us -> 23.9 us  [swap(): return lax.ppermute(value, axis, pairs)]
    unnamed x24 -> x20, local copies, waits for them, and re-layouts: 0.05 us -> 2.36 us
    pallas_call x1, Pallas kernels: 1.21 us -> 2.69 us  [staged(): kernel_call(project_kernel, [jax.ShapeDtypeStruct((heads, row_count, 2 *...]
  transfers between devices with their start and end apart: 31 -> 30, of which waited for: 19 -> 20; matrix products, arithmetic and copies ran while one was open for 0% -> 0% of each run, Pallas kernels for 8% -> 7%
where the time goes in v4:
time: 73 us; the launch traced here: 72.1 us
  waiting for transfers between devices  30.5 us (42%)
  starting transfers between devices  29.6 us (41%)
  Pallas kernels  9.55 us (13%)
  local copies, waits for them, and re-layouts  2.36 us (3%)
    ppermute x22, waiting for transfers between devices, swap(): return lax.ppermute(value, axis, pairs)  23.9 us
    ppermute x22, starting transfers between devices, swap(): return lax.ppermute(value, axis, pairs)  20.4 us
    ppermute x4, starting transfers between devices, staged(): lax.ppermute(out, place, [(target, source) for source, target in crossing...  4.68 us
    ppermute x4, starting transfers between devices, staged(): pieces = [lax.ppermute(packed, place, crossing(k)) for k in range(groups)]  4.47 us
    ppermute x4, waiting for transfers between devices, staged(): pieces = [lax.ppermute(packed, place, crossing(k)) for k in range(groups)]  3.48 us
    ppermute x4, waiting for transfers between devices, staged(): lax.ppermute(out, place, [(target, source) for source, target in crossing...  3.05 us
    pallas_call x1, Pallas kernels, staged(): kernel_call(project_kernel, [jax.ShapeDtypeStruct((heads, row_count, 2 *...  2.69 us
    unnamed x20, local copies, waits for them, and re-layouts  2.36 us
  transfers between devices with their start and end apart: 30, of which 20 were waited for; matrix products, arithmetic and copies ran while one was open for 0% of the time, Pallas kernels for 7%

profile of v4, /device:TPU:0, one launch (start us, length us, event | category | flops | bytes accessed | tf_op | source)
XLA Modules:
  0.0 72.1 jit_solution(16429665163263337551)
XLA Ops:
  0.5 2.7 %shard_map.127 = (bf16[5,24,128]{2,1,0:T(8,128)(2,1)}, f32[24,1536]{1,0:T(8,128)}, f32[6,128]{1,0:T(8,128)}, f32[24,128]{1,0:T(8,128)}, f32[1,1536]{1,0:T(1,128)}) custom-call(bf16[6,4,1536]{2,1,0:T(4,128)(2,1)} %refs_0_.1, f32[1536]{0:T(1024)} %refs_1_.1, f32[1536]{0:T(1024)} %refs_2_.1, bf16[320,1536]{1,0:T(8,128)(2,1)} %bitcast.4, s32[6]{0:T(128)} %refs_4_.3, ...), custom_call_target="tpu_custom_call" | custom-call | flops 5000000000 | bytes 15000000 | tf_op jit(solution)/shard_map/pallas_call | solution.py:614
  3.2 3.5 %collective-permute-start.2 = (bf16[5,24,128]{2,1,0:T(8,128)(2,1)}, bf16[5,24,128]{2,1,0:T(8,128)(2,1)S(1)}, u32[]{:S(2)}, u32[]{:S(2)}) collective-permute-start(bf16[5,24,128]{2,1,0:T(8,128)(2,1)} %get-tuple-element.25.refs_0_), channel_id=1, source_target_pairs={{0,24},{4,28},{8,16},{12,20},{16,8},{20,12},{24,0},{28,4},{1,25},{... | collective-permute-start | bytes 92168 | tf_op jit(solution)/shard_map/ppermute | solution.py:239
  7.3 1.6 %collective-permute-done.2.refs_3_ = bf16[5,24,128]{2,1,0:T(8,128)(2,1)S(1)} collective-permute-done((bf16[5,24,128]{2,1,0:T(8,128)(2,1)}, bf16[5,24,128]{2,1,0:T(8,128)(2,1)S(1)}, u32[]{:S(2)}, u32[]{:S(2)}) %collective-permute-start.2) | collective-permute-done | bytes 30752 | tf_op jit(solution)/shard_map/ppermute | solution.py:239
  8.9 1.9 %collective-permute-done.1.refs_2_ = bf16[5,24,128]{2,1,0:T(8,128)(2,1)S(1)} collective-permute-done((bf16[5,24,128]{2,1,0:T(8,128)(2,1)}, bf16[5,24,128]{2,1,0:T(8,128)(2,1)S(1)}, u32[]{:S(2)}, u32[]{:S(2)}) %collective-permute-start.1) | collective-permute-done | bytes 30752 | tf_op jit(solution)/shard_map/ppermute | solution.py:239
  15.3 2.8 %collective-permute-start.9 = (bf16[72,640]{1,0:T(8,128)(2,1)S(1)}, bf16[72,640]{1,0:T(8,128)(2,1)S(1)}, u32[]{:S(2)}, u32[]{:S(2)}) collective-permute-start(bf16[72,640]{1,0:T(8,128)(2,1)S(1)} %shard_map.128.refs_0_), channel_id=1, source_target_pairs={{0,24},{4,28},{8,16},{12,20},{16,8},{20,12},{24,0},{28,4},{1,25},{... | collective-permute-start | bytes 276488 | tf_op jit(solution)/shard_map/ppermute | solution.py:239
  18.6 1.1 %shard_map.129.refs_8_ = bf16[72,640]{1,0:T(8,128)(2,1)S(1)} custom-call(bf16[5,24,128]{2,1,0:T(8,128)(2,1)S(1)} %copy-done.6, bf16[5,24,128]{2,1,0:T(8,128)(2,1)S(1)} %collective-permute-done.refs_1_, bf16[5,24,128]{2,1,0:T(8,128)(2,1)S(1)} %collective-permute-done.1.refs_2_, bf16[5,24,128]{2,1,0:T(8,128)(2,1)S(1)} %collective-permute-done.2.refs_3_, ...), custom_call_target="tpu_custom_call" | custom-call | flops 500000000 | bytes 1500000 | tf_op jit(solution)/shard_map/pallas_call | solution.py:672
  20.6 2.3 %collective-permute-done.9.refs_3_ = bf16[72,640]{1,0:T(8,128)(2,1)S(1)} collective-permute-done((bf16[72,640]{1,0:T(8,128)(2,1)S(1)}, bf16[72,640]{1,0:T(8,128)(2,1)S(1)}, u32[]{:S(2)}, u32[]{:S(2)}) %collective-permute-start.9) | collective-permute-done | bytes 92192 | tf_op jit(solution)/shard_map/ppermute | solution.py:239
  22.8 1.2 %collective-permute-done.8.refs_2_ = bf16[72,640]{1,0:T(8,128)(2,1)S(1)} collective-permute-done((bf16[72,640]{1,0:T(8,128)(2,1)S(1)}, bf16[72,640]{1,0:T(8,128)(2,1)S(1)}, u32[]{:S(2)}, u32[]{:S(2)}) %collective-permute-start.8) | collective-permute-done | bytes 92192 | tf_op jit(solution)/shard_map/ppermute | solution.py:239
  26.4 1.9 %shard_map.130 = (bf16[24,512]{1,0:T(8,128)(2,1)S(1)}, f32[24,192]{1,0:T(8,128)S(1)}) custom-call(bf16[72,640]{1,0:T(8,128)(2,1)S(1)} %shard_map.128.refs_0_, bf16[72,640]{1,0:T(8,128)(2,1)S(1)} %collective-permute-done.7.refs_1_, bf16[72,640]{1,0:T(8,128)(2,1)S(1)} %collective-permute-done.8.refs_2_, bf16[72,640]{1,0:T(8,128)(2,1)S(1)} %collective-permute-done.9.refs_3_, ...), custom_call_target="tpu_custom_call" | custom-call | flops 500000000 | bytes 1500000 | tf_op jit(solution)/shard_map/pallas_call | solution.py:680
  28.9 2.5 %collective-permute-start.17 = (bf16[24,512]{1,0:T(8,128)(2,1)S(1)}, bf16[24,512]{1,0:T(8,128)(2,1)S(1)}, u32[]{:S(2)}, u32[]{:S(2)}) collective-permute-start(bf16[24,512]{1,0:T(8,128)(2,1)S(1)} %get-tuple-element.32), channel_id=1, source_target_pairs={{0,20},{1,28},{2,4},{3,12},{4,16},{5,24},{6,0},{7,8},{8,21},{9,29}... | collective-permute-start | bytes 73736 | tf_op jit(solution)/shard_map/ppermute | solution.py:698
  31.4 1.3 %collective-permute-start.16 = (bf16[24,512]{1,0:T(8,128)(2,1)S(1)}, bf16[24,512]{1,0:T(8,128)(2,1)S(1)}, u32[]{:S(2)}, u32[]{:S(2)}) collective-permute-start(bf16[24,512]{1,0:T(8,128)(2,1)S(1)} %get-tuple-element.32), channel_id=1, source_target_pairs={{0,12},{1,4},{2,28},{3,20},{4,8},{5,0},{6,24},{7,16},{8,13},{9,5},... | collective-permute-start | bytes 73736 | tf_op jit(solution)/shard_map/ppermute | solution.py:698
  33.6 2.7 %collective-permute-done.16.refs_1_ = bf16[24,512]{1,0:T(8,128)(2,1)S(1)} collective-permute-done((bf16[24,512]{1,0:T(8,128)(2,1)S(1)}, bf16[24,512]{1,0:T(8,128)(2,1)S(1)}, u32[]{:S(2)}, u32[]{:S(2)}) %collective-permute-start.16) | collective-permute-done | bytes 24608 | tf_op jit(solution)/shard_map/ppermute | solution.py:698
  37.3 6.6 %collective-permute-start.19 = (bf16[48,1152]{1,0:T(8,128)(2,1)S(1)}, bf16[48,1152]{1,0:T(8,128)(2,1)S(1)}, u32[]{:S(2)}, u32[]{:S(2)}) collective-permute-start(bf16[48,1152]{1,0:T(8,128)(2,1)S(1)} %get-tuple-element.34), channel_id=1, source_target_pairs={{0,3},{1,2},{2,1},{3,0},{4,7},{5,6},{6,5},{7,4},{8,11},{9,10},{10,... | collective-permute-start | bytes 331784 | tf_op jit(solution)/shard_map/ppermute | solution.py:239
  44.5 3.2 %collective-permute-done.19.refs_1_ = bf16[48,1152]{1,0:T(8,128)(2,1)S(1)} collective-permute-done((bf16[48,1152]{1,0:T(8,128)(2,1)S(1)}, bf16[48,1152]{1,0:T(8,128)(2,1)S(1)}, u32[]{:S(2)}, u32[]{:S(2)}) %collective-permute-start.19) | collective-permute-done | bytes 110624 | tf_op jit(solution)/shard_map/ppermute | solution.py:239
  47.8 3.0 %collective-permute-done.20.refs_2_ = bf16[48,1152]{1,0:T(8,128)(2,1)S(1)} collective-permute-done((bf16[48,1152]{1,0:T(8,128)(2,1)S(1)}, bf16[48,1152]{1,0:T(8,128)(2,1)S(1)}, u32[]{:S(2)}, u32[]{:S(2)}) %collective-permute-start.20) | collective-permute-done | bytes 110624 | tf_op jit(solution)/shard_map/ppermute | solution.py:239
  50.7 2.7 %collective-permute-done.21.refs_3_ = bf16[48,1152]{1,0:T(8,128)(2,1)S(1)} collective-permute-done((bf16[48,1152]{1,0:T(8,128)(2,1)S(1)}, bf16[48,1152]{1,0:T(8,128)(2,1)S(1)}, u32[]{:S(2)}, u32[]{:S(2)}) %collective-permute-start.21) | collective-permute-done | bytes 110624 | tf_op jit(solution)/shard_map/ppermute | solution.py:239
  53.7 2.7 %collective-permute-start.24 = (bf16[48,512]{1,0:T(8,128)(2,1)S(1)}, bf16[48,512]{1,0:T(8,128)(2,1)S(1)}, u32[]{:S(2)}, u32[]{:S(2)}) collective-permute-start(bf16[48,512]{1,0:T(8,128)(2,1)S(1)} %shard_map.132.refs_0_), channel_id=1, source_target_pairs={{0,3},{1,2},{2,1},{3,0},{4,7},{5,6},{6,5},{7,4},{8,11},{9,10},{10,... | collective-permute-start | bytes 147464 | tf_op jit(solution)/shard_map/ppermute | solution.py:239
  56.5 1.7 %collective-permute-start.22 = (bf16[48,512]{1,0:T(8,128)(2,1)S(1)}, bf16[48,512]{1,0:T(8,128)(2,1)S(1)}, u32[]{:S(2)}, u32[]{:S(2)}) collective-permute-start(bf16[48,512]{1,0:T(8,128)(2,1)S(1)} %shard_map.132.refs_0_), channel_id=1, source_target_pairs={{0,1},{1,0},{2,3},{3,2},{4,5},{5,4},{6,7},{7,6},{8,9},{9,8},{10,11... | collective-permute-start | bytes 147464 | tf_op jit(solution)/shard_map/ppermute | solution.py:239
  58.2 1.8 %collective-permute-done.24.refs_3_ = bf16[48,512]{1,0:T(8,128)(2,1)S(1)} collective-permute-done((bf16[48,512]{1,0:T(8,128)(2,1)S(1)}, bf16[48,512]{1,0:T(8,128)(2,1)S(1)}, u32[]{:S(2)}, u32[]{:S(2)}) %collective-permute-start.24) | collective-permute-done | bytes 49184 | tf_op jit(solution)/shard_map/ppermute | solution.py:239
  60.0 1.4 %collective-permute-done.23.refs_2_ = bf16[48,512]{1,0:T(8,128)(2,1)S(1)} collective-permute-done((bf16[48,512]{1,0:T(8,128)(2,1)S(1)}, bf16[48,512]{1,0:T(8,128)(2,1)S(1)}, u32[]{:S(2)}, u32[]{:S(2)}) %collective-permute-start.23) | collective-permute-done | bytes 49184 | tf_op jit(solution)/shard_map/ppermute | solution.py:239
  62.5 1.2 %collective-permute-done.25.arrived_ref = bf16[96,192]{1,0:T(8,128)(2,1)S(1)} collective-permute-done((bf16[96,192]{1,0:T(8,128)(2,1)S(1)}, bf16[96,192]{1,0:T(8,128)(2,1)S(1)}, u32[]{:S(2)}, u32[]{:S(2)}) %collective-permute-start.25) | collective-permute-done | bytes 36896 | tf_op jit(solution)/shard_map/ppermute | solution.py:239
  64.7 2.7 %collective-permute-start.28 = (bf16[24,192]{1,0:T(8,128)(2,1)S(1)}, bf16[24,192]{1,0:T(8,128)(2,1)S(1)}, u32[]{:S(2)}, u32[]{:S(2)}) collective-permute-start(bf16[24,192]{1,0:T(8,128)(2,1)S(1)} %get-tuple-element.43), channel_id=1, source_target_pairs={{20,0},{28,1},{4,2},{12,3},{16,4},{24,5},{0,6},{8,7},{21,8},{29,9}... | collective-permute-start | bytes 27656 | tf_op jit(solution)/shard_map/ppermute | solution.py:728
  68.4 1.2 %collective-permute-done.28.refs_2_ = bf16[24,192]{1,0:T(8,128)(2,1)S(1)} collective-permute-done((bf16[24,192]{1,0:T(8,128)(2,1)S(1)}, bf16[24,192]{1,0:T(8,128)(2,1)S(1)}, u32[]{:S(2)}, u32[]{:S(2)}) %collective-permute-start.28) | collective-permute-done | bytes 9248 | tf_op jit(solution)/shard_map/ppermute | solution.py:728
  69.6 1.8 %collective-permute-done.29.refs_3_ = bf16[24,192]{1,0:T(8,128)(2,1)S(1)} collective-permute-done((bf16[24,192]{1,0:T(8,128)(2,1)S(1)}, bf16[24,192]{1,0:T(8,128)(2,1)S(1)}, u32[]{:S(2)}, u32[]{:S(2)}) %collective-permute-start.29) | collective-permute-done | bytes 9248 | tf_op jit(solution)/shard_map/ppermute | solution.py:728
  (65 shorter events, 16.3 us)
Async XLA Ops:
  0.0 25.5 %collective-permute-start.14 = (bf16[192,1536]{1,0:T(8,128)(2,1)}, bf16[192,1536]{1,0:T(8,128)(2,1)S(1)}, u32[]{:S(2)}, u32[]{:S(2)}) collective-permute-start(bf16[192,1536]{1,0:T(8,128)(2,1)} %bitcast.2), channel_id=1, source_target_pairs={{0,4},{4,0},{8,12},{12,8},{16,20},{20,16},{24,28},{28,24},{1,5},{5... | collective-permute-start | bytes 1769480 | tf_op jit(solution)/shard_map/ppermute | solution.py:239
  3.2 5.7 %collective-permute-start.2 = (bf16[5,24,128]{2,1,0:T(8,128)(2,1)}, bf16[5,24,128]{2,1,0:T(8,128)(2,1)S(1)}, u32[]{:S(2)}, u32[]{:S(2)}) collective-permute-start(bf16[5,24,128]{2,1,0:T(8,128)(2,1)} %get-tuple-element.25.refs_0_), channel_id=1, source_target_pairs={{0,24},{4,28},{8,16},{12,20},{16,8},{20,12},{24,0},{28,4},{1,25},{... | collective-permute-start | bytes 92168 | tf_op jit(solution)/shard_map/ppermute | solution.py:239
  6.7 4.1 %collective-permute-start.1 = (bf16[5,24,128]{2,1,0:T(8,128)(2,1)}, bf16[5,24,128]{2,1,0:T(8,128)(2,1)S(1)}, u32[]{:S(2)}, u32[]{:S(2)}) collective-permute-start(bf16[5,24,128]{2,1,0:T(8,128)(2,1)} %get-tuple-element.25.refs_0_), channel_id=1, source_target_pairs={{0,16},{4,20},{8,24},{12,28},{16,0},{20,4},{24,8},{28,12},{1,17},{... | collective-permute-start | bytes 92168 | tf_op jit(solution)/shard_map/ppermute | solution.py:239
  7.2 4.1 %collective-permute-start = (bf16[5,24,128]{2,1,0:T(8,128)(2,1)}, bf16[5,24,128]{2,1,0:T(8,128)(2,1)S(1)}, u32[]{:S(2)}, u32[]{:S(2)}) collective-permute-start(bf16[5,24,128]{2,1,0:T(8,128)(2,1)} %get-tuple-element.25.refs_0_), channel_id=1, source_target_pairs={{0,8},{4,12},{8,0},{12,4},{16,24},{20,28},{24,16},{28,20},{1,9},{5... | collective-permute-start | bytes 92168 | tf_op jit(solution)/shard_map/ppermute | solution.py:239
  7.3 4.0 %collective-permute-start.3 = (bf16[5,24,128]{2,1,0:T(8,128)(2,1)}, bf16[5,24,128]{2,1,0:T(8,128)(2,1)S(1)}, u32[]{:S(2)}, u32[]{:S(2)}) collective-permute-start(bf16[5,24,128]{2,1,0:T(8,128)(2,1)} %get-tuple-element.25.refs_0_), channel_id=1, source_target_pairs={{0,4},{4,0},{8,12},{12,8},{16,20},{20,16},{24,28},{28,24},{1,5},{5... | collective-permute-start | bytes 92168 | tf_op jit(solution)/shard_map/ppermute | solution.py:239
  8.9 2.4 %collective-permute-start.6 = (bf16[5,24,128]{2,1,0:T(8,128)(2,1)S(1)}, bf16[5,24,128]{2,1,0:T(8,128)(2,1)S(1)}, u32[]{:S(2)}, u32[]{:S(2)}) collective-permute-start(bf16[5,24,128]{2,1,0:T(8,128)(2,1)S(1)} %collective-permute-done.2.refs_3_), channel_id=1, source_target_pairs={{0,4},{4,0},{8,12},{12,8},{16,20},{20,16},{24,28},{28,24},{1,5},{5... | collective-permute-start | bytes 92168 | tf_op jit(solution)/shard_map/ppermute | solution.py:239
  15.0 5.6 %collective-permute-start.7 = (bf16[72,640]{1,0:T(8,128)(2,1)S(1)}, bf16[72,640]{1,0:T(8,128)(2,1)S(1)}, u32[]{:S(2)}, u32[]{:S(2)}) collective-permute-start(bf16[72,640]{1,0:T(8,128)(2,1)S(1)} %shard_map.128.refs_0_), channel_id=1, source_target_pairs={{0,8},{4,12},{8,0},{12,4},{16,24},{20,28},{24,16},{28,20},{1,9},{5... | collective-permute-start | bytes 276488 | tf_op jit(solution)/shard_map/ppermute | solution.py:239
  15.3 7.6 %collective-permute-start.9 = (bf16[72,640]{1,0:T(8,128)(2,1)S(1)}, bf16[72,640]{1,0:T(8,128)(2,1)S(1)}, u32[]{:S(2)}, u32[]{:S(2)}) collective-permute-start(bf16[72,640]{1,0:T(8,128)(2,1)S(1)} %shard_map.128.refs_0_), channel_id=1, source_target_pairs={{0,24},{4,28},{8,16},{12,20},{16,8},{20,12},{24,0},{28,4},{1,25},{... | collective-permute-start | bytes 276488 | tf_op jit(solution)/shard_map/ppermute | solution.py:239
  18.1 6.0 %collective-permute-start.8 = (bf16[72,640]{1,0:T(8,128)(2,1)S(1)}, bf16[72,640]{1,0:T(8,128)(2,1)S(1)}, u32[]{:S(2)}, u32[]{:S(2)}) collective-permute-start(bf16[72,640]{1,0:T(8,128)(2,1)S(1)} %shard_map.128.refs_0_), channel_id=1, source_target_pairs={{0,16},{4,20},{8,24},{12,28},{16,0},{20,4},{24,8},{28,12},{1,17},{... | collective-permute-start | bytes 276488 | tf_op jit(solution)/shard_map/ppermute | solution.py:239
  18.6 6.0 %collective-permute-start.10 = (bf16[72,640]{1,0:T(8,128)(2,1)S(1)}, bf16[72,640]{1,0:T(8,128)(2,1)S(1)}, u32[]{:S(2)}, u32[]{:S(2)}) collective-permute-start(bf16[72,640]{1,0:T(8,128)(2,1)S(1)} %shard_map.128.refs_0_), channel_id=1, source_target_pairs={{0,4},{4,0},{8,12},{12,8},{16,20},{20,16},{24,28},{28,24},{1,5},{5... | collective-permute-start | bytes 276488 | tf_op jit(solution)/shard_map/ppermute | solution.py:239
  28.4 5.2 %collective-permute-start.18 = (bf16[24,512]{1,0:T(8,128)(2,1)S(1)}, bf16[24,512]{1,0:T(8,128)(2,1)S(1)}, u32[]{:S(2)}, u32[]{:S(2)}) collective-permute-start(bf16[24,512]{1,0:T(8,128)(2,1)S(1)} %get-tuple-element.32), channel_id=1, source_target_pairs={{0,28},{1,20},{2,12},{3,4},{4,24},{5,16},{6,8},{7,0},{8,29},{9,21}... | collective-permute-start | bytes 73736 | tf_op jit(solution)/shard_map/ppermute | solution.py:698
  28.9 4.8 %collective-permute-start.17 = (bf16[24,512]{1,0:T(8,128)(2,1)S(1)}, bf16[24,512]{1,0:T(8,128)(2,1)S(1)}, u32[]{:S(2)}, u32[]{:S(2)}) collective-permute-start(bf16[24,512]{1,0:T(8,128)(2,1)S(1)} %get-tuple-element.32), channel_id=1, source_target_pairs={{0,20},{1,28},{2,4},{3,12},{4,16},{5,24},{6,0},{7,8},{8,21},{9,29}... | collective-permute-start | bytes 73736 | tf_op jit(solution)/shard_map/ppermute | solution.py:698
  31.4 5.0 %collective-permute-start.16 = (bf16[24,512]{1,0:T(8,128)(2,1)S(1)}, bf16[24,512]{1,0:T(8,128)(2,1)S(1)}, u32[]{:S(2)}, u32[]{:S(2)}) collective-permute-start(bf16[24,512]{1,0:T(8,128)(2,1)S(1)} %get-tuple-element.32), channel_id=1, source_target_pairs={{0,12},{1,4},{2,28},{3,20},{4,8},{5,0},{6,24},{7,16},{8,13},{9,5},... | collective-permute-start | bytes 73736 | tf_op jit(solution)/shard_map/ppermute | solution.py:698
  32.7 3.6 %collective-permute-start.15 = (bf16[24,512]{1,0:T(8,128)(2,1)S(1)}, bf16[24,512]{1,0:T(8,128)(2,1)S(1)}, u32[]{:S(2)}, u32[]{:S(2)}) collective-permute-start(bf16[24,512]{1,0:T(8,128)(2,1)S(1)} %get-tuple-element.32), channel_id=1, source_target_pairs={{0,4},{1,12},{2,20},{3,28},{4,0},{5,8},{6,16},{7,24},{8,5},{9,13},... | collective-permute-start | bytes 73736 | tf_op jit(solution)/shard_map/ppermute | solution.py:698
  37.3 10.5 %collective-permute-start.19 = (bf16[48,1152]{1,0:T(8,128)(2,1)S(1)}, bf16[48,1152]{1,0:T(8,128)(2,1)S(1)}, u32[]{:S(2)}, u32[]{:S(2)}) collective-permute-start(bf16[48,1152]{1,0:T(8,128)(2,1)S(1)} %get-tuple-element.34), channel_id=1, source_target_pairs={{0,3},{1,2},{2,1},{3,0},{4,7},{5,6},{6,5},{7,4},{8,11},{9,10},{10,... | collective-permute-start | bytes 331784 | tf_op jit(solution)/shard_map/ppermute | solution.py:239
  43.9 6.9 %collective-permute-start.20 = (bf16[48,1152]{1,0:T(8,128)(2,1)S(1)}, bf16[48,1152]{1,0:T(8,128)(2,1)S(1)}, u32[]{:S(2)}, u32[]{:S(2)}) collective-permute-start(bf16[48,1152]{1,0:T(8,128)(2,1)S(1)} %get-tuple-element.35), channel_id=1, source_target_pairs={{0,1},{1,0},{2,3},{3,2},{4,5},{5,4},{6,7},{7,6},{8,9},{9,8},{10,11... | collective-permute-start | bytes 331784 | tf_op jit(solution)/shard_map/ppermute | solution.py:239
  43.9 9.6 %collective-permute-start.21 = (bf16[48,1152]{1,0:T(8,128)(2,1)S(1)}, bf16[48,1152]{1,0:T(8,128)(2,1)S(1)}, u32[]{:S(2)}, u32[]{:S(2)}) collective-permute-start(bf16[48,1152]{1,0:T(8,128)(2,1)S(1)} %get-tuple-element.36), channel_id=1, source_target_pairs={{0,2},{1,3},{2,0},{3,1},{4,6},{5,7},{6,4},{7,5},{8,10},{9,11},{10,... | collective-permute-start | bytes 331784 | tf_op jit(solution)/shard_map/ppermute | solution.py:239
  53.7 6.3 %collective-permute-start.24 = (bf16[48,512]{1,0:T(8,128)(2,1)S(1)}, bf16[48,512]{1,0:T(8,128)(2,1)S(1)}, u32[]{:S(2)}, u32[]{:S(2)}) collective-permute-start(bf16[48,512]{1,0:T(8,128)(2,1)S(1)} %shard_map.132.refs_0_), channel_id=1, source_target_pairs={{0,3},{1,2},{2,1},{3,0},{4,7},{5,6},{6,5},{7,4},{8,11},{9,10},{10,... | collective-permute-start | bytes 147464 | tf_op jit(solution)/shard_map/ppermute | solution.py:239
  56.4 5.0 %collective-permute-start.23 = (bf16[48,512]{1,0:T(8,128)(2,1)S(1)}, bf16[48,512]{1,0:T(8,128)(2,1)S(1)}, u32[]{:S(2)}, u32[]{:S(2)}) collective-permute-start(bf16[48,512]{1,0:T(8,128)(2,1)S(1)} %shard_map.132.refs_0_), channel_id=1, source_target_pairs={{0,2},{1,3},{2,0},{3,1},{4,6},{5,7},{6,4},{7,5},{8,10},{9,11},{10,... | collective-permute-start | bytes 147464 | tf_op jit(solution)/shard_map/ppermute | solution.py:239
  56.5 5.0 %collective-permute-start.22 = (bf16[48,512]{1,0:T(8,128)(2,1)S(1)}, bf16[48,512]{1,0:T(8,128)(2,1)S(1)}, u32[]{:S(2)}, u32[]{:S(2)}) collective-permute-start(bf16[48,512]{1,0:T(8,128)(2,1)S(1)} %shard_map.132.refs_0_), channel_id=1, source_target_pairs={{0,1},{1,0},{2,3},{3,2},{4,5},{5,4},{6,7},{7,6},{8,9},{9,8},{10,11... | collective-permute-start | bytes 147464 | tf_op jit(solution)/shard_map/ppermute | solution.py:239
  63.7 4.7 %collective-permute-start.26 = (bf16[24,192]{1,0:T(8,128)(2,1)S(1)}, bf16[24,192]{1,0:T(8,128)(2,1)S(1)}, u32[]{:S(2)}, u32[]{:S(2)}) collective-permute-start(bf16[24,192]{1,0:T(8,128)(2,1)S(1)} %get-tuple-element.41), channel_id=1, source_target_pairs={{4,0},{12,1},{20,2},{28,3},{0,4},{8,5},{16,6},{24,7},{5,8},{13,9},... | collective-permute-start | bytes 27656 | tf_op jit(solution)/shard_map/ppermute | solution.py:728
  63.9 4.5 %collective-permute-start.27 = (bf16[24,192]{1,0:T(8,128)(2,1)S(1)}, bf16[24,192]{1,0:T(8,128)(2,1)S(1)}, u32[]{:S(2)}, u32[]{:S(2)}) collective-permute-start(bf16[24,192]{1,0:T(8,128)(2,1)S(1)} %get-tuple-element.42), channel_id=1, source_target_pairs={{12,0},{4,1},{28,2},{20,3},{8,4},{0,5},{24,6},{16,7},{13,8},{5,9},... | collective-permute-start | bytes 27656 | tf_op jit(solution)/shard_map/ppermute | solution.py:728
  64.7 4.9 %collective-permute-start.28 = (bf16[24,192]{1,0:T(8,128)(2,1)S(1)}, bf16[24,192]{1,0:T(8,128)(2,1)S(1)}, u32[]{:S(2)}, u32[]{:S(2)}) collective-permute-start(bf16[24,192]{1,0:T(8,128)(2,1)S(1)} %get-tuple-element.43), channel_id=1, source_target_pairs={{20,0},{28,1},{4,2},{12,3},{16,4},{24,5},{0,6},{8,7},{21,8},{29,9}... | collective-permute-start | bytes 27656 | tf_op jit(solution)/shard_map/ppermute | solution.py:728
  67.4 4.0 %collective-permute-start.29 = (bf16[24,192]{1,0:T(8,128)(2,1)S(1)}, bf16[24,192]{1,0:T(8,128)(2,1)S(1)}, u32[]{:S(2)}, u32[]{:S(2)}) collective-permute-start(bf16[24,192]{1,0:T(8,128)(2,1)S(1)} %get-tuple-element.44), channel_id=1, source_target_pairs={{28,0},{20,1},{12,2},{4,3},{24,4},{16,5},{8,6},{0,7},{29,8},{21,9}... | collective-permute-start | bytes 27656 | tf_op jit(solution)/shard_map/ppermute | solution.py:728
  (16 other events, 148.3 us)

commit v5 on v4

--- a/solution.py
+++ b/solution.py
@@ -198,6 +198,7 @@
 STAT = 128
 WIDE = KVD + STAT
 VMEM = pl.BlockSpec(memory_space=pltpu.VMEM)
+SMEM = pl.BlockSpec(memory_space=pltpu.SMEM)
 HBM = pl.BlockSpec(memory_space=pltpu.HBM)
 
 
@@ -244,22 +245,12 @@
 
 
 def project_kernel(*refs):
-    x_hbm, attn_hbm, moe_hbm, w_hbm, lengths_hbm, pages_hbm, routes_hbm, weights_hbm = refs[:8]
-    heads_ref, x_ref, live_ref, routing_ref, gain_ref = refs[8:13]
-    x_in, attn_gain, moe_gain, w_in, lengths, pages, routes, weights, sem = refs[13:]
+    x_hbm, attn_hbm, w_hbm, lengths_hbm, heads_ref, x_ref = refs[:6]
+    x_in, attn_gain, w_in, lengths, sem = refs[6:]
     loads = [
         pltpu.make_async_copy(source, target, sem.at[i])
         for i, (source, target) in enumerate(
-            [
-                (lengths_hbm, lengths),
-                (x_hbm, x_in),
-                (attn_hbm, attn_gain),
-                (w_hbm, w_in),
-                (pages_hbm, pages),
-                (routes_hbm, routes),
-                (weights_hbm, weights),
-                (moe_hbm, moe_gain),
-            ]
+            [(lengths_hbm, lengths), (x_hbm, x_in), (attn_hbm, attn_gain), (w_hbm, w_in)]
         )
     ]
     for load in loads:
@@ -291,16 +282,20 @@
         both = jnp.concatenate([one, one], axis=1)
         turned = both * cosine + pltpu.roll(both, HD // 2, 1) * sine
         heads_ref[i] = jnp.where(first + i < HEADS + KVH, turned, both).astype(BF16)
-    for load in loads[4:]:
-        load.wait()
+
+
+def prepare_kernel(heads_in, pages, lengths, routes, weights, moe_gain, *out_refs):
+    heads_ref, live_ref, routing_ref, gain_ref = out_refs
+    heads_ref[...] = heads_in[...]
     slots = live_ref.shape[1]
     slot = iota((1, slots), 1)
-    for r in range(requests):
+    for r in range(live_ref.shape[0]):
         page = jnp.zeros((1, slots), jnp.int32)
         for j in range(slots // PAGE):
             page = jnp.where(slot // PAGE == j, pages[r, j], page)
         live = page * PAGE + slot % PAGE < lengths[r]
         live_ref[r : r + 1, :] = jnp.where(live, 1.0, 0.0)
+    row_count = routing_ref.shape[0]
     high, middle, low = split3(rows_of(weights))
     routing_ref[...] = jnp.concatenate(
         [rows_of(routes), high, middle, low, jnp.zeros((row_count, STAT - 4 * TOP), F32)], axis=1
@@ -484,14 +479,17 @@
 
 
 def gate_kernel(groups, *refs):
-    piece_refs, w_ref = refs[:groups], refs[groups]
+    near_refs, far_refs, w_ref = refs[: groups // 2], refs[groups // 2 : groups], refs[groups]
     message_refs = refs[groups + 1 : 2 * groups + 1]
     placed_ref, scale_ref, full_ref = refs[2 * groups + 1 :]
     member, me = lax.axis_index("seq"), lax.axis_index("req")
     width = w_ref.shape[1]
-    row_count = piece_refs[0].shape[0]
+    row_count = near_refs[0].shape[0]
     tokens = groups * row_count
-    pieces = jnp.concatenate([ref[...].astype(F32) for ref in piece_refs], axis=0)
+    near = jnp.concatenate([ref[...].astype(F32) for ref in near_refs], axis=0)
+    far = jnp.concatenate([ref[...].astype(F32) for ref in far_refs], axis=0)
+    first = member % 2 == 0
+    pieces = jnp.concatenate([jnp.where(first, far, near), jnp.where(first, near, far)], axis=0)
     mixed, routing = pieces[:, :width].astype(BF16), pieces[:, width:]
     power = routing[:, 4 * TOP : 4 * TOP + 1] + (
         routing[:, 4 * TOP + 1 : 4 * TOP + 2] + routing[:, 4 * TOP + 2 : 4 * TOP + 3]
@@ -567,10 +565,10 @@
             (((0,), (0,)), ((), ())),
             preferred_element_type=F32,
         )
-    width = w_ref.shape[2] // 2
-    left, right = total[:, :width], total[:, width:]
-    send_ref[...] = jnp.where(core == 0, left, right).astype(BF16)
-    keep_ref[...] = jnp.where(core == 0, right, left)
+    half = total.shape[0] // 2
+    low, high = total[:half], total[half:]
+    send_ref[...] = jnp.where(core == 0, high, low).astype(BF16)
+    keep_ref[...] = jnp.where(core == 0, low, high)
 
 
 def spread_kernel(keep_ref, arrived_ref, *out_refs):
@@ -580,11 +578,20 @@
         out_ref[...] = total[k * row_count : (k + 1) * row_count].astype(BF16)
 
 
-def final_kernel(resid_ref, *refs):
-    arrived_refs, out_ref = refs[:-1], refs[-1]
-    total = resid_ref[...]
-    for ref in arrived_refs:
+def halve_kernel(resid_ref, *refs):
+    arrived_refs, send_ref, keep_ref = refs[:-2], refs[-2], refs[-1]
+    total = arrived_refs[0][...].astype(F32)
+    for ref in arrived_refs[1:]:
         total = total + ref[...].astype(F32)
+    width = total.shape[1] // 2
+    left, right = total[:, :width], total[:, width:]
+    first = lax.axis_index("seq") % 2 == 0
+    send_ref[...] = jnp.where(first, right, left)
+    keep_ref[...] = resid_ref[...] + jnp.where(first, left, right)
+
+
+def final_kernel(keep_ref, arrived_ref, out_ref):
+    total = keep_ref[...] + arrived_ref[...]
     for r in range(out_ref.shape[0]):
         out_ref[r] = total[r * NSTEP : (r + 1) * NSTEP].astype(BF16)
 
@@ -611,52 +618,39 @@
     heads = w_qkv.shape[1] // HD
     width = w_o.shape[1]
 
-    own_heads, x, live, routing, gain = kernel_call(
+    heads_shape = jax.ShapeDtypeStruct((heads, row_count, 2 * HD), BF16)
+    own_heads, x = kernel_call(
         project_kernel,
+        [heads_shape, jax.ShapeDtypeStruct((row_count, D), F32)],
+        [HBM] * 4,
         [
-            jax.ShapeDtypeStruct((heads, row_count, 2 * HD), BF16),
-            jax.ShapeDtypeStruct((row_count, D), F32),
+            pltpu.VMEM(x_in.shape, BF16),
+            pltpu.VMEM((D,), F32),
+            pltpu.VMEM((w_qkv.shape[1], D), BF16),
+            pltpu.SMEM(lengths.shape, jnp.int32),
+            pltpu.SemaphoreType.DMA((4,)),
+        ],
+        vmem_mib=60,
+        cost=5.0,
+    )(x_in, attn_gain, w_qkv.T, lengths)
+
+    def gathered(own):
+        return [own] + [swap(own, "seq", 2 * k) for k in range(1, chips)]
+
+    near = gathered(own_heads)
+    first = near[1]
+    near[0], live, routing, gain = kernel_call(
+        prepare_kernel,
+        [
+            heads_shape,
             jax.ShapeDtypeStruct((requests, cache_k.shape[1]), F32),
             jax.ShapeDtypeStruct((row_count, STAT), F32),
             jax.ShapeDtypeStruct((1, D), F32),
         ],
-        [HBM] * 8,
-        [
-            pltpu.VMEM(x_in.shape, BF16),
-            pltpu.VMEM((D,), F32),
-            pltpu.VMEM((D,), F32),
-            pltpu.VMEM((w_qkv.shape[1], D), BF16),
-            pltpu.SMEM(lengths.shape, jnp.int32),
-            pltpu.SMEM(page_map.shape, jnp.int32),
-            pltpu.VMEM(routes.shape, jnp.int32),
-            pltpu.VMEM(route_weights.shape, F32),
-            pltpu.SemaphoreType.DMA((8,)),
-        ],
-        vmem_mib=60,
-        cost=5.0,
-    )(x_in, attn_gain, moe_gain, w_qkv.T, lengths, page_map, routes, route_weights)
-    def gathered(own, *first):
-        near = [swap(own, "seq", 2 * k) for k in range(chips - 1, 0, -1)]
-        near = [own] + near[::-1]
-        near[1] = after(near[1], *first) if first else near[1]
-        return near, [swap(piece, "seq", 1) for piece in near]
-
-    near, far = gathered(own_heads)
-    def gathered(own, *first):
-        near = [swap(own, "seq", 2 * k) for k in range(chips - 1, 0, -1)]
-        near = [own] + near[::-1]
-        near[1] = after(near[1], *first) if first else near[1]
-        return near, [swap(piece, "seq", 1) for piece in near]
-
-    near, far = gathered(own_heads)
-    def gathered(own, *first):
-        near = [swap(own, "seq", 2 * k) for k in range(chips - 1, 0, -1)]
-        near = [own] + near[::-1]
-        near[1] = after(near[1], *first) if first else near[1]
-        return near, [swap(piece, "seq", 1) for piece in near]
-
-    near, far = gathered(own_heads)
-    down = lax.all_to_all(w_down, "req", 0, 0, tiled=True)
+        [VMEM] + [SMEM] * 2 + [VMEM] * 3,
+    )(after(own_heads, near[1]), page_map, lengths, routes, route_weights, moe_gain)
+    near[1] = after(near[1], live)
+    far = [swap(piece, "seq", 1) for piece in [after(own_heads, first)] + near[1:]]
     part_shape = jax.ShapeDtypeStruct((GROUP * row_count, WIDE), BF16)
     head_scratch = [
         pltpu.VMEM((2, chips, heads, row_count, 2 * HD), BF16),
@@ -674,9 +668,10 @@
         part_shape,
         [VMEM] * (2 * chips),
         head_scratch,
-        cost=0.5,
     )(*near, *far)
-    near, far = gathered(part, fresh)
+    near = gathered(part)
+    near[1] = after(near[1], fresh)
+    far = [swap(piece, "seq", 1) for piece in [part] + near[1:]]
     packed, resid = kernel_call(
         lambda *refs: merge_kernel(members + 1, *refs),
         [
@@ -686,16 +681,23 @@
         [VMEM] * (members + 6),
     )(*near, *far, fresh, x, gain, routing, w_o.T, swap(w_o.T, "seq", 1))
 
-    def crossing(mask):
+    everyone = [(p, c, q) for p in range(chips) for c in range(2) for q in range(groups)]
+
+    def crossing(j):
         return [
-            ((2 * p + c) * groups + q, (2 * (q ^ mask) + 1 - c) * groups + p)
-            for p in range(chips)
-            for c in range(2)
-            for q in range(groups)
+            ((2 * p + c) * groups + q, (2 * (q ^ (2 * c + j)) + 1 - c) * groups + p)
+            for p, c, q in everyone
         ]
 
+    def returning(j):
+        return [
+            ((2 * p + c) * groups + q, (2 * q + 1 - c) * groups + (p ^ (2 * c + j)))
+            for p, c, q in everyone
+        ]
+
     place = ("seq", "req")
-    pieces = [lax.ppermute(packed, place, crossing(k)) for k in range(groups)]
+    near = [lax.ppermute(packed, place, crossing(j)) for j in range(groups // 2)]
+    far = [swap(piece, "seq", 1) for piece in near]
     experts = w_gate_up.shape[0]
     slots = groups * CAP
     *messages, placed, scale = kernel_call(
@@ -707,32 +709,32 @@
         ],
         [VMEM] * (groups + 1),
         [pltpu.VMEM((experts, slots, 2 * FFE + STAT), BF16)],
-    )(*pieces, w_gate_up)
+    )(*near, *far, w_gate_up)
     sums = [messages[0]] + [swap(messages[k], "req", k) for k in (3, 1, 2)]
     hidden = kernel_call(
         hidden_kernel, jax.ShapeDtypeStruct((slots, FFE), BF16), [VMEM] * groups
     )(*sums)
     hiddens = [hidden] + [swap(hidden, "req", k) for k in range(1, groups)]
+    half = (groups * row_count // 2, 2 * width)
     send, keep = kernel_call(
         lambda *refs: down_kernel(groups, *refs),
-        [
-            jax.ShapeDtypeStruct((groups * row_count, width), BF16),
-            jax.ShapeDtypeStruct((groups * row_count, width), F32),
-        ],
+        [jax.ShapeDtypeStruct(half, BF16), jax.ShapeDtypeStruct(half, F32)],
         [VMEM] * (groups + 3),
     )(*hiddens, w_down, placed, scale)
     outs = kernel_call(
-        spread_kernel, [jax.ShapeDtypeStruct((row_count, width), BF16)] * groups, [VMEM] * 2
+        spread_kernel,
+        [jax.ShapeDtypeStruct((row_count, 2 * width), BF16)] * (groups // 2),
+        [VMEM] * 2,
     )(keep, swap(send, "seq", 1))
-    arrived = [
-        lax.ppermute(out, place, [(target, source) for source, target in crossing(k)])
-        for k, out in enumerate(outs)
-    ]
+    arrived = [lax.ppermute(out, place, returning(j)) for j, out in enumerate(outs)]
+    send, keep = kernel_call(
+        halve_kernel,
+        [jax.ShapeDtypeStruct((row_count, width), F32)] * 2,
+        [VMEM] * (1 + groups // 2),
+    )(resid, *arrived)
     return kernel_call(
-        final_kernel,
-        jax.ShapeDtypeStruct((requests, NSTEP, width), BF16),
-        [VMEM] * (groups + 1),
-    )(resid, *arrived)
+        final_kernel, jax.ShapeDtypeStruct((requests, NSTEP, width), BF16), [VMEM] * 2
+    )(keep, swap(send, "seq", 1))
 
 
 def local(*args):

time: 73 us -> 67.3 us (0.922); the launches traced: 72.1 us -> 67.1 us
  starting transfers between devices: 29.6 us -> 26.7 us
  local copies, waits for them, and re-layouts: 2.36 us -> 0.79 us
  waiting for transfers between devices: 30.5 us -> 29.4 us
    ppermute x8 -> x4, starting transfers between devices: 9.15 us -> 4.01 us  [the longest x2 2.02 us: staged(): lax.ppermute(out, place, returning(j))]
    ppermute x22 -> x25, starting transfers between devices: 20.4 us -> 22.7 us  [swap(): return lax.ppermute(value, axis, pairs)]
    unnamed x20 -> x24, local copies, waits for them, and re-layouts: 2.36 us -> 0.79 us
    ppermute x22 -> x25, waiting for transfers between devices: 23.9 us -> 22.8 us  [swap(): return lax.ppermute(value, axis, pairs)]
    pallas_call x2 -> x4, Pallas kernels: 2.71 us -> 3.41 us  [the longest x1 2.58 us: staged(): kernel_call(project_kernel, [heads_shape, jax.ShapeDtypeStruct((row_count...]
    ppermute x8 -> x4, waiting for transfers between devices: 6.53 us -> 6.55 us  [the longest x2 3.4 us: staged(): lax.ppermute(packed, place, crossing(j))]
  transfers between devices with their start and end apart: 30 -> 29, of which waited for: 20 -> 24; matrix products, arithmetic and copies ran while one was open for 0% -> 0% of each run, Pallas kernels for 7% -> 8%
where the time goes in v5:
time: 67.3 us; the launch traced here: 67.1 us
  waiting for transfers between devices  29.4 us (44%)
  starting transfers between devices  26.7 us (40%)
  Pallas kernels  10.1 us (15%)
  local copies, waits for them, and re-layouts  0.79 us (1%)
    ppermute x25, waiting for transfers between devices, swap(): return lax.ppermute(value, axis, pairs)  22.8 us
    ppermute x25, starting transfers between devices, swap(): return lax.ppermute(value, axis, pairs)  22.7 us
    ppermute x2, waiting for transfers between devices, staged(): lax.ppermute(packed, place, crossing(j))  3.4 us
    ppermute x2, waiting for transfers between devices, staged(): lax.ppermute(out, place, returning(j))  3.15 us
    pallas_call x1, Pallas kernels, staged(): kernel_call(project_kernel, [heads_shape, jax.ShapeDtypeStruct((row_count...  2.58 us
    ppermute x2, starting transfers between devices, staged(): lax.ppermute(out, place, returning(j))  2.02 us
    ppermute x2, starting transfers between devices, staged(): lax.ppermute(packed, place, crossing(j))  2 us
    pallas_call x1, Pallas kernels, staged(): kernel_call(lambda *refs: merge_kernel(members + 1, *refs), [jax.ShapeDty...  1.92 us
  transfers between devices with their start and end apart: 29, of which 24 were waited for; matrix products, arithmetic and copies ran while one was open for 0% of the time, Pallas kernels for 8%

profile of v5, /device:TPU:0, one launch (start us, length us, event | category | flops | bytes accessed | tf_op | source)
XLA Modules:
  0.0 67.1 jit_solution(6458932801898430376)
XLA Ops:
  0.5 2.6 %shard_map.127 = (bf16[5,24,128]{2,1,0:T(8,128)(2,1)}, f32[24,1536]{1,0:T(8,128)}) custom-call(bf16[6,4,1536]{2,1,0:T(4,128)(2,1)} %refs_0_.1, f32[1536]{0:T(1024)} %refs_1_.1, bf16[320,1536]{1,0:T(8,128)(2,1)} %bitcast.4, s32[6]{0:T(128)} %lengths.1), custom_call_target="tpu_custom_call" | custom-call | flops 5000000000 | bytes 15000000 | tf_op jit(solution)/shard_map/pallas_call | solution.py:622
  3.1 2.6 %collective-permute-start = (bf16[5,24,128]{2,1,0:T(8,128)(2,1)}, bf16[5,24,128]{2,1,0:T(8,128)(2,1)S(1)}, u32[]{:S(2)}, u32[]{:S(2)}) collective-permute-start(bf16[5,24,128]{2,1,0:T(8,128)(2,1)} %get-tuple-element.29.heads_in), channel_id=1, source_target_pairs={{0,8},{4,12},{8,0},{12,4},{16,24},{20,28},{24,16},{28,20},{1,9},{5... | collective-permute-start | bytes 92168 | tf_op jit(solution)/shard_map/ppermute | solution.py:240
  5.7 1.5 %collective-permute-start.2 = (bf16[5,24,128]{2,1,0:T(8,128)(2,1)}, bf16[5,24,128]{2,1,0:T(8,128)(2,1)S(1)}, u32[]{:S(2)}, u32[]{:S(2)}) collective-permute-start(bf16[5,24,128]{2,1,0:T(8,128)(2,1)} %get-tuple-element.29.heads_in), channel_id=1, source_target_pairs={{0,24},{4,28},{8,16},{12,20},{16,8},{20,12},{24,0},{28,4},{1,25},{... | collective-permute-start | bytes 92168 | tf_op jit(solution)/shard_map/ppermute | solution.py:240
  9.4 1.3 %collective-permute-done.2.refs_3_ = bf16[5,24,128]{2,1,0:T(8,128)(2,1)S(1)} collective-permute-done((bf16[5,24,128]{2,1,0:T(8,128)(2,1)}, bf16[5,24,128]{2,1,0:T(8,128)(2,1)S(1)}, u32[]{:S(2)}, u32[]{:S(2)}) %collective-permute-start.2) | collective-permute-done | bytes 30752 | tf_op jit(solution)/shard_map/ppermute | solution.py:240
  12.6 1.1 %shard_map.129.refs_0_ = bf16[72,640]{1,0:T(8,128)(2,1)S(1)} custom-call(bf16[5,24,128]{2,1,0:T(8,128)(2,1)S(1)} %get-tuple-element.30.refs_0_, bf16[5,24,128]{2,1,0:T(8,128)(2,1)S(1)} %collective-permute-done.refs_1_, bf16[5,24,128]{2,1,0:T(8,128)(2,1)S(1)} %collective-permute-done.1.refs_2_, bf16[5,24,128]{2,1,0:T(8,128)(2,1)S(1)} %collective-permute-done.2.refs_3_, ...), custom_call_target="tpu_custom_call" | custom-call | flops 500000000 | bytes 1500000 | tf_op jit(solution)/shard_map/pallas_call | solution.py:660
  13.7 1.6 %collective-permute-start.7 = (bf16[72,640]{1,0:T(8,128)(2,1)S(1)}, bf16[72,640]{1,0:T(8,128)(2,1)S(1)}, u32[]{:S(2)}, u32[]{:S(2)}) collective-permute-start(bf16[72,640]{1,0:T(8,128)(2,1)S(1)} %shard_map.129.refs_0_), channel_id=1, source_target_pairs={{0,8},{4,12},{8,0},{12,4},{16,24},{20,28},{24,16},{28,20},{1,9},{5... | collective-permute-start | bytes 276488 | tf_op jit(solution)/shard_map/ppermute | solution.py:240
  15.3 1.3 %collective-permute-start.9 = (bf16[72,640]{1,0:T(8,128)(2,1)S(1)}, bf16[72,640]{1,0:T(8,128)(2,1)S(1)}, u32[]{:S(2)}, u32[]{:S(2)}) collective-permute-start(bf16[72,640]{1,0:T(8,128)(2,1)S(1)} %shard_map.129.refs_0_), channel_id=1, source_target_pairs={{0,24},{4,28},{8,16},{12,20},{16,8},{20,12},{24,0},{28,4},{1,25},{... | collective-permute-start | bytes 276488 | tf_op jit(solution)/shard_map/ppermute | solution.py:240
  17.3 1.1 %shard_map.130.refs_8_ = bf16[72,640]{1,0:T(8,128)(2,1)S(1)} custom-call(bf16[5,24,128]{2,1,0:T(8,128)(2,1)S(1)} %get-tuple-element.30.refs_0_, bf16[5,24,128]{2,1,0:T(8,128)(2,1)S(1)} %collective-permute-done.refs_1_, bf16[5,24,128]{2,1,0:T(8,128)(2,1)S(1)} %collective-permute-done.1.refs_2_, bf16[5,24,128]{2,1,0:T(8,128)(2,1)S(1)} %collective-permute-done.2.refs_3_, ...), custom_call_target="tpu_custom_call" | custom-call | flops 500000000 | bytes 1500000 | tf_op jit(solution)/shard_map/pallas_call | solution.py:666
  19.2 2.0 %collective-permute-done.9.refs_3_ = bf16[72,640]{1,0:T(8,128)(2,1)S(1)} collective-permute-done((bf16[72,640]{1,0:T(8,128)(2,1)S(1)}, bf16[72,640]{1,0:T(8,128)(2,1)S(1)}, u32[]{:S(2)}, u32[]{:S(2)}) %collective-permute-start.9) | collective-permute-done | bytes 92192 | tf_op jit(solution)/shard_map/ppermute | solution.py:240
  21.2 1.4 %collective-permute-done.8.refs_2_ = bf16[72,640]{1,0:T(8,128)(2,1)S(1)} collective-permute-done((bf16[72,640]{1,0:T(8,128)(2,1)S(1)}, bf16[72,640]{1,0:T(8,128)(2,1)S(1)}, u32[]{:S(2)}, u32[]{:S(2)}) %collective-permute-start.8) | collective-permute-done | bytes 92192 | tf_op jit(solution)/shard_map/ppermute | solution.py:240
  24.1 1.9 %shard_map.131 = (bf16[24,512]{1,0:T(8,128)(2,1)S(1)}, f32[24,192]{1,0:T(8,128)S(1)}) custom-call(bf16[72,640]{1,0:T(8,128)(2,1)S(1)} %shard_map.129.refs_0_, bf16[72,640]{1,0:T(8,128)(2,1)S(1)} %collective-permute-done.7.refs_1_, bf16[72,640]{1,0:T(8,128)(2,1)S(1)} %collective-permute-done.8.refs_2_, bf16[72,640]{1,0:T(8,128)(2,1)S(1)} %collective-permute-done.9.refs_3_, ...), custom_call_target="tpu_custom_call" | custom-call | flops 500000000 | bytes 1500000 | tf_op jit(solution)/shard_map/pallas_call | solution.py:675
  26.0 1.2 %collective-permute-start.16 = (bf16[24,512]{1,0:T(8,128)(2,1)S(1)}, bf16[24,512]{1,0:T(8,128)(2,1)S(1)}, u32[]{:S(2)}, u32[]{:S(2)}) collective-permute-start(bf16[24,512]{1,0:T(8,128)(2,1)S(1)} %get-tuple-element.38), channel_id=1, source_target_pairs={{0,12},{1,4},{2,28},{3,20},{4,24},{5,16},{6,8},{7,0},{8,13},{9,5},... | collective-permute-start | bytes 73736 | tf_op jit(solution)/shard_map/ppermute | solution.py:699
  28.0 3.1 %collective-permute-done.16.refs_1_ = bf16[24,512]{1,0:T(8,128)(2,1)S(1)} collective-permute-done((bf16[24,512]{1,0:T(8,128)(2,1)S(1)}, bf16[24,512]{1,0:T(8,128)(2,1)S(1)}, u32[]{:S(2)}, u32[]{:S(2)}) %collective-permute-start.16) | collective-permute-done | bytes 24608 | tf_op jit(solution)/shard_map/ppermute | solution.py:699
  33.6 5.3 %collective-permute-start.19 = (bf16[48,1152]{1,0:T(8,128)(2,1)S(1)}, bf16[48,1152]{1,0:T(8,128)(2,1)S(1)}, u32[]{:S(2)}, u32[]{:S(2)}) collective-permute-start(bf16[48,1152]{1,0:T(8,128)(2,1)S(1)} %get-tuple-element.40), channel_id=1, source_target_pairs={{0,3},{1,2},{2,1},{3,0},{4,7},{5,6},{6,5},{7,4},{8,11},{9,10},{10,... | collective-permute-start | bytes 331784 | tf_op jit(solution)/shard_map/ppermute | solution.py:240
  39.5 3.3 %collective-permute-done.19.refs_1_ = bf16[48,1152]{1,0:T(8,128)(2,1)S(1)} collective-permute-done((bf16[48,1152]{1,0:T(8,128)(2,1)S(1)}, bf16[48,1152]{1,0:T(8,128)(2,1)S(1)}, u32[]{:S(2)}, u32[]{:S(2)}) %collective-permute-start.19) | collective-permute-done | bytes 110624 | tf_op jit(solution)/shard_map/ppermute | solution.py:240
  42.8 3.7 %collective-permute-done.20.refs_2_ = bf16[48,1152]{1,0:T(8,128)(2,1)S(1)} collective-permute-done((bf16[48,1152]{1,0:T(8,128)(2,1)S(1)}, bf16[48,1152]{1,0:T(8,128)(2,1)S(1)}, u32[]{:S(2)}, u32[]{:S(2)}) %collective-permute-start.20) | collective-permute-done | bytes 110624 | tf_op jit(solution)/shard_map/ppermute | solution.py:240
  46.6 1.5 %collective-permute-done.21.refs_3_ = bf16[48,1152]{1,0:T(8,128)(2,1)S(1)} collective-permute-done((bf16[48,1152]{1,0:T(8,128)(2,1)S(1)}, bf16[48,1152]{1,0:T(8,128)(2,1)S(1)}, u32[]{:S(2)}, u32[]{:S(2)}) %collective-permute-start.21) | collective-permute-done | bytes 110624 | tf_op jit(solution)/shard_map/ppermute | solution.py:240
  50.3 2.5 %collective-permute-start.22 = (bf16[48,512]{1,0:T(8,128)(2,1)S(1)}, bf16[48,512]{1,0:T(8,128)(2,1)S(1)}, u32[]{:S(2)}, u32[]{:S(2)}) collective-permute-start(bf16[48,512]{1,0:T(8,128)(2,1)S(1)} %shard_map.133.refs_0_), channel_id=1, source_target_pairs={{0,1},{1,0},{2,3},{3,2},{4,5},{5,4},{6,7},{7,6},{8,9},{9,8},{10,11... | collective-permute-start | bytes 147464 | tf_op jit(solution)/shard_map/ppermute | solution.py:240
  52.8 2.0 %collective-permute-done.24.refs_3_ = bf16[48,512]{1,0:T(8,128)(2,1)S(1)} collective-permute-done((bf16[48,512]{1,0:T(8,128)(2,1)S(1)}, bf16[48,512]{1,0:T(8,128)(2,1)S(1)}, u32[]{:S(2)}, u32[]{:S(2)}) %collective-permute-start.24) | collective-permute-done | bytes 49184 | tf_op jit(solution)/shard_map/ppermute | solution.py:240
  56.4 1.2 %collective-permute-done.25.arrived_ref = bf16[48,384]{1,0:T(8,128)(2,1)S(1)} collective-permute-done((bf16[48,384]{1,0:T(8,128)(2,1)S(1)}, bf16[48,384]{1,0:T(8,128)(2,1)S(1)}, u32[]{:S(2)}, u32[]{:S(2)}) %collective-permute-start.25) | collective-permute-done | bytes 36896 | tf_op jit(solution)/shard_map/ppermute | solution.py:240
  57.8 1.8 %collective-permute-start.27 = (bf16[24,384]{1,0:T(8,128)(2,1)S(1)}, bf16[24,384]{1,0:T(8,128)(2,1)S(1)}, u32[]{:S(2)}, u32[]{:S(2)}) collective-permute-start(bf16[24,384]{1,0:T(8,128)(2,1)S(1)} %get-tuple-element.48), channel_id=1, source_target_pairs={{0,5},{1,13},{2,21},{3,29},{4,3},{5,11},{6,19},{7,27},{8,4},{9,12}... | collective-permute-start | bytes 55304 | tf_op jit(solution)/shard_map/ppermute | solution.py:729
  59.6 1.3 %collective-permute-done.26.refs_0_ = bf16[24,384]{1,0:T(8,128)(2,1)S(1)} collective-permute-done((bf16[24,384]{1,0:T(8,128)(2,1)S(1)}, bf16[24,384]{1,0:T(8,128)(2,1)S(1)}, u32[]{:S(2)}, u32[]{:S(2)}) %collective-permute-start.26) | collective-permute-done | bytes 18464 | tf_op jit(solution)/shard_map/ppermute | solution.py:729
  60.9 1.9 %collective-permute-done.27.refs_1_ = bf16[24,384]{1,0:T(8,128)(2,1)S(1)} collective-permute-done((bf16[24,384]{1,0:T(8,128)(2,1)S(1)}, bf16[24,384]{1,0:T(8,128)(2,1)S(1)}, u32[]{:S(2)}, u32[]{:S(2)}) %collective-permute-start.27) | collective-permute-done | bytes 18464 | tf_op jit(solution)/shard_map/ppermute | solution.py:729
  62.9 2.8 %collective-permute-start.28 = (f32[24,192]{1,0:T(8,128)S(1)}, f32[24,192]{1,0:T(8,128)S(1)}, u32[]{:S(2)}, u32[]{:S(2)}) collective-permute-start(f32[24,192]{1,0:T(8,128)S(1)} %get-tuple-element.50), channel_id=1, source_target_pairs={{0,4},{4,0},{8,12},{12,8},{16,20},{20,16},{24,28},{28,24},{1,5},{5... | collective-permute-start | bytes 55304 | tf_op jit(solution)/shard_map/ppermute | solution.py:240
  (69 shorter events, 17.2 us)
Async XLA Ops:
  0.0 24.1 %collective-permute-start.14 = (bf16[192,1536]{1,0:T(8,128)(2,1)}, bf16[192,1536]{1,0:T(8,128)(2,1)S(1)}, u32[]{:S(2)}, u32[]{:S(2)}) collective-permute-start(bf16[192,1536]{1,0:T(8,128)(2,1)} %bitcast.2), channel_id=1, source_target_pairs={{0,4},{4,0},{8,12},{12,8},{16,20},{20,16},{24,28},{28,24},{1,5},{5... | collective-permute-start | bytes 1769480 | tf_op jit(solution)/shard_map/ppermute | solution.py:240
  3.1 4.8 %collective-permute-start = (bf16[5,24,128]{2,1,0:T(8,128)(2,1)}, bf16[5,24,128]{2,1,0:T(8,128)(2,1)S(1)}, u32[]{:S(2)}, u32[]{:S(2)}) collective-permute-start(bf16[5,24,128]{2,1,0:T(8,128)(2,1)} %get-tuple-element.29.heads_in), channel_id=1, source_target_pairs={{0,8},{4,12},{8,0},{12,4},{16,24},{20,28},{24,16},{28,20},{1,9},{5... | collective-permute-start | bytes 92168 | tf_op jit(solution)/shard_map/ppermute | solution.py:240
  5.7 5.0 %collective-permute-start.2 = (bf16[5,24,128]{2,1,0:T(8,128)(2,1)}, bf16[5,24,128]{2,1,0:T(8,128)(2,1)S(1)}, u32[]{:S(2)}, u32[]{:S(2)}) collective-permute-start(bf16[5,24,128]{2,1,0:T(8,128)(2,1)} %get-tuple-element.29.heads_in), channel_id=1, source_target_pairs={{0,24},{4,28},{8,16},{12,20},{16,8},{20,12},{24,0},{28,4},{1,25},{... | collective-permute-start | bytes 92168 | tf_op jit(solution)/shard_map/ppermute | solution.py:240
  7.2 4.1 %collective-permute-start.1 = (bf16[5,24,128]{2,1,0:T(8,128)(2,1)}, bf16[5,24,128]{2,1,0:T(8,128)(2,1)S(1)}, u32[]{:S(2)}, u32[]{:S(2)}) collective-permute-start(bf16[5,24,128]{2,1,0:T(8,128)(2,1)} %get-tuple-element.29.heads_in), channel_id=1, source_target_pairs={{0,16},{4,20},{8,24},{12,28},{16,0},{20,4},{24,8},{28,12},{1,17},{... | collective-permute-start | bytes 92168 | tf_op jit(solution)/shard_map/ppermute | solution.py:240
  7.9 4.6 %collective-permute-start.3 = (bf16[5,24,128]{2,1,0:T(8,128)(2,1)}, bf16[5,24,128]{2,1,0:T(8,128)(2,1)S(1)}, u32[]{:S(2)}, u32[]{:S(2)}) collective-permute-start(bf16[5,24,128]{2,1,0:T(8,128)(2,1)} %get-tuple-element.29.heads_in), channel_id=1, source_target_pairs={{0,4},{4,0},{8,12},{12,8},{16,20},{20,16},{24,28},{28,24},{1,5},{5... | collective-permute-start | bytes 92168 | tf_op jit(solution)/shard_map/ppermute | solution.py:240
  11.3 1.4 %collective-permute-start.4 = (bf16[5,24,128]{2,1,0:T(8,128)(2,1)S(1)}, bf16[5,24,128]{2,1,0:T(8,128)(2,1)S(1)}, u32[]{:S(2)}, u32[]{:S(2)}) collective-permute-start(bf16[5,24,128]{2,1,0:T(8,128)(2,1)S(1)} %collective-permute-done.refs_1_), channel_id=1, source_target_pairs={{0,4},{4,0},{8,12},{12,8},{16,20},{20,16},{24,28},{28,24},{1,5},{5... | collective-permute-start | bytes 92168 | tf_op jit(solution)/shard_map/ppermute | solution.py:240
  13.7 5.5 %collective-permute-start.7 = (bf16[72,640]{1,0:T(8,128)(2,1)S(1)}, bf16[72,640]{1,0:T(8,128)(2,1)S(1)}, u32[]{:S(2)}, u32[]{:S(2)}) collective-permute-start(bf16[72,640]{1,0:T(8,128)(2,1)S(1)} %shard_map.129.refs_0_), channel_id=1, source_target_pairs={{0,8},{4,12},{8,0},{12,4},{16,24},{20,28},{24,16},{28,20},{1,9},{5... | collective-permute-start | bytes 276488 | tf_op jit(solution)/shard_map/ppermute | solution.py:240
  15.3 6.0 %collective-permute-start.9 = (bf16[72,640]{1,0:T(8,128)(2,1)S(1)}, bf16[72,640]{1,0:T(8,128)(2,1)S(1)}, u32[]{:S(2)}, u32[]{:S(2)}) collective-permute-start(bf16[72,640]{1,0:T(8,128)(2,1)S(1)} %shard_map.129.refs_0_), channel_id=1, source_target_pairs={{0,24},{4,28},{8,16},{12,20},{16,8},{20,12},{24,0},{28,4},{1,25},{... | collective-permute-start | bytes 276488 | tf_op jit(solution)/shard_map/ppermute | solution.py:240
  16.5 6.1 %collective-permute-start.8 = (bf16[72,640]{1,0:T(8,128)(2,1)S(1)}, bf16[72,640]{1,0:T(8,128)(2,1)S(1)}, u32[]{:S(2)}, u32[]{:S(2)}) collective-permute-start(bf16[72,640]{1,0:T(8,128)(2,1)S(1)} %shard_map.129.refs_0_), channel_id=1, source_target_pairs={{0,16},{4,20},{8,24},{12,28},{16,0},{20,4},{24,8},{28,12},{1,17},{... | collective-permute-start | bytes 276488 | tf_op jit(solution)/shard_map/ppermute | solution.py:240
  17.3 5.9 %collective-permute-start.10 = (bf16[72,640]{1,0:T(8,128)(2,1)S(1)}, bf16[72,640]{1,0:T(8,128)(2,1)S(1)}, u32[]{:S(2)}, u32[]{:S(2)}) collective-permute-start(bf16[72,640]{1,0:T(8,128)(2,1)S(1)} %shard_map.129.refs_0_), channel_id=1, source_target_pairs={{0,4},{4,0},{8,12},{12,8},{16,20},{20,16},{24,28},{28,24},{1,5},{5... | collective-permute-start | bytes 276488 | tf_op jit(solution)/shard_map/ppermute | solution.py:240
  21.2 1.9 %collective-permute-start.13 = (bf16[72,640]{1,0:T(8,128)(2,1)S(1)}, bf16[72,640]{1,0:T(8,128)(2,1)S(1)}, u32[]{:S(2)}, u32[]{:S(2)}) collective-permute-start(bf16[72,640]{1,0:T(8,128)(2,1)S(1)} %collective-permute-done.9.refs_3_), channel_id=1, source_target_pairs={{0,4},{4,0},{8,12},{12,8},{16,20},{20,16},{24,28},{28,24},{1,5},{5... | collective-permute-start | bytes 276488 | tf_op jit(solution)/shard_map/ppermute | solution.py:240
  22.7 1.3 %collective-permute-start.12 = (bf16[72,640]{1,0:T(8,128)(2,1)S(1)}, bf16[72,640]{1,0:T(8,128)(2,1)S(1)}, u32[]{:S(2)}, u32[]{:S(2)}) collective-permute-start(bf16[72,640]{1,0:T(8,128)(2,1)S(1)} %collective-permute-done.8.refs_2_), channel_id=1, source_target_pairs={{0,4},{4,0},{8,12},{12,8},{16,20},{20,16},{24,28},{28,24},{1,5},{5... | collective-permute-start | bytes 276488 | tf_op jit(solution)/shard_map/ppermute | solution.py:240
  22.7 1.4 %collective-permute-start.11 = (bf16[72,640]{1,0:T(8,128)(2,1)S(1)}, bf16[72,640]{1,0:T(8,128)(2,1)S(1)}, u32[]{:S(2)}, u32[]{:S(2)}) collective-permute-start(bf16[72,640]{1,0:T(8,128)(2,1)S(1)} %collective-permute-done.7.refs_1_), channel_id=1, source_target_pairs={{0,4},{4,0},{8,12},{12,8},{16,20},{20,16},{24,28},{28,24},{1,5},{5... | collective-permute-start | bytes 276488 | tf_op jit(solution)/shard_map/ppermute | solution.py:240
  26.0 5.1 %collective-permute-start.16 = (bf16[24,512]{1,0:T(8,128)(2,1)S(1)}, bf16[24,512]{1,0:T(8,128)(2,1)S(1)}, u32[]{:S(2)}, u32[]{:S(2)}) collective-permute-start(bf16[24,512]{1,0:T(8,128)(2,1)S(1)} %get-tuple-element.38), channel_id=1, source_target_pairs={{0,12},{1,4},{2,28},{3,20},{4,24},{5,16},{6,8},{7,0},{8,13},{9,5},... | collective-permute-start | bytes 73736 | tf_op jit(solution)/shard_map/ppermute | solution.py:699
  27.2 4.2 %collective-permute-start.15 = (bf16[24,512]{1,0:T(8,128)(2,1)S(1)}, bf16[24,512]{1,0:T(8,128)(2,1)S(1)}, u32[]{:S(2)}, u32[]{:S(2)}) collective-permute-start(bf16[24,512]{1,0:T(8,128)(2,1)S(1)} %get-tuple-element.38), channel_id=1, source_target_pairs={{0,4},{1,12},{2,20},{3,28},{4,16},{5,24},{6,0},{7,8},{8,5},{9,13},... | collective-permute-start | bytes 73736 | tf_op jit(solution)/shard_map/ppermute | solution.py:699
  33.6 9.2 %collective-permute-start.19 = (bf16[48,1152]{1,0:T(8,128)(2,1)S(1)}, bf16[48,1152]{1,0:T(8,128)(2,1)S(1)}, u32[]{:S(2)}, u32[]{:S(2)}) collective-permute-start(bf16[48,1152]{1,0:T(8,128)(2,1)S(1)} %get-tuple-element.40), channel_id=1, source_target_pairs={{0,3},{1,2},{2,1},{3,0},{4,7},{5,6},{6,5},{7,4},{8,11},{9,10},{10,... | collective-permute-start | bytes 331784 | tf_op jit(solution)/shard_map/ppermute | solution.py:240
  38.9 7.7 %collective-permute-start.20 = (bf16[48,1152]{1,0:T(8,128)(2,1)S(1)}, bf16[48,1152]{1,0:T(8,128)(2,1)S(1)}, u32[]{:S(2)}, u32[]{:S(2)}) collective-permute-start(bf16[48,1152]{1,0:T(8,128)(2,1)S(1)} %get-tuple-element.41), channel_id=1, source_target_pairs={{0,1},{1,0},{2,3},{3,2},{4,5},{5,4},{6,7},{7,6},{8,9},{9,8},{10,11... | collective-permute-start | bytes 331784 | tf_op jit(solution)/shard_map/ppermute | solution.py:240
  38.9 9.2 %collective-permute-start.21 = (bf16[48,1152]{1,0:T(8,128)(2,1)S(1)}, bf16[48,1152]{1,0:T(8,128)(2,1)S(1)}, u32[]{:S(2)}, u32[]{:S(2)}) collective-permute-start(bf16[48,1152]{1,0:T(8,128)(2,1)S(1)} %get-tuple-element.42), channel_id=1, source_target_pairs={{0,2},{1,3},{2,0},{3,1},{4,6},{5,7},{6,4},{7,5},{8,10},{9,11},{10,... | collective-permute-start | bytes 331784 | tf_op jit(solution)/shard_map/ppermute | solution.py:240
  48.3 6.5 %collective-permute-start.24 = (bf16[48,512]{1,0:T(8,128)(2,1)S(1)}, bf16[48,512]{1,0:T(8,128)(2,1)S(1)}, u32[]{:S(2)}, u32[]{:S(2)}) collective-permute-start(bf16[48,512]{1,0:T(8,128)(2,1)S(1)} %shard_map.133.refs_0_), channel_id=1, source_target_pairs={{0,3},{1,2},{2,1},{3,0},{4,7},{5,6},{6,5},{7,4},{8,11},{9,10},{10,... | collective-permute-start | bytes 147464 | tf_op jit(solution)/shard_map/ppermute | solution.py:240
  49.3 6.1 %collective-permute-start.23 = (bf16[48,512]{1,0:T(8,128)(2,1)S(1)}, bf16[48,512]{1,0:T(8,128)(2,1)S(1)}, u32[]{:S(2)}, u32[]{:S(2)}) collective-permute-start(bf16[48,512]{1,0:T(8,128)(2,1)S(1)} %shard_map.133.refs_0_), channel_id=1, source_target_pairs={{0,2},{1,3},{2,0},{3,1},{4,6},{5,7},{6,4},{7,5},{8,10},{9,11},{10,... | collective-permute-start | bytes 147464 | tf_op jit(solution)/shard_map/ppermute | solution.py:240
  50.3 5.2 %collective-permute-start.22 = (bf16[48,512]{1,0:T(8,128)(2,1)S(1)}, bf16[48,512]{1,0:T(8,128)(2,1)S(1)}, u32[]{:S(2)}, u32[]{:S(2)}) collective-permute-start(bf16[48,512]{1,0:T(8,128)(2,1)S(1)} %shard_map.133.refs_0_), channel_id=1, source_target_pairs={{0,1},{1,0},{2,3},{3,2},{4,5},{5,4},{6,7},{7,6},{8,9},{9,8},{10,11... | collective-permute-start | bytes 147464 | tf_op jit(solution)/shard_map/ppermute | solution.py:240
  57.6 3.3 %collective-permute-start.26 = (bf16[24,384]{1,0:T(8,128)(2,1)S(1)}, bf16[24,384]{1,0:T(8,128)(2,1)S(1)}, u32[]{:S(2)}, u32[]{:S(2)}) collective-permute-start(bf16[24,384]{1,0:T(8,128)(2,1)S(1)} %get-tuple-element.47), channel_id=1, source_target_pairs={{0,4},{1,12},{2,20},{3,28},{4,2},{5,10},{6,18},{7,26},{8,5},{9,13}... | collective-permute-start | bytes 55304 | tf_op jit(solution)/shard_map/ppermute | solution.py:729
  57.8 5.0 %collective-permute-start.27 = (bf16[24,384]{1,0:T(8,128)(2,1)S(1)}, bf16[24,384]{1,0:T(8,128)(2,1)S(1)}, u32[]{:S(2)}, u32[]{:S(2)}) collective-permute-start(bf16[24,384]{1,0:T(8,128)(2,1)S(1)} %get-tuple-element.48), channel_id=1, source_target_pairs={{0,5},{1,13},{2,21},{3,29},{4,3},{5,11},{6,19},{7,27},{8,4},{9,12}... | collective-permute-start | bytes 55304 | tf_op jit(solution)/shard_map/ppermute | solution.py:729
  62.9 3.6 %collective-permute-start.28 = (f32[24,192]{1,0:T(8,128)S(1)}, f32[24,192]{1,0:T(8,128)S(1)}, u32[]{:S(2)}, u32[]{:S(2)}) collective-permute-start(f32[24,192]{1,0:T(8,128)S(1)} %get-tuple-element.50), channel_id=1, source_target_pairs={{0,4},{4,0},{8,12},{12,8},{16,20},{20,16},{24,28},{28,24},{1,5},{5... | collective-permute-start | bytes 55304 | tf_op jit(solution)/shard_map/ppermute | solution.py:240
  (17 other events, 165.1 us)

commit v6 on v5

--- a/solution.py
+++ b/solution.py
@@ -19,6 +19,7 @@
 KVD = 512
 GROUP = 3
 CAP = 12
+MASKS = ((3, 2), (1, 0))
 
 
 EPS = 1e-05
@@ -269,7 +270,9 @@
     sine = jnp.where(lane % HD < HD // 2, -jnp.sin(angle), jnp.sin(angle))
     loads[1].wait()
     x = rows_of(x_in)
-    x_ref[...] = x
+    width = x_ref.shape[1]
+    own = pl.ds(pl.multiple_of((lax.axis_index("seq") // 2) * width, STAT), width)
+    x_ref[...] = jnp.concatenate([x_in[r, :, own].astype(F32) for r in range(requests)], axis=0)
     power = jnp.mean(x * x, axis=-1, keepdims=True)
     loads[2].wait()
     normed = (x * lax.rsqrt(power + EPS) * attn_gain[...].reshape(1, D)).astype(BF16)
@@ -441,15 +444,14 @@
     inverse = 1.0 / denominator
     row_total = parts[0].shape[0]
     row_count = row_total // GROUP
-    left = iota((row_total, STAT), 1) < HD
-    columns = []
-    for m in range(KVH // 2):
-        value = jnp.zeros((row_total, STAT), F32)
-        for part, factor in zip(parts, factors):
-            spread = jnp.where(left, factor[:, 2 * m : 2 * m + 1], factor[:, 2 * m + 1 : 2 * m + 2])
-            value = value + spread * part[:, m * STAT : (m + 1) * STAT]
-        spread = jnp.where(left, inverse[:, 2 * m : 2 * m + 1], inverse[:, 2 * m + 1 : 2 * m + 2])
-        columns.append(value * spread)
+    owner = iota((STAT, KVD), 1) // HD == iota((STAT, KVD), 0)
+    spread = jnp.where(owner, 1.0, 0.0).astype(BF16)
+    valid = iota((row_total, STAT), 1) < KVH
+    merged = jnp.zeros((row_total, KVD), F32)
+    for part, factor in zip(parts, factors):
+        weight = jnp.where(valid, factor * inverse, 0.0).astype(BF16)
+        merged = merged + jnp.dot(weight, spread, preferred_element_type=F32) * part[:, :KVD]
+    columns = [merged[:, m * STAT : (m + 1) * STAT] for m in range(KVH // 2)]
 
     def head(h, side):
         k, g = h // GROUP, h % GROUP
@@ -464,7 +466,7 @@
     width = near_w.shape[0]
     member = lax.axis_index("seq")
     both = pl.ds(pl.multiple_of((member // 2) * (2 * width), STAT), 2 * width)
-    resid = x_ref[:, both] + share
+    resid = x_ref[...] + share
     resid_ref[...] = jnp.where(member % 2 == 0, resid[:, :width], resid[:, width:])
     stats = routing_ref[...]
     lane = iota(stats.shape, 1)
@@ -506,12 +508,19 @@
     )
     slots = groups * CAP
     shape = (slots, tokens)
-    home = (iota(shape, 1) // row_count) ^ (member // 2)
+    block = iota(shape, 1) // row_count
+    home = jnp.zeros(shape, jnp.int32)
+    for b, mask in enumerate((3, 2, 1, 0)):
+        home = jnp.where(block == b, mask ^ (member // 2), home)
     slot = iota(shape, 0)
     same_group = slot // CAP == home
     ordinal_of_slot = (slot % CAP).astype(F32)
-    placed, scales, powers = [], [], []
-    power_row = across(power, eye)
+    placed, scales = [], []
+    row = iota((16, tokens), 0)
+    power_rows = jnp.zeros((16, tokens), F32)
+    for i, part in enumerate(split3(across(power, eye))):
+        power_rows = jnp.where(row == i, part, power_rows)
+    power_rows = power_rows.astype(BF16)
     for e in range(experts):
         match = chosen == (member * experts + e).astype(F32)
         routed = jnp.max(jnp.where(match, 1.0, 0.0), axis=1, keepdims=True)
@@ -520,35 +529,39 @@
         here = same_group & (across(routed, eye) > 0.5) & (ordinal_of_slot == ordinal)
         placed.append(jnp.where(here, 1.0, 0.0))
         scales.append(jnp.sum(jnp.where(here, across(scale, eye), 0.0), axis=1, keepdims=True))
-        powers.append(jnp.sum(jnp.where(here, power_row, 0.0), axis=1, keepdims=True))
-    lane = iota((slots, STAT), 1)
     all_placed = jnp.concatenate(placed, axis=0).astype(BF16)
     taken = jnp.dot(all_placed, mixed, preferred_element_type=F32).astype(BF16)
     for e in range(experts):
         rows = slice(e * slots, (e + 1) * slots)
         placed_ref[e] = all_placed[rows]
         scale_ref[e] = jnp.broadcast_to(scales[e], scale_ref.shape[1:])
-        full_ref[e, :, : 2 * FFE] = jnp.dot(
-            taken[rows], w_ref[e], preferred_element_type=F32
-        ).astype(BF16)
-        high, middle, low = split3(powers[e])
-        full_ref[e, :, 2 * FFE :] = jnp.where(
-            lane == 0, high, jnp.where(lane == 1, middle, jnp.where(lane == 2, low, 0.0))
+        gate_up = jnp.dot(taken[rows], w_ref[e], preferred_element_type=F32).astype(BF16)
+        for j in range(2 * FFE // STAT):
+            full_ref[e, j * slots : (j + 1) * slots, :] = gate_up[:, j * STAT : (j + 1) * STAT]
+        slot_power = dot_nt(power_rows, placed_ref[e])
+        full_ref[e, 2 * FFE // STAT * slots :, :] = jnp.concatenate(
+            [slot_power, jnp.zeros((16, STAT - slots), F32)], axis=1
         ).astype(BF16)
     for k in range(groups):
         message_refs[k][...] = full_ref[me ^ k]
 
 
 def hidden_kernel(*refs):
+    out_ref = refs[-1]
     gate_up = refs[0][...].astype(F32)
     for ref in refs[1:-1]:
         gate_up = gate_up + ref[...].astype(F32)
-    power = gate_up[:, 2 * FFE : 2 * FFE + 1] + (
-        gate_up[:, 2 * FFE + 1 : 2 * FFE + 2] + gate_up[:, 2 * FFE + 2 : 2 * FFE + 3]
-    )
-    gate_up = gate_up[:, : 2 * FFE] * lax.rsqrt(power / D + EPS)
-    gate, up = gate_up[:, :FFE], gate_up[:, FFE:]
-    refs[-1][...] = (gate / (1.0 + jnp.exp(-gate)) * up).astype(BF16)
+    slots = out_ref.shape[0]
+    chunks = FFE // STAT
+    stats = gate_up[2 * chunks * slots :, :slots]
+    power = stats[0:1] + (stats[1:2] + stats[2:3])
+    eye = iota((slots, slots), 0) == iota((slots, slots), 1)
+    power = jnp.sum(jnp.where(eye, power, 0.0), axis=1, keepdims=True)
+    scale = lax.rsqrt(power / D + EPS)
+    for j in range(chunks):
+        gate = gate_up[j * slots : (j + 1) * slots] * scale
+        up = gate_up[(chunks + j) * slots : (chunks + j + 1) * slots] * scale
+        out_ref[:, j * STAT : (j + 1) * STAT] = (gate / (1.0 + jnp.exp(-gate)) * up).astype(BF16)
 
 
 def down_kernel(groups, *refs):
@@ -621,7 +634,7 @@
     heads_shape = jax.ShapeDtypeStruct((heads, row_count, 2 * HD), BF16)
     own_heads, x = kernel_call(
         project_kernel,
-        [heads_shape, jax.ShapeDtypeStruct((row_count, D), F32)],
+        [heads_shape, jax.ShapeDtypeStruct((row_count, 2 * width), F32)],
         [HBM] * 4,
         [
             pltpu.VMEM(x_in.shape, BF16),
@@ -685,13 +698,13 @@
 
     def crossing(j):
         return [
-            ((2 * p + c) * groups + q, (2 * (q ^ (2 * c + j)) + 1 - c) * groups + p)
+            ((2 * p + c) * groups + q, (2 * (q ^ MASKS[c][j]) + 1 - c) * groups + p)
             for p, c, q in everyone
         ]
 
     def returning(j):
         return [
-            ((2 * p + c) * groups + q, (2 * q + 1 - c) * groups + (p ^ (2 * c + j)))
+            ((2 * p + c) * groups + q, (2 * q + 1 - c) * groups + (p ^ MASKS[c][j]))
             for p, c, q in everyone
         ]
 
@@ -700,15 +713,16 @@
     far = [swap(piece, "seq", 1) for piece in near]
     experts = w_gate_up.shape[0]
     slots = groups * CAP
+    message = jax.ShapeDtypeStruct((2 * FFE // STAT * slots + 16, STAT), BF16)
     *messages, placed, scale = kernel_call(
         lambda *refs: gate_kernel(groups, *refs),
-        [jax.ShapeDtypeStruct((slots, 2 * FFE + STAT), BF16)] * groups
+        [message] * groups
         + [
             jax.ShapeDtypeStruct((experts, slots, groups * row_count), BF16),
             jax.ShapeDtypeStruct((experts, slots, STAT), F32),
         ],
         [VMEM] * (groups + 1),
-        [pltpu.VMEM((experts, slots, 2 * FFE + STAT), BF16)],
+        [pltpu.VMEM((experts, *message.shape), BF16)],
     )(*near, *far, w_gate_up)
     sums = [messages[0]] + [swap(messages[k], "req", k) for k in (3, 1, 2)]
     hidden = kernel_call(

time: 67.3 us -> 65 us (0.966)
  waiting for transfers between devices: 29.4 us -> 25.6 us
  starting transfers between devices: 26.7 us -> 28.5 us
  Pallas kernels: 10.1 us -> 9.15 us
    ppermute x25, starting transfers between devices: 22.7 us -> 18.7 us  [swap(): return lax.ppermute(value, axis, pairs)]
    ppermute x2, starting transfers between devices: 2 us -> 5.74 us  [staged(): lax.ppermute(packed, place, crossing(j))]
    ppermute x2, starting transfers between devices: 2.02 us -> 4.12 us  [staged(): lax.ppermute(out, place, returning(j))]
    ppermute x2, waiting for transfers between devices: 3.4 us -> 1.52 us  [staged(): lax.ppermute(packed, place, crossing(j))]
    ppermute x2, waiting for transfers between devices: 3.15 us -> 1.46 us  [staged(): lax.ppermute(out, place, returning(j))]
    pallas_call x1, Pallas kernels: 1.92 us -> 1.21 us  [staged(): kernel_call(lambda *refs: merge_kernel(members + 1, *refs), [jax.ShapeDty...]
  transfers between devices with their start and end apart: 29 -> 29, of which waited for: 24 -> 21; matrix products, arithmetic and copies ran while one was open for 0% -> 0% of each run, Pallas kernels for 8% -> 8%
where the time goes in v6:
time: 65 us; the launch traced here: 64.3 us
  starting transfers between devices  28.5 us (44%)
  waiting for transfers between devices  25.6 us (39%)
  Pallas kernels  9.15 us (14%)
  local copies, waits for them, and re-layouts  0.79 us (1%)
    ppermute x25, waiting for transfers between devices, swap(): return lax.ppermute(value, axis, pairs)  22.6 us
    ppermute x25, starting transfers between devices, swap(): return lax.ppermute(value, axis, pairs)  18.7 us
    ppermute x2, starting transfers between devices, staged(): lax.ppermute(packed, place, crossing(j))  5.74 us
    ppermute x2, starting transfers between devices, staged(): lax.ppermute(out, place, returning(j))  4.12 us
    pallas_call x1, Pallas kernels, staged(): kernel_call(project_kernel, [heads_shape, jax.ShapeDtypeStruct((row_count...  2.58 us
    ppermute x2, waiting for transfers between devices, staged(): lax.ppermute(packed, place, crossing(j))  1.52 us
    ppermute x2, waiting for transfers between devices, staged(): lax.ppermute(out, place, returning(j))  1.46 us
  transfers between devices with their start and end apart: 29, of which 21 were waited for; matrix products, arithmetic and copies ran while one was open for 0% of the time, Pallas kernels for 8%

profile of v6, /device:TPU:0, one launch (start us, length us, event | category | flops | bytes accessed | tf_op | source)
XLA Modules:
  0.0 64.3 jit_solution(11338907067207724914)
XLA Ops:
  0.5 2.6 %shard_map.127 = (bf16[5,24,128]{2,1,0:T(8,128)(2,1)}, f32[24,384]{1,0:T(8,128)}) custom-call(bf16[6,4,1536]{2,1,0:T(4,128)(2,1)} %refs_0_.1, f32[1536]{0:T(1024)} %refs_1_.1, bf16[320,1536]{1,0:T(8,128)(2,1)} %bitcast.4, s32[6]{0:T(128)} %lengths.1), custom_call_target="tpu_custom_call" | custom-call | flops 5000000000 | bytes 15000000 | tf_op jit(solution)/shard_map/pallas_call | solution.py:635
  3.1 2.6 %collective-permute-start = (bf16[5,24,128]{2,1,0:T(8,128)(2,1)}, bf16[5,24,128]{2,1,0:T(8,128)(2,1)S(1)}, u32[]{:S(2)}, u32[]{:S(2)}) collective-permute-start(bf16[5,24,128]{2,1,0:T(8,128)(2,1)} %get-tuple-element.29.heads_in), channel_id=1, source_target_pairs={{0,8},{4,12},{8,0},{12,4},{16,24},{20,28},{24,16},{28,20},{1,9},{5... | collective-permute-start | bytes 92168 | tf_op jit(solution)/shard_map/ppermute | solution.py:241
  5.7 1.5 %collective-permute-start.2 = (bf16[5,24,128]{2,1,0:T(8,128)(2,1)}, bf16[5,24,128]{2,1,0:T(8,128)(2,1)S(1)}, u32[]{:S(2)}, u32[]{:S(2)}) collective-permute-start(bf16[5,24,128]{2,1,0:T(8,128)(2,1)} %get-tuple-element.29.heads_in), channel_id=1, source_target_pairs={{0,24},{4,28},{8,16},{12,20},{16,8},{20,12},{24,0},{28,4},{1,25},{... | collective-permute-start | bytes 92168 | tf_op jit(solution)/shard_map/ppermute | solution.py:241
  9.4 1.3 %collective-permute-done.2.refs_3_ = bf16[5,24,128]{2,1,0:T(8,128)(2,1)S(1)} collective-permute-done((bf16[5,24,128]{2,1,0:T(8,128)(2,1)}, bf16[5,24,128]{2,1,0:T(8,128)(2,1)S(1)}, u32[]{:S(2)}, u32[]{:S(2)}) %collective-permute-start.2) | collective-permute-done | bytes 30752 | tf_op jit(solution)/shard_map/ppermute | solution.py:241
  13.7 1.6 %collective-permute-start.7 = (bf16[72,640]{1,0:T(8,128)(2,1)S(1)}, bf16[72,640]{1,0:T(8,128)(2,1)S(1)}, u32[]{:S(2)}, u32[]{:S(2)}) collective-permute-start(bf16[72,640]{1,0:T(8,128)(2,1)S(1)} %shard_map.129.refs_0_), channel_id=1, source_target_pairs={{0,8},{4,12},{8,0},{12,4},{16,24},{20,28},{24,16},{28,20},{1,9},{5... | collective-permute-start | bytes 276488 | tf_op jit(solution)/shard_map/ppermute | solution.py:241
  15.3 1.3 %collective-permute-start.9 = (bf16[72,640]{1,0:T(8,128)(2,1)S(1)}, bf16[72,640]{1,0:T(8,128)(2,1)S(1)}, u32[]{:S(2)}, u32[]{:S(2)}) collective-permute-start(bf16[72,640]{1,0:T(8,128)(2,1)S(1)} %shard_map.129.refs_0_), channel_id=1, source_target_pairs={{0,24},{4,28},{8,16},{12,20},{16,8},{20,12},{24,0},{28,4},{1,25},{... | collective-permute-start | bytes 276488 | tf_op jit(solution)/shard_map/ppermute | solution.py:241
  19.2 2.0 %collective-permute-done.9.refs_3_ = bf16[72,640]{1,0:T(8,128)(2,1)S(1)} collective-permute-done((bf16[72,640]{1,0:T(8,128)(2,1)S(1)}, bf16[72,640]{1,0:T(8,128)(2,1)S(1)}, u32[]{:S(2)}, u32[]{:S(2)}) %collective-permute-start.9) | collective-permute-done | bytes 92192 | tf_op jit(solution)/shard_map/ppermute | solution.py:241
  21.2 1.4 %collective-permute-done.8.refs_2_ = bf16[72,640]{1,0:T(8,128)(2,1)S(1)} collective-permute-done((bf16[72,640]{1,0:T(8,128)(2,1)S(1)}, bf16[72,640]{1,0:T(8,128)(2,1)S(1)}, u32[]{:S(2)}, u32[]{:S(2)}) %collective-permute-start.8) | collective-permute-done | bytes 92192 | tf_op jit(solution)/shard_map/ppermute | solution.py:241
  24.1 1.2 %shard_map.131 = (bf16[24,512]{1,0:T(8,128)(2,1)S(1)}, f32[24,192]{1,0:T(8,128)S(1)}) custom-call(bf16[72,640]{1,0:T(8,128)(2,1)S(1)} %shard_map.129.refs_0_, bf16[72,640]{1,0:T(8,128)(2,1)S(1)} %collective-permute-done.7.refs_1_, bf16[72,640]{1,0:T(8,128)(2,1)S(1)} %collective-permute-done.8.refs_2_, bf16[72,640]{1,0:T(8,128)(2,1)S(1)} %collective-permute-done.9.refs_3_, ...), custom_call_target="tpu_custom_call" | custom-call | flops 500000000 | bytes 1500000 | tf_op jit(solution)/shard_map/pallas_call | solution.py:688
  26.3 4.8 %collective-permute-start.15 = (bf16[24,512]{1,0:T(8,128)(2,1)S(1)}, bf16[24,512]{1,0:T(8,128)(2,1)S(1)}, u32[]{:S(2)}, u32[]{:S(2)}) collective-permute-start(bf16[24,512]{1,0:T(8,128)(2,1)S(1)} %get-tuple-element.38), channel_id=1, source_target_pairs={{0,28},{1,20},{2,12},{3,4},{4,8},{5,0},{6,24},{7,16},{8,29},{9,21}... | collective-permute-start | bytes 73736 | tf_op jit(solution)/shard_map/ppermute | solution.py:712
  31.1 1.5 %collective-permute-done.15.refs_0_ = bf16[24,512]{1,0:T(8,128)(2,1)S(1)} collective-permute-done((bf16[24,512]{1,0:T(8,128)(2,1)S(1)}, bf16[24,512]{1,0:T(8,128)(2,1)S(1)}, u32[]{:S(2)}, u32[]{:S(2)}) %collective-permute-start.15) | collective-permute-done | bytes 24608 | tf_op jit(solution)/shard_map/ppermute | solution.py:712
  32.6 1.2 %collective-permute-done.17.refs_2_ = bf16[24,512]{1,0:T(8,128)(2,1)S(1)} collective-permute-done((bf16[24,512]{1,0:T(8,128)(2,1)S(1)}, bf16[24,512]{1,0:T(8,128)(2,1)S(1)}, u32[]{:S(2)}, u32[]{:S(2)}) %collective-permute-start.17) | collective-permute-done | bytes 24608 | tf_op jit(solution)/shard_map/ppermute | solution.py:241
  34.6 4.3 %collective-permute-start.19 = (bf16[400,128]{1,0:T(8,128)(2,1)S(1)}, bf16[400,128]{1,0:T(8,128)(2,1)S(1)}, u32[]{:S(2)}, u32[]{:S(2)}) collective-permute-start(bf16[400,128]{1,0:T(8,128)(2,1)S(1)} %get-tuple-element.40), channel_id=1, source_target_pairs={{0,3},{1,2},{2,1},{3,0},{4,7},{5,6},{6,5},{7,4},{8,11},{9,10},{10,... | collective-permute-start | bytes 307208 | tf_op jit(solution)/shard_map/ppermute | solution.py:241
  39.6 3.1 %collective-permute-done.19.refs_1_ = bf16[400,128]{1,0:T(8,128)(2,1)S(1)} collective-permute-done((bf16[400,128]{1,0:T(8,128)(2,1)S(1)}, bf16[400,128]{1,0:T(8,128)(2,1)S(1)}, u32[]{:S(2)}, u32[]{:S(2)}) %collective-permute-start.19) | collective-permute-done | bytes 102432 | tf_op jit(solution)/shard_map/ppermute | solution.py:241
  42.7 3.7 %collective-permute-done.20.refs_2_ = bf16[400,128]{1,0:T(8,128)(2,1)S(1)} collective-permute-done((bf16[400,128]{1,0:T(8,128)(2,1)S(1)}, bf16[400,128]{1,0:T(8,128)(2,1)S(1)}, u32[]{:S(2)}, u32[]{:S(2)}) %collective-permute-start.20) | collective-permute-done | bytes 102432 | tf_op jit(solution)/shard_map/ppermute | solution.py:241
  47.0 1.9 %collective-permute-start.24 = (bf16[48,512]{1,0:T(8,128)(2,1)S(1)}, bf16[48,512]{1,0:T(8,128)(2,1)S(1)}, u32[]{:S(2)}, u32[]{:S(2)}) collective-permute-start(bf16[48,512]{1,0:T(8,128)(2,1)S(1)} %shard_map.133.refs_0_), channel_id=1, source_target_pairs={{0,3},{1,2},{2,1},{3,0},{4,7},{5,6},{6,5},{7,4},{8,11},{9,10},{10,... | collective-permute-start | bytes 147464 | tf_op jit(solution)/shard_map/ppermute | solution.py:241
  49.6 1.9 %collective-permute-start.22 = (bf16[48,512]{1,0:T(8,128)(2,1)S(1)}, bf16[48,512]{1,0:T(8,128)(2,1)S(1)}, u32[]{:S(2)}, u32[]{:S(2)}) collective-permute-start(bf16[48,512]{1,0:T(8,128)(2,1)S(1)} %shard_map.133.refs_0_), channel_id=1, source_target_pairs={{0,1},{1,0},{2,3},{3,2},{4,5},{5,4},{6,7},{7,6},{8,9},{9,8},{10,11... | collective-permute-start | bytes 147464 | tf_op jit(solution)/shard_map/ppermute | solution.py:241
  51.5 1.6 %collective-permute-done.24.refs_3_ = bf16[48,512]{1,0:T(8,128)(2,1)S(1)} collective-permute-done((bf16[48,512]{1,0:T(8,128)(2,1)S(1)}, bf16[48,512]{1,0:T(8,128)(2,1)S(1)}, u32[]{:S(2)}, u32[]{:S(2)}) %collective-permute-start.24) | collective-permute-done | bytes 49184 | tf_op jit(solution)/shard_map/ppermute | solution.py:241
  53.1 1.5 %collective-permute-done.23.refs_2_ = bf16[48,512]{1,0:T(8,128)(2,1)S(1)} collective-permute-done((bf16[48,512]{1,0:T(8,128)(2,1)S(1)}, bf16[48,512]{1,0:T(8,128)(2,1)S(1)}, u32[]{:S(2)}, u32[]{:S(2)}) %collective-permute-start.23) | collective-permute-done | bytes 49184 | tf_op jit(solution)/shard_map/ppermute | solution.py:241
  55.5 1.2 %collective-permute-done.25.arrived_ref = bf16[48,384]{1,0:T(8,128)(2,1)S(1)} collective-permute-done((bf16[48,384]{1,0:T(8,128)(2,1)S(1)}, bf16[48,384]{1,0:T(8,128)(2,1)S(1)}, u32[]{:S(2)}, u32[]{:S(2)}) %collective-permute-start.25) | collective-permute-done | bytes 36896 | tf_op jit(solution)/shard_map/ppermute | solution.py:241
  56.7 2.5 %collective-permute-start.26 = (bf16[24,384]{1,0:T(8,128)(2,1)S(1)}, bf16[24,384]{1,0:T(8,128)(2,1)S(1)}, u32[]{:S(2)}, u32[]{:S(2)}) collective-permute-start(bf16[24,384]{1,0:T(8,128)(2,1)S(1)} %get-tuple-element.47), channel_id=1, source_target_pairs={{0,7},{1,15},{2,23},{3,31},{4,1},{5,9},{6,17},{7,25},{8,6},{9,14},... | collective-permute-start | bytes 55304 | tf_op jit(solution)/shard_map/ppermute | solution.py:743
  59.2 1.7 %collective-permute-start.27 = (bf16[24,384]{1,0:T(8,128)(2,1)S(1)}, bf16[24,384]{1,0:T(8,128)(2,1)S(1)}, u32[]{:S(2)}, u32[]{:S(2)}) collective-permute-start(bf16[24,384]{1,0:T(8,128)(2,1)S(1)} %get-tuple-element.48), channel_id=1, source_target_pairs={{0,6},{1,14},{2,22},{3,30},{4,0},{5,8},{6,16},{7,24},{8,7},{9,15},... | collective-permute-start | bytes 55304 | tf_op jit(solution)/shard_map/ppermute | solution.py:743
  60.9 1.5 %collective-permute-done.27.refs_1_ = bf16[24,384]{1,0:T(8,128)(2,1)S(1)} collective-permute-done((bf16[24,384]{1,0:T(8,128)(2,1)S(1)}, bf16[24,384]{1,0:T(8,128)(2,1)S(1)}, u32[]{:S(2)}, u32[]{:S(2)}) %collective-permute-start.27) | collective-permute-done | bytes 18464 | tf_op jit(solution)/shard_map/ppermute | solution.py:743
  62.5 1.2 %collective-permute-done.28.arrived_ref = f32[24,192]{1,0:T(8,128)S(1)} collective-permute-done((f32[24,192]{1,0:T(8,128)S(1)}, f32[24,192]{1,0:T(8,128)S(1)}, u32[]{:S(2)}, u32[]{:S(2)}) %collective-permute-start.28) | collective-permute-done | bytes 18464 | tf_op jit(solution)/shard_map/ppermute | solution.py:241
  (69 shorter events, 15.2 us)
Async XLA Ops:
  0.0 24.1 %collective-permute-start.14 = (bf16[192,1536]{1,0:T(8,128)(2,1)}, bf16[192,1536]{1,0:T(8,128)(2,1)S(1)}, u32[]{:S(2)}, u32[]{:S(2)}) collective-permute-start(bf16[192,1536]{1,0:T(8,128)(2,1)} %bitcast.2), channel_id=1, source_target_pairs={{0,4},{4,0},{8,12},{12,8},{16,20},{20,16},{24,28},{28,24},{1,5},{5... | collective-permute-start | bytes 1769480 | tf_op jit(solution)/shard_map/ppermute | solution.py:241
  3.1 4.8 %collective-permute-start = (bf16[5,24,128]{2,1,0:T(8,128)(2,1)}, bf16[5,24,128]{2,1,0:T(8,128)(2,1)S(1)}, u32[]{:S(2)}, u32[]{:S(2)}) collective-permute-start(bf16[5,24,128]{2,1,0:T(8,128)(2,1)} %get-tuple-element.29.heads_in), channel_id=1, source_target_pairs={{0,8},{4,12},{8,0},{12,4},{16,24},{20,28},{24,16},{28,20},{1,9},{5... | collective-permute-start | bytes 92168 | tf_op jit(solution)/shard_map/ppermute | solution.py:241
  5.7 5.0 %collective-permute-start.2 = (bf16[5,24,128]{2,1,0:T(8,128)(2,1)}, bf16[5,24,128]{2,1,0:T(8,128)(2,1)S(1)}, u32[]{:S(2)}, u32[]{:S(2)}) collective-permute-start(bf16[5,24,128]{2,1,0:T(8,128)(2,1)} %get-tuple-element.29.heads_in), channel_id=1, source_target_pairs={{0,24},{4,28},{8,16},{12,20},{16,8},{20,12},{24,0},{28,4},{1,25},{... | collective-permute-start | bytes 92168 | tf_op jit(solution)/shard_map/ppermute | solution.py:241
  7.2 4.1 %collective-permute-start.1 = (bf16[5,24,128]{2,1,0:T(8,128)(2,1)}, bf16[5,24,128]{2,1,0:T(8,128)(2,1)S(1)}, u32[]{:S(2)}, u32[]{:S(2)}) collective-permute-start(bf16[5,24,128]{2,1,0:T(8,128)(2,1)} %get-tuple-element.29.heads_in), channel_id=1, source_target_pairs={{0,16},{4,20},{8,24},{12,28},{16,0},{20,4},{24,8},{28,12},{1,17},{... | collective-permute-start | bytes 92168 | tf_op jit(solution)/shard_map/ppermute | solution.py:241
  7.9 4.6 %collective-permute-start.3 = (bf16[5,24,128]{2,1,0:T(8,128)(2,1)}, bf16[5,24,128]{2,1,0:T(8,128)(2,1)S(1)}, u32[]{:S(2)}, u32[]{:S(2)}) collective-permute-start(bf16[5,24,128]{2,1,0:T(8,128)(2,1)} %get-tuple-element.29.heads_in), channel_id=1, source_target_pairs={{0,4},{4,0},{8,12},{12,8},{16,20},{20,16},{24,28},{28,24},{1,5},{5... | collective-permute-start | bytes 92168 | tf_op jit(solution)/shard_map/ppermute | solution.py:241
  11.3 1.4 %collective-permute-start.4 = (bf16[5,24,128]{2,1,0:T(8,128)(2,1)S(1)}, bf16[5,24,128]{2,1,0:T(8,128)(2,1)S(1)}, u32[]{:S(2)}, u32[]{:S(2)}) collective-permute-start(bf16[5,24,128]{2,1,0:T(8,128)(2,1)S(1)} %collective-permute-done.refs_1_), channel_id=1, source_target_pairs={{0,4},{4,0},{8,12},{12,8},{16,20},{20,16},{24,28},{28,24},{1,5},{5... | collective-permute-start | bytes 92168 | tf_op jit(solution)/shard_map/ppermute | solution.py:241
  13.7 5.5 %collective-permute-start.7 = (bf16[72,640]{1,0:T(8,128)(2,1)S(1)}, bf16[72,640]{1,0:T(8,128)(2,1)S(1)}, u32[]{:S(2)}, u32[]{:S(2)}) collective-permute-start(bf16[72,640]{1,0:T(8,128)(2,1)S(1)} %shard_map.129.refs_0_), channel_id=1, source_target_pairs={{0,8},{4,12},{8,0},{12,4},{16,24},{20,28},{24,16},{28,20},{1,9},{5... | collective-permute-start | bytes 276488 | tf_op jit(solution)/shard_map/ppermute | solution.py:241
  15.3 6.0 %collective-permute-start.9 = (bf16[72,640]{1,0:T(8,128)(2,1)S(1)}, bf16[72,640]{1,0:T(8,128)(2,1)S(1)}, u32[]{:S(2)}, u32[]{:S(2)}) collective-permute-start(bf16[72,640]{1,0:T(8,128)(2,1)S(1)} %shard_map.129.refs_0_), channel_id=1, source_target_pairs={{0,24},{4,28},{8,16},{12,20},{16,8},{20,12},{24,0},{28,4},{1,25},{... | collective-permute-start | bytes 276488 | tf_op jit(solution)/shard_map/ppermute | solution.py:241
  16.5 6.1 %collective-permute-start.8 = (bf16[72,640]{1,0:T(8,128)(2,1)S(1)}, bf16[72,640]{1,0:T(8,128)(2,1)S(1)}, u32[]{:S(2)}, u32[]{:S(2)}) collective-permute-start(bf16[72,640]{1,0:T(8,128)(2,1)S(1)} %shard_map.129.refs_0_), channel_id=1, source_target_pairs={{0,16},{4,20},{8,24},{12,28},{16,0},{20,4},{24,8},{28,12},{1,17},{... | collective-permute-start | bytes 276488 | tf_op jit(solution)/shard_map/ppermute | solution.py:241
  17.3 5.9 %collective-permute-start.10 = (bf16[72,640]{1,0:T(8,128)(2,1)S(1)}, bf16[72,640]{1,0:T(8,128)(2,1)S(1)}, u32[]{:S(2)}, u32[]{:S(2)}) collective-permute-start(bf16[72,640]{1,0:T(8,128)(2,1)S(1)} %shard_map.129.refs_0_), channel_id=1, source_target_pairs={{0,4},{4,0},{8,12},{12,8},{16,20},{20,16},{24,28},{28,24},{1,5},{5... | collective-permute-start | bytes 276488 | tf_op jit(solution)/shard_map/ppermute | solution.py:241
  21.2 1.9 %collective-permute-start.13 = (bf16[72,640]{1,0:T(8,128)(2,1)S(1)}, bf16[72,640]{1,0:T(8,128)(2,1)S(1)}, u32[]{:S(2)}, u32[]{:S(2)}) collective-permute-start(bf16[72,640]{1,0:T(8,128)(2,1)S(1)} %collective-permute-done.9.refs_3_), channel_id=1, source_target_pairs={{0,4},{4,0},{8,12},{12,8},{16,20},{20,16},{24,28},{28,24},{1,5},{5... | collective-permute-start | bytes 276488 | tf_op jit(solution)/shard_map/ppermute | solution.py:241
  22.7 1.3 %collective-permute-start.12 = (bf16[72,640]{1,0:T(8,128)(2,1)S(1)}, bf16[72,640]{1,0:T(8,128)(2,1)S(1)}, u32[]{:S(2)}, u32[]{:S(2)}) collective-permute-start(bf16[72,640]{1,0:T(8,128)(2,1)S(1)} %collective-permute-done.8.refs_2_), channel_id=1, source_target_pairs={{0,4},{4,0},{8,12},{12,8},{16,20},{20,16},{24,28},{28,24},{1,5},{5... | collective-permute-start | bytes 276488 | tf_op jit(solution)/shard_map/ppermute | solution.py:241
  22.7 1.4 %collective-permute-start.11 = (bf16[72,640]{1,0:T(8,128)(2,1)S(1)}, bf16[72,640]{1,0:T(8,128)(2,1)S(1)}, u32[]{:S(2)}, u32[]{:S(2)}) collective-permute-start(bf16[72,640]{1,0:T(8,128)(2,1)S(1)} %collective-permute-done.7.refs_1_), channel_id=1, source_target_pairs={{0,4},{4,0},{8,12},{12,8},{16,20},{20,16},{24,28},{28,24},{1,5},{5... | collective-permute-start | bytes 276488 | tf_op jit(solution)/shard_map/ppermute | solution.py:241
  25.3 5.7 %collective-permute-start.16 = (bf16[24,512]{1,0:T(8,128)(2,1)S(1)}, bf16[24,512]{1,0:T(8,128)(2,1)S(1)}, u32[]{:S(2)}, u32[]{:S(2)}) collective-permute-start(bf16[24,512]{1,0:T(8,128)(2,1)S(1)} %get-tuple-element.38), channel_id=1, source_target_pairs={{0,20},{1,28},{2,4},{3,12},{4,0},{5,8},{6,16},{7,24},{8,21},{9,29}... | collective-permute-start | bytes 73736 | tf_op jit(solution)/shard_map/ppermute | solution.py:712
  26.3 6.3 %collective-permute-start.15 = (bf16[24,512]{1,0:T(8,128)(2,1)S(1)}, bf16[24,512]{1,0:T(8,128)(2,1)S(1)}, u32[]{:S(2)}, u32[]{:S(2)}) collective-permute-start(bf16[24,512]{1,0:T(8,128)(2,1)S(1)} %get-tuple-element.38), channel_id=1, source_target_pairs={{0,28},{1,20},{2,12},{3,4},{4,8},{5,0},{6,24},{7,16},{8,29},{9,21}... | collective-permute-start | bytes 73736 | tf_op jit(solution)/shard_map/ppermute | solution.py:712
  31.1 1.5 %collective-permute-start.18 = (bf16[24,512]{1,0:T(8,128)(2,1)S(1)}, bf16[24,512]{1,0:T(8,128)(2,1)S(1)}, u32[]{:S(2)}, u32[]{:S(2)}) collective-permute-start(bf16[24,512]{1,0:T(8,128)(2,1)S(1)} %collective-permute-done.16.refs_1_), channel_id=1, source_target_pairs={{0,4},{4,0},{8,12},{12,8},{16,20},{20,16},{24,28},{28,24},{1,5},{5... | collective-permute-start | bytes 73736 | tf_op jit(solution)/shard_map/ppermute | solution.py:241
  34.6 8.0 %collective-permute-start.19 = (bf16[400,128]{1,0:T(8,128)(2,1)S(1)}, bf16[400,128]{1,0:T(8,128)(2,1)S(1)}, u32[]{:S(2)}, u32[]{:S(2)}) collective-permute-start(bf16[400,128]{1,0:T(8,128)(2,1)S(1)} %get-tuple-element.40), channel_id=1, source_target_pairs={{0,3},{1,2},{2,1},{3,0},{4,7},{5,6},{6,5},{7,4},{8,11},{9,10},{10,... | collective-permute-start | bytes 307208 | tf_op jit(solution)/shard_map/ppermute | solution.py:241
  39.0 7.4 %collective-permute-start.20 = (bf16[400,128]{1,0:T(8,128)(2,1)S(1)}, bf16[400,128]{1,0:T(8,128)(2,1)S(1)}, u32[]{:S(2)}, u32[]{:S(2)}) collective-permute-start(bf16[400,128]{1,0:T(8,128)(2,1)S(1)} %get-tuple-element.41), channel_id=1, source_target_pairs={{0,1},{1,0},{2,3},{3,2},{4,5},{5,4},{6,7},{7,6},{8,9},{9,8},{10,11... | collective-permute-start | bytes 307208 | tf_op jit(solution)/shard_map/ppermute | solution.py:241
  39.0 7.9 %collective-permute-start.21 = (bf16[400,128]{1,0:T(8,128)(2,1)S(1)}, bf16[400,128]{1,0:T(8,128)(2,1)S(1)}, u32[]{:S(2)}, u32[]{:S(2)}) collective-permute-start(bf16[400,128]{1,0:T(8,128)(2,1)S(1)} %get-tuple-element.42), channel_id=1, source_target_pairs={{0,2},{1,3},{2,0},{3,1},{4,6},{5,7},{6,4},{7,5},{8,10},{9,11},{10,... | collective-permute-start | bytes 307208 | tf_op jit(solution)/shard_map/ppermute | solution.py:241
  47.0 6.1 %collective-permute-start.24 = (bf16[48,512]{1,0:T(8,128)(2,1)S(1)}, bf16[48,512]{1,0:T(8,128)(2,1)S(1)}, u32[]{:S(2)}, u32[]{:S(2)}) collective-permute-start(bf16[48,512]{1,0:T(8,128)(2,1)S(1)} %shard_map.133.refs_0_), channel_id=1, source_target_pairs={{0,3},{1,2},{2,1},{3,0},{4,7},{5,6},{6,5},{7,4},{8,11},{9,10},{10,... | collective-permute-start | bytes 147464 | tf_op jit(solution)/shard_map/ppermute | solution.py:241
  49.0 5.6 %collective-permute-start.23 = (bf16[48,512]{1,0:T(8,128)(2,1)S(1)}, bf16[48,512]{1,0:T(8,128)(2,1)S(1)}, u32[]{:S(2)}, u32[]{:S(2)}) collective-permute-start(bf16[48,512]{1,0:T(8,128)(2,1)S(1)} %shard_map.133.refs_0_), channel_id=1, source_target_pairs={{0,2},{1,3},{2,0},{3,1},{4,6},{5,7},{6,4},{7,5},{8,10},{9,11},{10,... | collective-permute-start | bytes 147464 | tf_op jit(solution)/shard_map/ppermute | solution.py:241
  49.6 5.1 %collective-permute-start.22 = (bf16[48,512]{1,0:T(8,128)(2,1)S(1)}, bf16[48,512]{1,0:T(8,128)(2,1)S(1)}, u32[]{:S(2)}, u32[]{:S(2)}) collective-permute-start(bf16[48,512]{1,0:T(8,128)(2,1)S(1)} %shard_map.133.refs_0_), channel_id=1, source_target_pairs={{0,1},{1,0},{2,3},{3,2},{4,5},{5,4},{6,7},{7,6},{8,9},{9,8},{10,11... | collective-permute-start | bytes 147464 | tf_op jit(solution)/shard_map/ppermute | solution.py:241
  56.7 4.1 %collective-permute-start.26 = (bf16[24,384]{1,0:T(8,128)(2,1)S(1)}, bf16[24,384]{1,0:T(8,128)(2,1)S(1)}, u32[]{:S(2)}, u32[]{:S(2)}) collective-permute-start(bf16[24,384]{1,0:T(8,128)(2,1)S(1)} %get-tuple-element.47), channel_id=1, source_target_pairs={{0,7},{1,15},{2,23},{3,31},{4,1},{5,9},{6,17},{7,25},{8,6},{9,14},... | collective-permute-start | bytes 55304 | tf_op jit(solution)/shard_map/ppermute | solution.py:743
  59.2 3.1 %collective-permute-start.27 = (bf16[24,384]{1,0:T(8,128)(2,1)S(1)}, bf16[24,384]{1,0:T(8,128)(2,1)S(1)}, u32[]{:S(2)}, u32[]{:S(2)}) collective-permute-start(bf16[24,384]{1,0:T(8,128)(2,1)S(1)} %get-tuple-element.48), channel_id=1, source_target_pairs={{0,6},{1,14},{2,22},{3,30},{4,0},{5,8},{6,16},{7,24},{8,7},{9,15},... | collective-permute-start | bytes 55304 | tf_op jit(solution)/shard_map/ppermute | solution.py:743
  (17 other events, 165.4 us)

commit v7 on v6

--- a/solution.py
+++ b/solution.py
@@ -203,7 +203,7 @@
 HBM = pl.BlockSpec(memory_space=pltpu.HBM)
 
 
-def kernel_call(body, out_shape, in_specs, scratch=(), out_specs=None, vmem_mib=8, cost=0.5):
+def kernel_call(body, out_shape, in_specs, scratch=(), out_specs=None, vmem_mib=8, cost=2.0):
     return pl.pallas_call(
         body,
         out_shape=out_shape,
@@ -684,7 +684,7 @@
     )(*near, *far)
     near = gathered(part)
     near[1] = after(near[1], fresh)
-    far = [swap(piece, "seq", 1) for piece in [part] + near[1:]]
+    far = [swap(piece, "seq", 1) for piece in [after(part, near[1])] + near[1:]]
     packed, resid = kernel_call(
         lambda *refs: merge_kernel(members + 1, *refs),
         [

time: 65 us -> 64.1 us (0.986)
  waiting for transfers between devices: 25.6 us -> 24.6 us
    ppermute x25, waiting for transfers between devices: 22.6 us -> 21.6 us  [swap(): return lax.ppermute(value, axis, pairs)]
  transfers between devices with their start and end apart: 29 -> 29, of which waited for: 21 -> 22; matrix products, arithmetic and copies ran while one was open for 0% -> 0% of each run, Pallas kernels for 8% -> 4%
where the time goes in v7:
time: 64.1 us; the launch traced here: 63.3 us
  starting transfers between devices  28.7 us (45%)
  waiting for transfers between devices  24.6 us (38%)
  Pallas kernels  9.11 us (14%)
  local copies, waits for them, and re-layouts  0.79 us (1%)
    ppermute x25, waiting for transfers between devices, swap(): return lax.ppermute(value, axis, pairs)  21.6 us
    ppermute x25, starting transfers between devices, swap(): return lax.ppermute(value, axis, pairs)  19 us
    ppermute x2, starting transfers between devices, staged(): lax.ppermute(packed, place, crossing(j))  5.74 us
    ppermute x2, starting transfers between devices, staged(): lax.ppermute(out, place, returning(j))  3.94 us
    pallas_call x1, Pallas kernels, staged(): kernel_call(project_kernel, [heads_shape, jax.ShapeDtypeStruct((row_count...  2.51 us
    ppermute x2, waiting for transfers between devices, staged(): lax.ppermute(packed, place, crossing(j))  1.52 us
    ppermute x2, waiting for transfers between devices, staged(): lax.ppermute(out, place, returning(j))  1.46 us
  transfers between devices with their start and end apart: 29, of which 22 were waited for; matrix products, arithmetic and copies ran while one was open for 0% of the time, Pallas kernels for 4%

profile of v7, /device:TPU:0, one launch (start us, length us, event | category | flops | bytes accessed | tf_op | source)
XLA Modules:
  0.0 63.3 jit_solution(4069150503331633284)
XLA Ops:
  0.0 2.5 %shard_map.127 = (bf16[5,24,128]{2,1,0:T(8,128)(2,1)}, f32[24,384]{1,0:T(8,128)}) custom-call(bf16[6,4,1536]{2,1,0:T(4,128)(2,1)} %refs_0_.1, f32[1536]{0:T(1024)} %refs_1_.1, bf16[320,1536]{1,0:T(8,128)(2,1)} %bitcast.4, s32[6]{0:T(128)} %lengths.1), custom_call_target="tpu_custom_call" | custom-call | flops 5000000000 | bytes 15000000 | tf_op jit(solution)/shard_map/pallas_call | solution.py:635
  2.5 3.0 %collective-permute-start = (bf16[5,24,128]{2,1,0:T(8,128)(2,1)}, bf16[5,24,128]{2,1,0:T(8,128)(2,1)S(1)}, u32[]{:S(2)}, u32[]{:S(2)}) collective-permute-start(bf16[5,24,128]{2,1,0:T(8,128)(2,1)} %get-tuple-element.30.heads_in), channel_id=1, source_target_pairs={{0,8},{4,12},{8,0},{12,4},{16,24},{20,28},{24,16},{28,20},{1,9},{5... | collective-permute-start | bytes 92168 | tf_op jit(solution)/shard_map/ppermute | solution.py:241
  5.6 1.5 %collective-permute-start.2 = (bf16[5,24,128]{2,1,0:T(8,128)(2,1)}, bf16[5,24,128]{2,1,0:T(8,128)(2,1)S(1)}, u32[]{:S(2)}, u32[]{:S(2)}) collective-permute-start(bf16[5,24,128]{2,1,0:T(8,128)(2,1)} %get-tuple-element.30.heads_in), channel_id=1, source_target_pairs={{0,24},{4,28},{8,16},{12,20},{16,8},{20,12},{24,0},{28,4},{1,25},{... | collective-permute-start | bytes 92168 | tf_op jit(solution)/shard_map/ppermute | solution.py:241
  9.1 1.4 %collective-permute-done.2.refs_3_ = bf16[5,24,128]{2,1,0:T(8,128)(2,1)S(1)} collective-permute-done((bf16[5,24,128]{2,1,0:T(8,128)(2,1)}, bf16[5,24,128]{2,1,0:T(8,128)(2,1)S(1)}, u32[]{:S(2)}, u32[]{:S(2)}) %collective-permute-start.2) | collective-permute-done | bytes 30752 | tf_op jit(solution)/shard_map/ppermute | solution.py:241
  13.6 1.6 %collective-permute-start.9 = (bf16[72,640]{1,0:T(8,128)(2,1)S(1)}, bf16[72,640]{1,0:T(8,128)(2,1)S(1)}, u32[]{:S(2)}, u32[]{:S(2)}) collective-permute-start(bf16[72,640]{1,0:T(8,128)(2,1)S(1)} %shard_map.129.refs_0_), channel_id=1, source_target_pairs={{0,24},{4,28},{8,16},{12,20},{16,8},{20,12},{24,0},{28,4},{1,25},{... | collective-permute-start | bytes 276488 | tf_op jit(solution)/shard_map/ppermute | solution.py:241
  15.2 1.4 %collective-permute-start.8 = (bf16[72,640]{1,0:T(8,128)(2,1)S(1)}, bf16[72,640]{1,0:T(8,128)(2,1)S(1)}, u32[]{:S(2)}, u32[]{:S(2)}) collective-permute-start(bf16[72,640]{1,0:T(8,128)(2,1)S(1)} %shard_map.129.refs_0_), channel_id=1, source_target_pairs={{0,16},{4,20},{8,24},{12,28},{16,0},{20,4},{24,8},{28,12},{1,17},{... | collective-permute-start | bytes 276488 | tf_op jit(solution)/shard_map/ppermute | solution.py:241
  17.2 1.1 %shard_map.130.refs_8_ = bf16[72,640]{1,0:T(8,128)(2,1)S(1)} custom-call(bf16[5,24,128]{2,1,0:T(8,128)(2,1)S(1)} %get-tuple-element.31.refs_0_, bf16[5,24,128]{2,1,0:T(8,128)(2,1)S(1)} %collective-permute-done.refs_1_, bf16[5,24,128]{2,1,0:T(8,128)(2,1)S(1)} %collective-permute-done.1.refs_2_, bf16[5,24,128]{2,1,0:T(8,128)(2,1)S(1)} %collective-permute-done.2.refs_3_, ...), custom_call_target="tpu_custom_call" | custom-call | flops 2000000000 | bytes 6000000 | tf_op jit(solution)/shard_map/pallas_call | solution.py:679
  18.2 2.9 %collective-permute-done.7.refs_1_ = bf16[72,640]{1,0:T(8,128)(2,1)S(1)} collective-permute-done((bf16[72,640]{1,0:T(8,128)(2,1)S(1)}, bf16[72,640]{1,0:T(8,128)(2,1)S(1)}, u32[]{:S(2)}, u32[]{:S(2)}) %collective-permute-start.7) | collective-permute-done | bytes 92192 | tf_op jit(solution)/shard_map/ppermute | solution.py:241
  23.3 1.2 %shard_map.131 = (bf16[24,512]{1,0:T(8,128)(2,1)S(1)}, f32[24,192]{1,0:T(8,128)S(1)}) custom-call(bf16[72,640]{1,0:T(8,128)(2,1)S(1)} %shard_map.129.refs_0_, bf16[72,640]{1,0:T(8,128)(2,1)S(1)} %collective-permute-done.7.refs_1_, bf16[72,640]{1,0:T(8,128)(2,1)S(1)} %collective-permute-done.8.refs_2_, bf16[72,640]{1,0:T(8,128)(2,1)S(1)} %collective-permute-done.9.refs_3_, ...), custom_call_target="tpu_custom_call" | custom-call | flops 2000000000 | bytes 6000000 | tf_op jit(solution)/shard_map/pallas_call | solution.py:688
  25.4 4.8 %collective-permute-start.15 = (bf16[24,512]{1,0:T(8,128)(2,1)S(1)}, bf16[24,512]{1,0:T(8,128)(2,1)S(1)}, u32[]{:S(2)}, u32[]{:S(2)}) collective-permute-start(bf16[24,512]{1,0:T(8,128)(2,1)S(1)} %get-tuple-element.40), channel_id=1, source_target_pairs={{0,28},{1,20},{2,12},{3,4},{4,8},{5,0},{6,24},{7,16},{8,29},{9,21}... | collective-permute-start | bytes 73736 | tf_op jit(solution)/shard_map/ppermute | solution.py:712
  30.2 1.5 %collective-permute-done.15.refs_0_ = bf16[24,512]{1,0:T(8,128)(2,1)S(1)} collective-permute-done((bf16[24,512]{1,0:T(8,128)(2,1)S(1)}, bf16[24,512]{1,0:T(8,128)(2,1)S(1)}, u32[]{:S(2)}, u32[]{:S(2)}) %collective-permute-start.15) | collective-permute-done | bytes 24608 | tf_op jit(solution)/shard_map/ppermute | solution.py:712
  31.8 1.2 %collective-permute-done.17.refs_2_ = bf16[24,512]{1,0:T(8,128)(2,1)S(1)} collective-permute-done((bf16[24,512]{1,0:T(8,128)(2,1)S(1)}, bf16[24,512]{1,0:T(8,128)(2,1)S(1)}, u32[]{:S(2)}, u32[]{:S(2)}) %collective-permute-start.17) | collective-permute-done | bytes 24608 | tf_op jit(solution)/shard_map/ppermute | solution.py:241
  33.8 4.4 %collective-permute-start.19 = (bf16[400,128]{1,0:T(8,128)(2,1)S(1)}, bf16[400,128]{1,0:T(8,128)(2,1)S(1)}, u32[]{:S(2)}, u32[]{:S(2)}) collective-permute-start(bf16[400,128]{1,0:T(8,128)(2,1)S(1)} %get-tuple-element.42), channel_id=1, source_target_pairs={{0,3},{1,2},{2,1},{3,0},{4,7},{5,6},{6,5},{7,4},{8,11},{9,10},{10,... | collective-permute-start | bytes 307208 | tf_op jit(solution)/shard_map/ppermute | solution.py:241
  38.8 3.1 %collective-permute-done.19.refs_1_ = bf16[400,128]{1,0:T(8,128)(2,1)S(1)} collective-permute-done((bf16[400,128]{1,0:T(8,128)(2,1)S(1)}, bf16[400,128]{1,0:T(8,128)(2,1)S(1)}, u32[]{:S(2)}, u32[]{:S(2)}) %collective-permute-start.19) | collective-permute-done | bytes 102432 | tf_op jit(solution)/shard_map/ppermute | solution.py:241
  41.9 3.7 %collective-permute-done.20.refs_2_ = bf16[400,128]{1,0:T(8,128)(2,1)S(1)} collective-permute-done((bf16[400,128]{1,0:T(8,128)(2,1)S(1)}, bf16[400,128]{1,0:T(8,128)(2,1)S(1)}, u32[]{:S(2)}, u32[]{:S(2)}) %collective-permute-start.20) | collective-permute-done | bytes 102432 | tf_op jit(solution)/shard_map/ppermute | solution.py:241
  46.2 1.9 %collective-permute-start.24 = (bf16[48,512]{1,0:T(8,128)(2,1)S(1)}, bf16[48,512]{1,0:T(8,128)(2,1)S(1)}, u32[]{:S(2)}, u32[]{:S(2)}) collective-permute-start(bf16[48,512]{1,0:T(8,128)(2,1)S(1)} %shard_map.133.refs_0_), channel_id=1, source_target_pairs={{0,3},{1,2},{2,1},{3,0},{4,7},{5,6},{6,5},{7,4},{8,11},{9,10},{10,... | collective-permute-start | bytes 147464 | tf_op jit(solution)/shard_map/ppermute | solution.py:241
  48.8 1.9 %collective-permute-start.22 = (bf16[48,512]{1,0:T(8,128)(2,1)S(1)}, bf16[48,512]{1,0:T(8,128)(2,1)S(1)}, u32[]{:S(2)}, u32[]{:S(2)}) collective-permute-start(bf16[48,512]{1,0:T(8,128)(2,1)S(1)} %shard_map.133.refs_0_), channel_id=1, source_target_pairs={{0,1},{1,0},{2,3},{3,2},{4,5},{5,4},{6,7},{7,6},{8,9},{9,8},{10,11... | collective-permute-start | bytes 147464 | tf_op jit(solution)/shard_map/ppermute | solution.py:241
  50.7 1.6 %collective-permute-done.24.refs_3_ = bf16[48,512]{1,0:T(8,128)(2,1)S(1)} collective-permute-done((bf16[48,512]{1,0:T(8,128)(2,1)S(1)}, bf16[48,512]{1,0:T(8,128)(2,1)S(1)}, u32[]{:S(2)}, u32[]{:S(2)}) %collective-permute-start.24) | collective-permute-done | bytes 49184 | tf_op jit(solution)/shard_map/ppermute | solution.py:241
  52.3 1.5 %collective-permute-done.23.refs_2_ = bf16[48,512]{1,0:T(8,128)(2,1)S(1)} collective-permute-done((bf16[48,512]{1,0:T(8,128)(2,1)S(1)}, bf16[48,512]{1,0:T(8,128)(2,1)S(1)}, u32[]{:S(2)}, u32[]{:S(2)}) %collective-permute-start.23) | collective-permute-done | bytes 49184 | tf_op jit(solution)/shard_map/ppermute | solution.py:241
  54.7 1.2 %collective-permute-done.25.arrived_ref = bf16[48,384]{1,0:T(8,128)(2,1)S(1)} collective-permute-done((bf16[48,384]{1,0:T(8,128)(2,1)S(1)}, bf16[48,384]{1,0:T(8,128)(2,1)S(1)}, u32[]{:S(2)}, u32[]{:S(2)}) %collective-permute-start.25) | collective-permute-done | bytes 36896 | tf_op jit(solution)/shard_map/ppermute | solution.py:241
  55.9 2.5 %collective-permute-start.26 = (bf16[24,384]{1,0:T(8,128)(2,1)S(1)}, bf16[24,384]{1,0:T(8,128)(2,1)S(1)}, u32[]{:S(2)}, u32[]{:S(2)}) collective-permute-start(bf16[24,384]{1,0:T(8,128)(2,1)S(1)} %get-tuple-element.49), channel_id=1, source_target_pairs={{0,7},{1,15},{2,23},{3,31},{4,1},{5,9},{6,17},{7,25},{8,6},{9,14},... | collective-permute-start | bytes 55304 | tf_op jit(solution)/shard_map/ppermute | solution.py:743
  58.4 1.5 %collective-permute-start.27 = (bf16[24,384]{1,0:T(8,128)(2,1)S(1)}, bf16[24,384]{1,0:T(8,128)(2,1)S(1)}, u32[]{:S(2)}, u32[]{:S(2)}) collective-permute-start(bf16[24,384]{1,0:T(8,128)(2,1)S(1)} %get-tuple-element.50), channel_id=1, source_target_pairs={{0,6},{1,14},{2,22},{3,30},{4,0},{5,8},{6,16},{7,24},{8,7},{9,15},... | collective-permute-start | bytes 55304 | tf_op jit(solution)/shard_map/ppermute | solution.py:743
  59.9 1.5 %collective-permute-done.27.refs_1_ = bf16[24,384]{1,0:T(8,128)(2,1)S(1)} collective-permute-done((bf16[24,384]{1,0:T(8,128)(2,1)S(1)}, bf16[24,384]{1,0:T(8,128)(2,1)S(1)}, u32[]{:S(2)}, u32[]{:S(2)}) %collective-permute-start.27) | collective-permute-done | bytes 18464 | tf_op jit(solution)/shard_map/ppermute | solution.py:743
  61.5 1.2 %collective-permute-done.28.arrived_ref = f32[24,192]{1,0:T(8,128)S(1)} collective-permute-done((f32[24,192]{1,0:T(8,128)S(1)}, f32[24,192]{1,0:T(8,128)S(1)}, u32[]{:S(2)}, u32[]{:S(2)}) %collective-permute-start.28) | collective-permute-done | bytes 18464 | tf_op jit(solution)/shard_map/ppermute | solution.py:241
  (69 shorter events, 13.0 us)
Async XLA Ops:
  2.5 5.1 %collective-permute-start = (bf16[5,24,128]{2,1,0:T(8,128)(2,1)}, bf16[5,24,128]{2,1,0:T(8,128)(2,1)S(1)}, u32[]{:S(2)}, u32[]{:S(2)}) collective-permute-start(bf16[5,24,128]{2,1,0:T(8,128)(2,1)} %get-tuple-element.30.heads_in), channel_id=1, source_target_pairs={{0,8},{4,12},{8,0},{12,4},{16,24},{20,28},{24,16},{28,20},{1,9},{5... | collective-permute-start | bytes 92168 | tf_op jit(solution)/shard_map/ppermute | solution.py:241
  5.6 5.0 %collective-permute-start.2 = (bf16[5,24,128]{2,1,0:T(8,128)(2,1)}, bf16[5,24,128]{2,1,0:T(8,128)(2,1)S(1)}, u32[]{:S(2)}, u32[]{:S(2)}) collective-permute-start(bf16[5,24,128]{2,1,0:T(8,128)(2,1)} %get-tuple-element.30.heads_in), channel_id=1, source_target_pairs={{0,24},{4,28},{8,16},{12,20},{16,8},{20,12},{24,0},{28,4},{1,25},{... | collective-permute-start | bytes 92168 | tf_op jit(solution)/shard_map/ppermute | solution.py:241
  7.1 4.1 %collective-permute-start.1 = (bf16[5,24,128]{2,1,0:T(8,128)(2,1)}, bf16[5,24,128]{2,1,0:T(8,128)(2,1)S(1)}, u32[]{:S(2)}, u32[]{:S(2)}) collective-permute-start(bf16[5,24,128]{2,1,0:T(8,128)(2,1)} %get-tuple-element.30.heads_in), channel_id=1, source_target_pairs={{0,16},{4,20},{8,24},{12,28},{16,0},{20,4},{24,8},{28,12},{1,17},{... | collective-permute-start | bytes 92168 | tf_op jit(solution)/shard_map/ppermute | solution.py:241
  7.1 16.2 %collective-permute-start.14 = (bf16[192,1536]{1,0:T(8,128)(2,1)S(1)}, bf16[192,1536]{1,0:T(8,128)(2,1)S(1)}, u32[]{:S(2)}, u32[]{:S(2)}) collective-permute-start(bf16[192,1536]{1,0:T(8,128)(2,1)S(1)} %bitcast.2), channel_id=1, source_target_pairs={{0,4},{4,0},{8,12},{12,8},{16,20},{20,16},{24,28},{28,24},{1,5},{5... | collective-permute-start | bytes 1769480 | tf_op jit(solution)/shard_map/ppermute | solution.py:241
  7.6 4.7 %collective-permute-start.3 = (bf16[5,24,128]{2,1,0:T(8,128)(2,1)}, bf16[5,24,128]{2,1,0:T(8,128)(2,1)S(1)}, u32[]{:S(2)}, u32[]{:S(2)}) collective-permute-start(bf16[5,24,128]{2,1,0:T(8,128)(2,1)} %get-tuple-element.30.heads_in), channel_id=1, source_target_pairs={{0,4},{4,0},{8,12},{12,8},{16,20},{20,16},{24,28},{28,24},{1,5},{5... | collective-permute-start | bytes 92168 | tf_op jit(solution)/shard_map/ppermute | solution.py:241
  11.2 1.4 %collective-permute-start.4 = (bf16[5,24,128]{2,1,0:T(8,128)(2,1)S(1)}, bf16[5,24,128]{2,1,0:T(8,128)(2,1)S(1)}, u32[]{:S(2)}, u32[]{:S(2)}) collective-permute-start(bf16[5,24,128]{2,1,0:T(8,128)(2,1)S(1)} %collective-permute-done.refs_1_), channel_id=1, source_target_pairs={{0,4},{4,0},{8,12},{12,8},{16,20},{20,16},{24,28},{28,24},{1,5},{5... | collective-permute-start | bytes 92168 | tf_op jit(solution)/shard_map/ppermute | solution.py:241
  13.6 7.6 %collective-permute-start.9 = (bf16[72,640]{1,0:T(8,128)(2,1)S(1)}, bf16[72,640]{1,0:T(8,128)(2,1)S(1)}, u32[]{:S(2)}, u32[]{:S(2)}) collective-permute-start(bf16[72,640]{1,0:T(8,128)(2,1)S(1)} %shard_map.129.refs_0_), channel_id=1, source_target_pairs={{0,24},{4,28},{8,16},{12,20},{16,8},{20,12},{24,0},{28,4},{1,25},{... | collective-permute-start | bytes 276488 | tf_op jit(solution)/shard_map/ppermute | solution.py:241
  15.2 6.3 %collective-permute-start.8 = (bf16[72,640]{1,0:T(8,128)(2,1)S(1)}, bf16[72,640]{1,0:T(8,128)(2,1)S(1)}, u32[]{:S(2)}, u32[]{:S(2)}) collective-permute-start(bf16[72,640]{1,0:T(8,128)(2,1)S(1)} %shard_map.129.refs_0_), channel_id=1, source_target_pairs={{0,16},{4,20},{8,24},{12,28},{16,0},{20,4},{24,8},{28,12},{1,17},{... | collective-permute-start | bytes 276488 | tf_op jit(solution)/shard_map/ppermute | solution.py:241
  16.6 4.6 %collective-permute-start.7 = (bf16[72,640]{1,0:T(8,128)(2,1)S(1)}, bf16[72,640]{1,0:T(8,128)(2,1)S(1)}, u32[]{:S(2)}, u32[]{:S(2)}) collective-permute-start(bf16[72,640]{1,0:T(8,128)(2,1)S(1)} %shard_map.129.refs_0_), channel_id=1, source_target_pairs={{0,8},{4,12},{8,0},{12,4},{16,24},{20,28},{24,16},{28,20},{1,9},{5... | collective-permute-start | bytes 276488 | tf_op jit(solution)/shard_map/ppermute | solution.py:241
  21.2 1.3 %collective-permute-start.13 = (bf16[72,640]{1,0:T(8,128)(2,1)S(1)}, bf16[72,640]{1,0:T(8,128)(2,1)S(1)}, u32[]{:S(2)}, u32[]{:S(2)}) collective-permute-start(bf16[72,640]{1,0:T(8,128)(2,1)S(1)} %collective-permute-done.9.refs_3_), channel_id=1, source_target_pairs={{0,4},{4,0},{8,12},{12,8},{16,20},{20,16},{24,28},{28,24},{1,5},{5... | collective-permute-start | bytes 276488 | tf_op jit(solution)/shard_map/ppermute | solution.py:241
  21.5 1.3 %collective-permute-start.12 = (bf16[72,640]{1,0:T(8,128)(2,1)S(1)}, bf16[72,640]{1,0:T(8,128)(2,1)S(1)}, u32[]{:S(2)}, u32[]{:S(2)}) collective-permute-start(bf16[72,640]{1,0:T(8,128)(2,1)S(1)} %collective-permute-done.8.refs_2_), channel_id=1, source_target_pairs={{0,4},{4,0},{8,12},{12,8},{16,20},{20,16},{24,28},{28,24},{1,5},{5... | collective-permute-start | bytes 276488 | tf_op jit(solution)/shard_map/ppermute | solution.py:241
  21.7 1.3 %collective-permute-start.10 = (bf16[72,640]{1,0:T(8,128)(2,1)S(1)}, bf16[72,640]{1,0:T(8,128)(2,1)S(1)}, u32[]{:S(2)}, u32[]{:S(2)}) collective-permute-start(bf16[72,640]{1,0:T(8,128)(2,1)S(1)} %shard_map.129.refs_0_), channel_id=1, source_target_pairs={{0,4},{4,0},{8,12},{12,8},{16,20},{20,16},{24,28},{28,24},{1,5},{5... | collective-permute-start | bytes 276488 | tf_op jit(solution)/shard_map/ppermute | solution.py:241
  22.0 1.3 %collective-permute-start.11 = (bf16[72,640]{1,0:T(8,128)(2,1)S(1)}, bf16[72,640]{1,0:T(8,128)(2,1)S(1)}, u32[]{:S(2)}, u32[]{:S(2)}) collective-permute-start(bf16[72,640]{1,0:T(8,128)(2,1)S(1)} %collective-permute-done.7.refs_1_), channel_id=1, source_target_pairs={{0,4},{4,0},{8,12},{12,8},{16,20},{20,16},{24,28},{28,24},{1,5},{5... | collective-permute-start | bytes 276488 | tf_op jit(solution)/shard_map/ppermute | solution.py:241
  24.5 5.7 %collective-permute-start.16 = (bf16[24,512]{1,0:T(8,128)(2,1)S(1)}, bf16[24,512]{1,0:T(8,128)(2,1)S(1)}, u32[]{:S(2)}, u32[]{:S(2)}) collective-permute-start(bf16[24,512]{1,0:T(8,128)(2,1)S(1)} %get-tuple-element.40), channel_id=1, source_target_pairs={{0,20},{1,28},{2,4},{3,12},{4,0},{5,8},{6,16},{7,24},{8,21},{9,29}... | collective-permute-start | bytes 73736 | tf_op jit(solution)/shard_map/ppermute | solution.py:712
  25.4 6.4 %collective-permute-start.15 = (bf16[24,512]{1,0:T(8,128)(2,1)S(1)}, bf16[24,512]{1,0:T(8,128)(2,1)S(1)}, u32[]{:S(2)}, u32[]{:S(2)}) collective-permute-start(bf16[24,512]{1,0:T(8,128)(2,1)S(1)} %get-tuple-element.40), channel_id=1, source_target_pairs={{0,28},{1,20},{2,12},{3,4},{4,8},{5,0},{6,24},{7,16},{8,29},{9,21}... | collective-permute-start | bytes 73736 | tf_op jit(solution)/shard_map/ppermute | solution.py:712
  30.2 1.5 %collective-permute-start.18 = (bf16[24,512]{1,0:T(8,128)(2,1)S(1)}, bf16[24,512]{1,0:T(8,128)(2,1)S(1)}, u32[]{:S(2)}, u32[]{:S(2)}) collective-permute-start(bf16[24,512]{1,0:T(8,128)(2,1)S(1)} %collective-permute-done.16.refs_1_), channel_id=1, source_target_pairs={{0,4},{4,0},{8,12},{12,8},{16,20},{20,16},{24,28},{28,24},{1,5},{5... | collective-permute-start | bytes 73736 | tf_op jit(solution)/shard_map/ppermute | solution.py:241
  33.8 8.1 %collective-permute-start.19 = (bf16[400,128]{1,0:T(8,128)(2,1)S(1)}, bf16[400,128]{1,0:T(8,128)(2,1)S(1)}, u32[]{:S(2)}, u32[]{:S(2)}) collective-permute-start(bf16[400,128]{1,0:T(8,128)(2,1)S(1)} %get-tuple-element.42), channel_id=1, source_target_pairs={{0,3},{1,2},{2,1},{3,0},{4,7},{5,6},{6,5},{7,4},{8,11},{9,10},{10,... | collective-permute-start | bytes 307208 | tf_op jit(solution)/shard_map/ppermute | solution.py:241
  38.2 7.4 %collective-permute-start.20 = (bf16[400,128]{1,0:T(8,128)(2,1)S(1)}, bf16[400,128]{1,0:T(8,128)(2,1)S(1)}, u32[]{:S(2)}, u32[]{:S(2)}) collective-permute-start(bf16[400,128]{1,0:T(8,128)(2,1)S(1)} %get-tuple-element.43), channel_id=1, source_target_pairs={{0,1},{1,0},{2,3},{3,2},{4,5},{5,4},{6,7},{7,6},{8,9},{9,8},{10,11... | collective-permute-start | bytes 307208 | tf_op jit(solution)/shard_map/ppermute | solution.py:241
  38.2 7.9 %collective-permute-start.21 = (bf16[400,128]{1,0:T(8,128)(2,1)S(1)}, bf16[400,128]{1,0:T(8,128)(2,1)S(1)}, u32[]{:S(2)}, u32[]{:S(2)}) collective-permute-start(bf16[400,128]{1,0:T(8,128)(2,1)S(1)} %get-tuple-element.44), channel_id=1, source_target_pairs={{0,2},{1,3},{2,0},{3,1},{4,6},{5,7},{6,4},{7,5},{8,10},{9,11},{10,... | collective-permute-start | bytes 307208 | tf_op jit(solution)/shard_map/ppermute | solution.py:241
  46.2 6.1 %collective-permute-start.24 = (bf16[48,512]{1,0:T(8,128)(2,1)S(1)}, bf16[48,512]{1,0:T(8,128)(2,1)S(1)}, u32[]{:S(2)}, u32[]{:S(2)}) collective-permute-start(bf16[48,512]{1,0:T(8,128)(2,1)S(1)} %shard_map.133.refs_0_), channel_id=1, source_target_pairs={{0,3},{1,2},{2,1},{3,0},{4,7},{5,6},{6,5},{7,4},{8,11},{9,10},{10,... | collective-permute-start | bytes 147464 | tf_op jit(solution)/shard_map/ppermute | solution.py:241
  48.2 5.6 %collective-permute-start.23 = (bf16[48,512]{1,0:T(8,128)(2,1)S(1)}, bf16[48,512]{1,0:T(8,128)(2,1)S(1)}, u32[]{:S(2)}, u32[]{:S(2)}) collective-permute-start(bf16[48,512]{1,0:T(8,128)(2,1)S(1)} %shard_map.133.refs_0_), channel_id=1, source_target_pairs={{0,2},{1,3},{2,0},{3,1},{4,6},{5,7},{6,4},{7,5},{8,10},{9,11},{10,... | collective-permute-start | bytes 147464 | tf_op jit(solution)/shard_map/ppermute | solution.py:241
  48.8 5.1 %collective-permute-start.22 = (bf16[48,512]{1,0:T(8,128)(2,1)S(1)}, bf16[48,512]{1,0:T(8,128)(2,1)S(1)}, u32[]{:S(2)}, u32[]{:S(2)}) collective-permute-start(bf16[48,512]{1,0:T(8,128)(2,1)S(1)} %shard_map.133.refs_0_), channel_id=1, source_target_pairs={{0,1},{1,0},{2,3},{3,2},{4,5},{5,4},{6,7},{7,6},{8,9},{9,8},{10,11... | collective-permute-start | bytes 147464 | tf_op jit(solution)/shard_map/ppermute | solution.py:241
  55.9 3.9 %collective-permute-start.26 = (bf16[24,384]{1,0:T(8,128)(2,1)S(1)}, bf16[24,384]{1,0:T(8,128)(2,1)S(1)}, u32[]{:S(2)}, u32[]{:S(2)}) collective-permute-start(bf16[24,384]{1,0:T(8,128)(2,1)S(1)} %get-tuple-element.49), channel_id=1, source_target_pairs={{0,7},{1,15},{2,23},{3,31},{4,1},{5,9},{6,17},{7,25},{8,6},{9,14},... | collective-permute-start | bytes 55304 | tf_op jit(solution)/shard_map/ppermute | solution.py:743
  58.4 2.9 %collective-permute-start.27 = (bf16[24,384]{1,0:T(8,128)(2,1)S(1)}, bf16[24,384]{1,0:T(8,128)(2,1)S(1)}, u32[]{:S(2)}, u32[]{:S(2)}) collective-permute-start(bf16[24,384]{1,0:T(8,128)(2,1)S(1)} %get-tuple-element.50), channel_id=1, source_target_pairs={{0,6},{1,14},{2,22},{3,30},{4,0},{5,8},{6,16},{7,24},{8,7},{9,15},... | collective-permute-start | bytes 55304 | tf_op jit(solution)/shard_map/ppermute | solution.py:743
  (17 other events, 90.2 us)

commit v8 on v7

--- a/solution.py
+++ b/solution.py
@@ -724,7 +724,7 @@
         [VMEM] * (groups + 1),
         [pltpu.VMEM((experts, *message.shape), BF16)],
     )(*near, *far, w_gate_up)
-    sums = [messages[0]] + [swap(messages[k], "req", k) for k in (3, 1, 2)]
+    sums = [messages[0]] + [swap(messages[k], "req", k) for k in (2, 1, 3)]
     hidden = kernel_call(
         hidden_kernel, jax.ShapeDtypeStruct((slots, FFE), BF16), [VMEM] * groups
     )(*sums)

time: 64.1 us -> 63.8 us (level)
  the two profiles are of different devices: /device:TPU:0 before, /device:TPU:7 now
where the time goes in v8:
time: 63.8 us; the launch traced here: 63.6 us
  starting transfers between devices  31.5 us (49%)
  waiting for transfers between devices  22.1 us (35%)
  Pallas kernels  9.1 us (14%)
  local copies, waits for them, and re-layouts  0.79 us (1%)
    ppermute x25, starting transfers between devices, swap(): return lax.ppermute(value, axis, pairs)  23.9 us
    ppermute x25, waiting for transfers between devices, swap(): return lax.ppermute(value, axis, pairs)  15.9 us
    ppermute x2, starting transfers between devices, staged(): lax.ppermute(packed, place, crossing(j))  4.09 us
    ppermute x2, waiting for transfers between devices, staged(): lax.ppermute(out, place, returning(j))  3.56 us
    ppermute x2, starting transfers between devices, staged(): lax.ppermute(out, place, returning(j))  3.53 us
    ppermute x2, waiting for transfers between devices, staged(): lax.ppermute(packed, place, crossing(j))  2.56 us
    pallas_call x1, Pallas kernels, staged(): kernel_call(project_kernel, [heads_shape, jax.ShapeDtypeStruct((row_count...  2.51 us
  transfers between devices with their start and end apart: 29, of which 18 were waited for; matrix products, arithmetic and copies ran while one was open for 0% of the time, Pallas kernels for 4%

profile of v8, /device:TPU:7, one launch (start us, length us, event | category | flops | bytes accessed | tf_op | source)
XLA Modules:
  0.0 63.6 jit_solution(17129814891626907368)
XLA Ops:
  0.0 2.5 %shard_map.127 = (bf16[5,24,128]{2,1,0:T(8,128)(2,1)}, f32[24,384]{1,0:T(8,128)}) custom-call(bf16[6,4,1536]{2,1,0:T(4,128)(2,1)} %refs_0_.1, f32[1536]{0:T(1024)} %refs_1_.1, bf16[320,1536]{1,0:T(8,128)(2,1)} %bitcast.4, s32[6]{0:T(128)} %lengths.1), custom_call_target="tpu_custom_call" | custom-call | flops 5000000000 | bytes 15000000 | tf_op jit(solution)/shard_map/pallas_call | solution.py:635
  2.9 1.2 %collective-permute-start.2 = (bf16[5,24,128]{2,1,0:T(8,128)(2,1)}, bf16[5,24,128]{2,1,0:T(8,128)(2,1)S(1)}, u32[]{:S(2)}, u32[]{:S(2)}) collective-permute-start(bf16[5,24,128]{2,1,0:T(8,128)(2,1)} %get-tuple-element.30.heads_in), channel_id=1, source_target_pairs={{0,24},{4,28},{8,16},{12,20},{16,8},{20,12},{24,0},{28,4},{1,25},{... | collective-permute-start | bytes 92168 | tf_op jit(solution)/shard_map/ppermute | solution.py:241
  4.0 1.2 %collective-permute-start.1 = (bf16[5,24,128]{2,1,0:T(8,128)(2,1)}, bf16[5,24,128]{2,1,0:T(8,128)(2,1)S(1)}, u32[]{:S(2)}, u32[]{:S(2)}) collective-permute-start(bf16[5,24,128]{2,1,0:T(8,128)(2,1)} %get-tuple-element.30.heads_in), channel_id=1, source_target_pairs={{0,16},{4,20},{8,24},{12,28},{16,0},{20,4},{24,8},{28,12},{1,17},{... | collective-permute-start | bytes 92168 | tf_op jit(solution)/shard_map/ppermute | solution.py:241
  5.3 1.5 %collective-permute-start.14 = (bf16[192,1536]{1,0:T(8,128)(2,1)S(1)}, bf16[192,1536]{1,0:T(8,128)(2,1)S(1)}, u32[]{:S(2)}, u32[]{:S(2)}) collective-permute-start(bf16[192,1536]{1,0:T(8,128)(2,1)S(1)} %bitcast.2), channel_id=1, source_target_pairs={{0,4},{4,0},{8,12},{12,8},{16,20},{20,16},{24,28},{28,24},{1,5},{5... | collective-permute-start | bytes 1769480 | tf_op jit(solution)/shard_map/ppermute | solution.py:241
  10.7 1.1 %shard_map.129.refs_0_ = bf16[72,640]{1,0:T(8,128)(2,1)S(1)} custom-call(bf16[5,24,128]{2,1,0:T(8,128)(2,1)S(1)} %get-tuple-element.31.refs_0_, bf16[5,24,128]{2,1,0:T(8,128)(2,1)S(1)} %collective-permute-done.refs_1_, bf16[5,24,128]{2,1,0:T(8,128)(2,1)S(1)} %collective-permute-done.1.refs_2_, bf16[5,24,128]{2,1,0:T(8,128)(2,1)S(1)} %collective-permute-done.2.refs_3_, ...), custom_call_target="tpu_custom_call" | custom-call | flops 2000000000 | bytes 6000000 | tf_op jit(solution)/shard_map/pallas_call | solution.py:673
  11.7 1.2 %collective-permute-start.9 = (bf16[72,640]{1,0:T(8,128)(2,1)S(1)}, bf16[72,640]{1,0:T(8,128)(2,1)S(1)}, u32[]{:S(2)}, u32[]{:S(2)}) collective-permute-start(bf16[72,640]{1,0:T(8,128)(2,1)S(1)} %shard_map.129.refs_0_), channel_id=1, source_target_pairs={{0,24},{4,28},{8,16},{12,20},{16,8},{20,12},{24,0},{28,4},{1,25},{... | collective-permute-start | bytes 276488 | tf_op jit(solution)/shard_map/ppermute | solution.py:241
  14.5 1.1 %shard_map.130.refs_8_ = bf16[72,640]{1,0:T(8,128)(2,1)S(1)} custom-call(bf16[5,24,128]{2,1,0:T(8,128)(2,1)S(1)} %get-tuple-element.31.refs_0_, bf16[5,24,128]{2,1,0:T(8,128)(2,1)S(1)} %collective-permute-done.refs_1_, bf16[5,24,128]{2,1,0:T(8,128)(2,1)S(1)} %collective-permute-done.1.refs_2_, bf16[5,24,128]{2,1,0:T(8,128)(2,1)S(1)} %collective-permute-done.2.refs_3_, ...), custom_call_target="tpu_custom_call" | custom-call | flops 2000000000 | bytes 6000000 | tf_op jit(solution)/shard_map/pallas_call | solution.py:679
  15.5 3.3 %collective-permute-done.7.refs_1_ = bf16[72,640]{1,0:T(8,128)(2,1)S(1)} collective-permute-done((bf16[72,640]{1,0:T(8,128)(2,1)S(1)}, bf16[72,640]{1,0:T(8,128)(2,1)S(1)}, u32[]{:S(2)}, u32[]{:S(2)}) %collective-permute-start.7) | collective-permute-done | bytes 92192 | tf_op jit(solution)/shard_map/ppermute | solution.py:241
  21.6 1.2 %shard_map.131 = (bf16[24,512]{1,0:T(8,128)(2,1)S(1)}, f32[24,192]{1,0:T(8,128)S(1)}) custom-call(bf16[72,640]{1,0:T(8,128)(2,1)S(1)} %shard_map.129.refs_0_, bf16[72,640]{1,0:T(8,128)(2,1)S(1)} %collective-permute-done.7.refs_1_, bf16[72,640]{1,0:T(8,128)(2,1)S(1)} %collective-permute-done.8.refs_2_, bf16[72,640]{1,0:T(8,128)(2,1)S(1)} %collective-permute-done.9.refs_3_, ...), custom_call_target="tpu_custom_call" | custom-call | flops 2000000000 | bytes 6000000 | tf_op jit(solution)/shard_map/pallas_call | solution.py:688
  22.8 4.1 %collective-permute-start.16 = (bf16[24,512]{1,0:T(8,128)(2,1)S(1)}, bf16[24,512]{1,0:T(8,128)(2,1)S(1)}, u32[]{:S(2)}, u32[]{:S(2)}) collective-permute-start(bf16[24,512]{1,0:T(8,128)(2,1)S(1)} %get-tuple-element.40), channel_id=1, source_target_pairs={{0,20},{1,28},{2,4},{3,12},{4,0},{5,8},{6,16},{7,24},{8,21},{9,29}... | collective-permute-start | bytes 73736 | tf_op jit(solution)/shard_map/ppermute | solution.py:712
  26.9 1.3 %collective-permute-done.16.refs_1_ = bf16[24,512]{1,0:T(8,128)(2,1)S(1)} collective-permute-done((bf16[24,512]{1,0:T(8,128)(2,1)S(1)}, bf16[24,512]{1,0:T(8,128)(2,1)S(1)}, u32[]{:S(2)}, u32[]{:S(2)}) %collective-permute-start.16) | collective-permute-done | bytes 24608 | tf_op jit(solution)/shard_map/ppermute | solution.py:712
  28.2 1.9 %collective-permute-start.18 = (bf16[24,512]{1,0:T(8,128)(2,1)S(1)}, bf16[24,512]{1,0:T(8,128)(2,1)S(1)}, u32[]{:S(2)}, u32[]{:S(2)}) collective-permute-start(bf16[24,512]{1,0:T(8,128)(2,1)S(1)} %collective-permute-done.16.refs_1_), channel_id=1, source_target_pairs={{0,4},{4,0},{8,12},{12,8},{16,20},{20,16},{24,28},{28,24},{1,5},{5... | collective-permute-start | bytes 73736 | tf_op jit(solution)/shard_map/ppermute | solution.py:241
  30.1 1.2 %collective-permute-done.15.refs_0_ = bf16[24,512]{1,0:T(8,128)(2,1)S(1)} collective-permute-done((bf16[24,512]{1,0:T(8,128)(2,1)S(1)}, bf16[24,512]{1,0:T(8,128)(2,1)S(1)}, u32[]{:S(2)}, u32[]{:S(2)}) %collective-permute-start.15) | collective-permute-done | bytes 24608 | tf_op jit(solution)/shard_map/ppermute | solution.py:712
  31.3 1.3 %collective-permute-start.17 = (bf16[24,512]{1,0:T(8,128)(2,1)S(1)}, bf16[24,512]{1,0:T(8,128)(2,1)S(1)}, u32[]{:S(2)}, u32[]{:S(2)}) collective-permute-start(bf16[24,512]{1,0:T(8,128)(2,1)S(1)} %collective-permute-done.15.refs_0_), channel_id=1, source_target_pairs={{0,4},{4,0},{8,12},{12,8},{16,20},{20,16},{24,28},{28,24},{1,5},{5... | collective-permute-start | bytes 73736 | tf_op jit(solution)/shard_map/ppermute | solution.py:241
  34.6 3.3 %collective-permute-start.21 = (bf16[400,128]{1,0:T(8,128)(2,1)S(1)}, bf16[400,128]{1,0:T(8,128)(2,1)S(1)}, u32[]{:S(2)}, u32[]{:S(2)}) collective-permute-start(bf16[400,128]{1,0:T(8,128)(2,1)S(1)} %get-tuple-element.44), channel_id=1, source_target_pairs={{0,3},{1,2},{2,1},{3,0},{4,7},{5,6},{6,5},{7,4},{8,11},{9,10},{10,... | collective-permute-start | bytes 307208 | tf_op jit(solution)/shard_map/ppermute | solution.py:241
  37.9 3.9 %collective-permute-done.19.refs_1_ = bf16[400,128]{1,0:T(8,128)(2,1)S(1)} collective-permute-done((bf16[400,128]{1,0:T(8,128)(2,1)S(1)}, bf16[400,128]{1,0:T(8,128)(2,1)S(1)}, u32[]{:S(2)}, u32[]{:S(2)}) %collective-permute-start.19) | collective-permute-done | bytes 102432 | tf_op jit(solution)/shard_map/ppermute | solution.py:241
  42.3 2.9 %collective-permute-start.24 = (bf16[48,512]{1,0:T(8,128)(2,1)S(1)}, bf16[48,512]{1,0:T(8,128)(2,1)S(1)}, u32[]{:S(2)}, u32[]{:S(2)}) collective-permute-start(bf16[48,512]{1,0:T(8,128)(2,1)S(1)} %shard_map.133.refs_0_), channel_id=1, source_target_pairs={{0,3},{1,2},{2,1},{3,0},{4,7},{5,6},{6,5},{7,4},{8,11},{9,10},{10,... | collective-permute-start | bytes 147464 | tf_op jit(solution)/shard_map/ppermute | solution.py:241
  45.2 1.9 %collective-permute-start.23 = (bf16[48,512]{1,0:T(8,128)(2,1)S(1)}, bf16[48,512]{1,0:T(8,128)(2,1)S(1)}, u32[]{:S(2)}, u32[]{:S(2)}) collective-permute-start(bf16[48,512]{1,0:T(8,128)(2,1)S(1)} %shard_map.133.refs_0_), channel_id=1, source_target_pairs={{0,2},{1,3},{2,0},{3,1},{4,6},{5,7},{6,4},{7,5},{8,10},{9,11},{10,... | collective-permute-start | bytes 147464 | tf_op jit(solution)/shard_map/ppermute | solution.py:241
  47.1 3.3 %collective-permute-done.23.refs_2_ = bf16[48,512]{1,0:T(8,128)(2,1)S(1)} collective-permute-done((bf16[48,512]{1,0:T(8,128)(2,1)S(1)}, bf16[48,512]{1,0:T(8,128)(2,1)S(1)}, u32[]{:S(2)}, u32[]{:S(2)}) %collective-permute-start.23) | collective-permute-done | bytes 49184 | tf_op jit(solution)/shard_map/ppermute | solution.py:241
  51.3 2.4 %collective-permute-start.25 = (bf16[48,384]{1,0:T(8,128)(2,1)S(1)}, bf16[48,384]{1,0:T(8,128)(2,1)S(1)}, u32[]{:S(2)}, u32[]{:S(2)}) collective-permute-start(bf16[48,384]{1,0:T(8,128)(2,1)S(1)} %get-tuple-element.48), channel_id=1, source_target_pairs={{0,4},{4,0},{8,12},{12,8},{16,20},{20,16},{24,28},{28,24},{1,5},{5... | collective-permute-start | bytes 110600 | tf_op jit(solution)/shard_map/ppermute | solution.py:241
  54.5 1.2 %collective-permute-start.26 = (bf16[24,384]{1,0:T(8,128)(2,1)S(1)}, bf16[24,384]{1,0:T(8,128)(2,1)S(1)}, u32[]{:S(2)}, u32[]{:S(2)}) collective-permute-start(bf16[24,384]{1,0:T(8,128)(2,1)S(1)} %get-tuple-element.49), channel_id=1, source_target_pairs={{0,7},{1,15},{2,23},{3,31},{4,1},{5,9},{6,17},{7,25},{8,6},{9,14},... | collective-permute-start | bytes 55304 | tf_op jit(solution)/shard_map/ppermute | solution.py:743
  55.8 2.3 %collective-permute-start.27 = (bf16[24,384]{1,0:T(8,128)(2,1)S(1)}, bf16[24,384]{1,0:T(8,128)(2,1)S(1)}, u32[]{:S(2)}, u32[]{:S(2)}) collective-permute-start(bf16[24,384]{1,0:T(8,128)(2,1)S(1)} %get-tuple-element.50), channel_id=1, source_target_pairs={{0,6},{1,14},{2,22},{3,30},{4,0},{5,8},{6,16},{7,24},{8,7},{9,15},... | collective-permute-start | bytes 55304 | tf_op jit(solution)/shard_map/ppermute | solution.py:743
  58.1 1.5 %collective-permute-done.26.refs_0_ = bf16[24,384]{1,0:T(8,128)(2,1)S(1)} collective-permute-done((bf16[24,384]{1,0:T(8,128)(2,1)S(1)}, bf16[24,384]{1,0:T(8,128)(2,1)S(1)}, u32[]{:S(2)}, u32[]{:S(2)}) %collective-permute-start.26) | collective-permute-done | bytes 18464 | tf_op jit(solution)/shard_map/ppermute | solution.py:743
  59.6 2.1 %collective-permute-done.27.refs_1_ = bf16[24,384]{1,0:T(8,128)(2,1)S(1)} collective-permute-done((bf16[24,384]{1,0:T(8,128)(2,1)S(1)}, bf16[24,384]{1,0:T(8,128)(2,1)S(1)}, u32[]{:S(2)}, u32[]{:S(2)}) %collective-permute-start.27) | collective-permute-done | bytes 18464 | tf_op jit(solution)/shard_map/ppermute | solution.py:743
  (69 shorter events, 14.6 us)
Async XLA Ops:
  2.6 4.2 %collective-permute-start = (bf16[5,24,128]{2,1,0:T(8,128)(2,1)}, bf16[5,24,128]{2,1,0:T(8,128)(2,1)S(1)}, u32[]{:S(2)}, u32[]{:S(2)}) collective-permute-start(bf16[5,24,128]{2,1,0:T(8,128)(2,1)} %get-tuple-element.30.heads_in), channel_id=1, source_target_pairs={{0,8},{4,12},{8,0},{12,4},{16,24},{20,28},{24,16},{28,20},{1,9},{5... | collective-permute-start | bytes 92168 | tf_op jit(solution)/shard_map/ppermute | solution.py:241
  2.9 6.0 %collective-permute-start.2 = (bf16[5,24,128]{2,1,0:T(8,128)(2,1)}, bf16[5,24,128]{2,1,0:T(8,128)(2,1)S(1)}, u32[]{:S(2)}, u32[]{:S(2)}) collective-permute-start(bf16[5,24,128]{2,1,0:T(8,128)(2,1)} %get-tuple-element.30.heads_in), channel_id=1, source_target_pairs={{0,24},{4,28},{8,16},{12,20},{16,8},{20,12},{24,0},{28,4},{1,25},{... | collective-permute-start | bytes 92168 | tf_op jit(solution)/shard_map/ppermute | solution.py:241
  4.0 4.9 %collective-permute-start.1 = (bf16[5,24,128]{2,1,0:T(8,128)(2,1)}, bf16[5,24,128]{2,1,0:T(8,128)(2,1)S(1)}, u32[]{:S(2)}, u32[]{:S(2)}) collective-permute-start(bf16[5,24,128]{2,1,0:T(8,128)(2,1)} %get-tuple-element.30.heads_in), channel_id=1, source_target_pairs={{0,16},{4,20},{8,24},{12,28},{16,0},{20,4},{24,8},{28,12},{1,17},{... | collective-permute-start | bytes 92168 | tf_op jit(solution)/shard_map/ppermute | solution.py:241
  5.3 16.3 %collective-permute-start.14 = (bf16[192,1536]{1,0:T(8,128)(2,1)S(1)}, bf16[192,1536]{1,0:T(8,128)(2,1)S(1)}, u32[]{:S(2)}, u32[]{:S(2)}) collective-permute-start(bf16[192,1536]{1,0:T(8,128)(2,1)S(1)} %bitcast.2), channel_id=1, source_target_pairs={{0,4},{4,0},{8,12},{12,8},{16,20},{20,16},{24,28},{28,24},{1,5},{5... | collective-permute-start | bytes 1769480 | tf_op jit(solution)/shard_map/ppermute | solution.py:241
  6.8 3.5 %collective-permute-start.3 = (bf16[5,24,128]{2,1,0:T(8,128)(2,1)}, bf16[5,24,128]{2,1,0:T(8,128)(2,1)S(1)}, u32[]{:S(2)}, u32[]{:S(2)}) collective-permute-start(bf16[5,24,128]{2,1,0:T(8,128)(2,1)} %get-tuple-element.30.heads_in), channel_id=1, source_target_pairs={{0,4},{4,0},{8,12},{12,8},{16,20},{20,16},{24,28},{28,24},{1,5},{5... | collective-permute-start | bytes 92168 | tf_op jit(solution)/shard_map/ppermute | solution.py:241
  9.0 1.3 %collective-permute-start.5 = (bf16[5,24,128]{2,1,0:T(8,128)(2,1)S(1)}, bf16[5,24,128]{2,1,0:T(8,128)(2,1)S(1)}, u32[]{:S(2)}, u32[]{:S(2)}) collective-permute-start(bf16[5,24,128]{2,1,0:T(8,128)(2,1)S(1)} %collective-permute-done.1.refs_2_), channel_id=1, source_target_pairs={{0,4},{4,0},{8,12},{12,8},{16,20},{20,16},{24,28},{28,24},{1,5},{5... | collective-permute-start | bytes 92168 | tf_op jit(solution)/shard_map/ppermute | solution.py:241
  11.7 7.1 %collective-permute-start.9 = (bf16[72,640]{1,0:T(8,128)(2,1)S(1)}, bf16[72,640]{1,0:T(8,128)(2,1)S(1)}, u32[]{:S(2)}, u32[]{:S(2)}) collective-permute-start(bf16[72,640]{1,0:T(8,128)(2,1)S(1)} %shard_map.129.refs_0_), channel_id=1, source_target_pairs={{0,24},{4,28},{8,16},{12,20},{16,8},{20,12},{24,0},{28,4},{1,25},{... | collective-permute-start | bytes 276488 | tf_op jit(solution)/shard_map/ppermute | solution.py:241
  12.9 6.8 %collective-permute-start.8 = (bf16[72,640]{1,0:T(8,128)(2,1)S(1)}, bf16[72,640]{1,0:T(8,128)(2,1)S(1)}, u32[]{:S(2)}, u32[]{:S(2)}) collective-permute-start(bf16[72,640]{1,0:T(8,128)(2,1)S(1)} %shard_map.129.refs_0_), channel_id=1, source_target_pairs={{0,16},{4,20},{8,24},{12,28},{16,0},{20,4},{24,8},{28,12},{1,17},{... | collective-permute-start | bytes 276488 | tf_op jit(solution)/shard_map/ppermute | solution.py:241
  13.8 5.1 %collective-permute-start.7 = (bf16[72,640]{1,0:T(8,128)(2,1)S(1)}, bf16[72,640]{1,0:T(8,128)(2,1)S(1)}, u32[]{:S(2)}, u32[]{:S(2)}) collective-permute-start(bf16[72,640]{1,0:T(8,128)(2,1)S(1)} %shard_map.129.refs_0_), channel_id=1, source_target_pairs={{0,8},{4,12},{8,0},{12,4},{16,24},{20,28},{24,16},{28,20},{1,9},{5... | collective-permute-start | bytes 276488 | tf_op jit(solution)/shard_map/ppermute | solution.py:241
  18.8 1.9 %collective-permute-start.13 = (bf16[72,640]{1,0:T(8,128)(2,1)S(1)}, bf16[72,640]{1,0:T(8,128)(2,1)S(1)}, u32[]{:S(2)}, u32[]{:S(2)}) collective-permute-start(bf16[72,640]{1,0:T(8,128)(2,1)S(1)} %collective-permute-done.9.refs_3_), channel_id=1, source_target_pairs={{0,4},{4,0},{8,12},{12,8},{16,20},{20,16},{24,28},{28,24},{1,5},{5... | collective-permute-start | bytes 276488 | tf_op jit(solution)/shard_map/ppermute | solution.py:241
  19.9 1.4 %collective-permute-start.10 = (bf16[72,640]{1,0:T(8,128)(2,1)S(1)}, bf16[72,640]{1,0:T(8,128)(2,1)S(1)}, u32[]{:S(2)}, u32[]{:S(2)}) collective-permute-start(bf16[72,640]{1,0:T(8,128)(2,1)S(1)} %shard_map.129.refs_0_), channel_id=1, source_target_pairs={{0,4},{4,0},{8,12},{12,8},{16,20},{20,16},{24,28},{28,24},{1,5},{5... | collective-permute-start | bytes 276488 | tf_op jit(solution)/shard_map/ppermute | solution.py:241
  22.8 5.4 %collective-permute-start.16 = (bf16[24,512]{1,0:T(8,128)(2,1)S(1)}, bf16[24,512]{1,0:T(8,128)(2,1)S(1)}, u32[]{:S(2)}, u32[]{:S(2)}) collective-permute-start(bf16[24,512]{1,0:T(8,128)(2,1)S(1)} %get-tuple-element.40), channel_id=1, source_target_pairs={{0,20},{1,28},{2,4},{3,12},{4,0},{5,8},{6,16},{7,24},{8,21},{9,29}... | collective-permute-start | bytes 73736 | tf_op jit(solution)/shard_map/ppermute | solution.py:712
  26.9 4.4 %collective-permute-start.15 = (bf16[24,512]{1,0:T(8,128)(2,1)S(1)}, bf16[24,512]{1,0:T(8,128)(2,1)S(1)}, u32[]{:S(2)}, u32[]{:S(2)}) collective-permute-start(bf16[24,512]{1,0:T(8,128)(2,1)S(1)} %get-tuple-element.40), channel_id=1, source_target_pairs={{0,28},{1,20},{2,12},{3,4},{4,8},{5,0},{6,24},{7,16},{8,29},{9,21}... | collective-permute-start | bytes 73736 | tf_op jit(solution)/shard_map/ppermute | solution.py:712
  28.2 4.4 %collective-permute-start.18 = (bf16[24,512]{1,0:T(8,128)(2,1)S(1)}, bf16[24,512]{1,0:T(8,128)(2,1)S(1)}, u32[]{:S(2)}, u32[]{:S(2)}) collective-permute-start(bf16[24,512]{1,0:T(8,128)(2,1)S(1)} %collective-permute-done.16.refs_1_), channel_id=1, source_target_pairs={{0,4},{4,0},{8,12},{12,8},{16,20},{20,16},{24,28},{28,24},{1,5},{5... | collective-permute-start | bytes 73736 | tf_op jit(solution)/shard_map/ppermute | solution.py:241
  31.3 2.1 %collective-permute-start.17 = (bf16[24,512]{1,0:T(8,128)(2,1)S(1)}, bf16[24,512]{1,0:T(8,128)(2,1)S(1)}, u32[]{:S(2)}, u32[]{:S(2)}) collective-permute-start(bf16[24,512]{1,0:T(8,128)(2,1)S(1)} %collective-permute-done.15.refs_0_), channel_id=1, source_target_pairs={{0,4},{4,0},{8,12},{12,8},{16,20},{20,16},{24,28},{28,24},{1,5},{5... | collective-permute-start | bytes 73736 | tf_op jit(solution)/shard_map/ppermute | solution.py:241
  34.3 7.5 %collective-permute-start.19 = (bf16[400,128]{1,0:T(8,128)(2,1)S(1)}, bf16[400,128]{1,0:T(8,128)(2,1)S(1)}, u32[]{:S(2)}, u32[]{:S(2)}) collective-permute-start(bf16[400,128]{1,0:T(8,128)(2,1)S(1)} %get-tuple-element.42), channel_id=1, source_target_pairs={{0,2},{1,3},{2,0},{3,1},{4,6},{5,7},{6,4},{7,5},{8,10},{9,11},{10,... | collective-permute-start | bytes 307208 | tf_op jit(solution)/shard_map/ppermute | solution.py:241
  34.4 7.4 %collective-permute-start.20 = (bf16[400,128]{1,0:T(8,128)(2,1)S(1)}, bf16[400,128]{1,0:T(8,128)(2,1)S(1)}, u32[]{:S(2)}, u32[]{:S(2)}) collective-permute-start(bf16[400,128]{1,0:T(8,128)(2,1)S(1)} %get-tuple-element.43), channel_id=1, source_target_pairs={{0,1},{1,0},{2,3},{3,2},{4,5},{5,4},{6,7},{7,6},{8,9},{9,8},{10,11... | collective-permute-start | bytes 307208 | tf_op jit(solution)/shard_map/ppermute | solution.py:241
  34.6 7.6 %collective-permute-start.21 = (bf16[400,128]{1,0:T(8,128)(2,1)S(1)}, bf16[400,128]{1,0:T(8,128)(2,1)S(1)}, u32[]{:S(2)}, u32[]{:S(2)}) collective-permute-start(bf16[400,128]{1,0:T(8,128)(2,1)S(1)} %get-tuple-element.44), channel_id=1, source_target_pairs={{0,3},{1,2},{2,1},{3,0},{4,7},{5,6},{6,5},{7,4},{8,11},{9,10},{10,... | collective-permute-start | bytes 307208 | tf_op jit(solution)/shard_map/ppermute | solution.py:241
  42.3 4.8 %collective-permute-start.24 = (bf16[48,512]{1,0:T(8,128)(2,1)S(1)}, bf16[48,512]{1,0:T(8,128)(2,1)S(1)}, u32[]{:S(2)}, u32[]{:S(2)}) collective-permute-start(bf16[48,512]{1,0:T(8,128)(2,1)S(1)} %shard_map.133.refs_0_), channel_id=1, source_target_pairs={{0,3},{1,2},{2,1},{3,0},{4,7},{5,6},{6,5},{7,4},{8,11},{9,10},{10,... | collective-permute-start | bytes 147464 | tf_op jit(solution)/shard_map/ppermute | solution.py:241
  45.2 5.2 %collective-permute-start.23 = (bf16[48,512]{1,0:T(8,128)(2,1)S(1)}, bf16[48,512]{1,0:T(8,128)(2,1)S(1)}, u32[]{:S(2)}, u32[]{:S(2)}) collective-permute-start(bf16[48,512]{1,0:T(8,128)(2,1)S(1)} %shard_map.133.refs_0_), channel_id=1, source_target_pairs={{0,2},{1,3},{2,0},{3,1},{4,6},{5,7},{6,4},{7,5},{8,10},{9,11},{10,... | collective-permute-start | bytes 147464 | tf_op jit(solution)/shard_map/ppermute | solution.py:241
  47.1 3.3 %collective-permute-start.22 = (bf16[48,512]{1,0:T(8,128)(2,1)S(1)}, bf16[48,512]{1,0:T(8,128)(2,1)S(1)}, u32[]{:S(2)}, u32[]{:S(2)}) collective-permute-start(bf16[48,512]{1,0:T(8,128)(2,1)S(1)} %shard_map.133.refs_0_), channel_id=1, source_target_pairs={{0,1},{1,0},{2,3},{3,2},{4,5},{5,4},{6,7},{7,6},{8,9},{9,8},{10,11... | collective-permute-start | bytes 147464 | tf_op jit(solution)/shard_map/ppermute | solution.py:241
  51.3 3.2 %collective-permute-start.25 = (bf16[48,384]{1,0:T(8,128)(2,1)S(1)}, bf16[48,384]{1,0:T(8,128)(2,1)S(1)}, u32[]{:S(2)}, u32[]{:S(2)}) collective-permute-start(bf16[48,384]{1,0:T(8,128)(2,1)S(1)} %get-tuple-element.48), channel_id=1, source_target_pairs={{0,4},{4,0},{8,12},{12,8},{16,20},{20,16},{24,28},{28,24},{1,5},{5... | collective-permute-start | bytes 110600 | tf_op jit(solution)/shard_map/ppermute | solution.py:241
  54.5 5.0 %collective-permute-start.26 = (bf16[24,384]{1,0:T(8,128)(2,1)S(1)}, bf16[24,384]{1,0:T(8,128)(2,1)S(1)}, u32[]{:S(2)}, u32[]{:S(2)}) collective-permute-start(bf16[24,384]{1,0:T(8,128)(2,1)S(1)} %get-tuple-element.49), channel_id=1, source_target_pairs={{0,7},{1,15},{2,23},{3,31},{4,1},{5,9},{6,17},{7,25},{8,6},{9,14},... | collective-permute-start | bytes 55304 | tf_op jit(solution)/shard_map/ppermute | solution.py:743
  55.8 5.9 %collective-permute-start.27 = (bf16[24,384]{1,0:T(8,128)(2,1)S(1)}, bf16[24,384]{1,0:T(8,128)(2,1)S(1)}, u32[]{:S(2)}, u32[]{:S(2)}) collective-permute-start(bf16[24,384]{1,0:T(8,128)(2,1)S(1)} %get-tuple-element.50), channel_id=1, source_target_pairs={{0,6},{1,14},{2,22},{3,30},{4,0},{5,8},{6,16},{7,24},{8,7},{9,15},... | collective-permute-start | bytes 55304 | tf_op jit(solution)/shard_map/ppermute | solution.py:743
  (17 other events, 90.1 us)
